TPU v7x, 1024 devices: a whole 4x8x16 slice. The times are simulated.
1024 devices in a mesh: node: 128 (over y, z), sub: 8 (over x, core).
Axes of the slice: x: 4, y: 8, z: 16, core: 2. Of those that a mesh axis runs over, the one named last changes fastest.
Arguments:
- right_side: bfloat16 [128, 256, 32, 128], P('node', 'sub'), may hold values from -6 to 6
- diag_blocks: bfloat16 [128, 256, 128, 128], P('node', 'sub'), as said below
- link_blocks: bfloat16 [128, 256, 128, 128], P('node', 'sub'), may hold values from -0.119628906 to 0.119628906
- restrict_map: bfloat16 [128, 128], replicated, may hold values from -0.8984375 to 0.8984375
- level_map: float32 [2, 128, 128], replicated, as said below
- coarse_inverse: float32 [256, 256], replicated, as said below
Outputs:
- relaxed: float32 [128, 256, 32, 128], P('node', 'sub')
- coarse_solution: float32 [128, 8, 32, 256], P('node', 'sub')
Inputs may be any that keep to these rules, and one draw needn't show every extreme that they name: diag_blocks are each 2 times the identity plus entries of deviation 0.34 / sqrt(128). level_map blocks are the identity plus entries of deviation 0.2 / sqrt(128). coarse_inverse is the identity plus entries of deviation 0.2 / sqrt(256).
All inputs are finite; a program needn't handle non-finite values.
Results may differ from a plain program's by a relative error of at most 0.0092.
Values may be sent and summed in bfloat16 or wider, within the bound.
No kernel may reach another device: no remote copies, remote signals or barrier semaphores. Data moves between devices by JAX's collectives and lax.ppermute only.
A program may use at most 32 MiB of HBM per device.

v0:
```python
import math

import jax
import jax.numpy as jnp
from jax import lax
from jax.sharding import PartitionSpec as P


def extended(shard, sides, width):
    for axis, dim in sides:
        count, length = (lax.axis_size(axis), shard.shape[dim])
        up = [(i, (i + 1) % count) for i in range(count - 1)]
        down = [(j, i) for i, j in up]
        last = lax.slice_in_dim(shard, length - width, length, axis=dim)
        initial = lax.slice_in_dim(shard, 0, width, axis=dim)
        before = lax.ppermute(last, axis, up)
        after = lax.ppermute(initial, axis, down)
        shard = jnp.concatenate([before, shard, after], axis=dim)
    return shard


def passed_along(block, axis, distance):
    devices = range(lax.axis_size(axis))
    route = [(i - distance, i) for i in devices if i - distance in devices]
    return lax.ppermute(block, axis, route)


def from_partner(value, axis, distance):
    mask = 2**distance
    pairs = [(source, source ^ mask) for source in range(lax.axis_size(axis))]
    return lax.ppermute(value, axis, pairs)


def apply_local(field, diag_blocks, link_blocks, prev_link):
    padded = extended(field, (("sub", 1),), 1)
    prev_vals = padded[:, :-2]
    next_vals = padded[:, 2:]
    total = jnp.einsum("nmvr,nmrs->nmvs", field, diag_blocks, preferred_element_type=jnp.float32)
    total = total + jnp.einsum(
        "nmvr,nmrs->nmvs", prev_vals, prev_link, preferred_element_type=jnp.float32
    )
    total = total + jnp.einsum(
        "nmvs,nmrs->nmvr", next_vals, link_blocks, preferred_element_type=jnp.float32
    )
    return total


def chebyshev(right_side, operate):
    theta = 2.0
    delta = 1.7
    sigma = theta / delta
    rho = 1.0 / sigma
    residue = right_side.astype(jnp.float32)
    direction = residue / theta
    relaxed = direction
    for step in range(4):
        residue = residue - operate(direction.astype(jnp.bfloat16))
        if step < 3:
            rho_new = 1.0 / (2.0 * sigma - rho)
            direction = rho_new * rho * direction + 2.0 * rho_new / delta * residue
            relaxed = relaxed + direction
            rho = rho_new
    return (relaxed, residue)


def level_step(coarse, level_map):
    return jnp.einsum(
        "cvr,crs->cvs",
        coarse,
        level_map,
        precision=lax.Precision.HIGHEST,
        preferred_element_type=jnp.float32,
    )


def shards(right_side, diag_blocks, link_blocks, restrict_map, level_map, coarse_inverse):
    tiles = right_side.shape[1]
    vecs = right_side.shape[2]
    rows = right_side.shape[3]
    edge_link = passed_along(link_blocks[:, -1:], "sub", 1)
    prev_link = jnp.concatenate([edge_link, link_blocks[:, :-1]], axis=1)

    def operate(field):
        return apply_local(field, diag_blocks, link_blocks, prev_link)

    relaxed, residue = chebyshev(right_side, operate)
    groups = level_map.shape[0]
    resb = residue.astype(jnp.bfloat16)
    projected = jnp.dot(resb.reshape(-1, rows), restrict_map, preferred_element_type=jnp.float32)
    coarse = jnp.sum(projected.reshape(groups, tiles // groups, vecs, rows), axis=1)
    scale = 1.0 / math.sqrt(2.0)
    sub_bits = lax.axis_size("sub").bit_length() - 1
    node_bits = lax.axis_size("node").bit_length() - 1
    for bit in range(sub_bits):
        partner = from_partner(coarse.astype(jnp.bfloat16), "sub", bit).astype(coarse.dtype)
        coarse = level_step((coarse + partner) * scale, level_map)
    for bit in range(node_bits):
        partner = from_partner(coarse, "node", bit)
        coarse = level_step((coarse + partner) * scale, level_map)
    flat = jnp.transpose(coarse, (1, 0, 2)).reshape(vecs, groups * rows)
    solved = jnp.dot(
        flat, coarse_inverse, precision=lax.Precision.HIGHEST, preferred_element_type=jnp.float32
    )
    return (relaxed, solved[None, None])


def solution(mesh):
    placed = (
        P("node", "sub", None, None),
        P("node", "sub", None, None),
        P("node", "sub", None, None),
        P(),
        P(),
        P(),
    )
    return jax.shard_map(
        shards,
        mesh=mesh,
        in_specs=placed,
        out_specs=(P("node", "sub", None, None), P("node", "sub", None, None)),
        check_vma=False,
    )
```

profile of v0, /device:TPU:2, one launch (start us, length us, event | category | flops | bytes accessed | tf_op | source)
XLA Modules:
  0.0 127.7 jit_solution(3078646156645205384)
XLA Ops:
  1.5 2.0 %collective-permute-start.1 = (bf16[1,1,128,128]{3,2,1,0:T(8,128)(2,1)S(1)}, bf16[1,1,128,128]{3,2,1,0:T(8,128)(2,1)S(1)}, u32[]{:S(2)}, u32[]{:S(2)}) collective-permute-start(bf16[1,1,128,128]{3,2,1,0:T(8,128)(2,1)S(1)} %slice.64), channel_id=1, source_target_pairs={{0,1},{1,2},{2,3},{3,4},{4,5},{5,6},{6,7},{8,9},{9,10},{10,11},{11... | collective-permute-start | bytes 98312 | tf_op jit(solution)/shard_map/ppermute | solution.py:25
  3.5 1.0 fusion.22
  4.6 3.8 %collective-permute-start.2 = (bf16[1,1,32,128]{3,2,1,0:T(8,128)(2,1)S(1)}, bf16[1,1,32,128]{3,2,1,0:T(8,128)(2,1)S(1)}, u32[]{:S(2)}, u32[]{:S(2)}) collective-permute-start(bf16[1,1,32,128]{3,2,1,0:T(8,128)(2,1)S(1)} %get-tuple-element.10), channel_id=1, source_target_pairs={{1,0},{2,1},{3,2},{4,3},{5,4},{6,5},{7,6},{9,8},{10,9},{11,10},{12... | collective-permute-start | bytes 24584 | tf_op jit(solution)/shard_map/ppermute | solution.py:17
  8.4 1.9 %collective-permute-start = (bf16[1,1,32,128]{3,2,1,0:T(8,128)(2,1)S(1)}, bf16[1,1,32,128]{3,2,1,0:T(8,128)(2,1)S(1)}, u32[]{:S(2)}, u32[]{:S(2)}) collective-permute-start(bf16[1,1,32,128]{3,2,1,0:T(8,128)(2,1)S(1)} %get-tuple-element.11), channel_id=1, source_target_pairs={{0,1},{1,2},{2,3},{3,4},{4,5},{5,6},{6,7},{8,9},{9,10},{10,11},{11... | collective-permute-start | bytes 24584 | tf_op jit(solution)/shard_map/ppermute | solution.py:16
  10.8 11.7 %collective-permute-done = bf16[1,1,32,128]{3,2,1,0:T(8,128)(2,1)S(1)} collective-permute-done((bf16[1,1,32,128]{3,2,1,0:T(8,128)(2,1)S(1)}, bf16[1,1,32,128]{3,2,1,0:T(8,128)(2,1)S(1)}, u32[]{:S(2)}, u32[]{:S(2)}) %collective-permute-start) | collective-permute-done | bytes 8224 | tf_op jit(solution)/shard_map/ppermute | solution.py:16
  23.6 1.9 %collective-permute-start.3 = (bf16[1,1,32,128]{3,2,1,0:T(8,128)(2,1)S(1)}, bf16[1,1,32,128]{3,2,1,0:T(8,128)(2,1)S(1)}, u32[]{:S(2)}, u32[]{:S(2)}) collective-permute-start(bf16[1,1,32,128]{3,2,1,0:T(8,128)(2,1)S(1)} %get-tuple-element.9), channel_id=1, source_target_pairs={{0,1},{1,2},{2,3},{3,4},{4,5},{5,6},{6,7},{8,9},{9,10},{10,11},{11... | collective-permute-start | bytes 24584 | tf_op jit(solution)/shard_map/ppermute | solution.py:16
  25.9 3.6 %collective-permute-start.4 = (bf16[1,1,32,128]{3,2,1,0:T(8,128)(2,1)S(1)}, bf16[1,1,32,128]{3,2,1,0:T(8,128)(2,1)S(1)}, u32[]{:S(2)}, u32[]{:S(2)}) collective-permute-start(bf16[1,1,32,128]{3,2,1,0:T(8,128)(2,1)S(1)} %get-tuple-element.8), channel_id=1, source_target_pairs={{1,0},{2,1},{3,2},{4,3},{5,4},{6,5},{7,6},{9,8},{10,9},{11,10},{12... | collective-permute-start | bytes 24584 | tf_op jit(solution)/shard_map/ppermute | solution.py:17
  31.6 1.9 %collective-permute-start.5 = (bf16[1,1,32,128]{3,2,1,0:T(8,128)(2,1)S(1)}, bf16[1,1,32,128]{3,2,1,0:T(8,128)(2,1)S(1)}, u32[]{:S(2)}, u32[]{:S(2)}) collective-permute-start(bf16[1,1,32,128]{3,2,1,0:T(8,128)(2,1)S(1)} %get-tuple-element.7), channel_id=1, source_target_pairs={{0,1},{1,2},{2,3},{3,4},{4,5},{5,6},{6,7},{8,9},{9,10},{10,11},{11... | collective-permute-start | bytes 24584 | tf_op jit(solution)/shard_map/ppermute | solution.py:16
  33.9 3.6 %collective-permute-start.6 = (bf16[1,1,32,128]{3,2,1,0:T(8,128)(2,1)S(1)}, bf16[1,1,32,128]{3,2,1,0:T(8,128)(2,1)S(1)}, u32[]{:S(2)}, u32[]{:S(2)}) collective-permute-start(bf16[1,1,32,128]{3,2,1,0:T(8,128)(2,1)S(1)} %get-tuple-element.6), channel_id=1, source_target_pairs={{1,0},{2,1},{3,2},{4,3},{5,4},{6,5},{7,6},{9,8},{10,9},{11,10},{12... | collective-permute-start | bytes 24584 | tf_op jit(solution)/shard_map/ppermute | solution.py:17
  38.9 1.5 %fusion.26 = (bf16[1,32,32,128]{3,2,1,0:T(8,128)(2,1)S(1)}, f32[1,32,32,128]{3,2,1,0:T(8,128)}, f32[1,32,32,128]{3,2,1,0:T(8,128)S(1)}) fusion(f32[1,32,32,128]{3,2,1,0:T(8,128)S(1)} %get-tuple-element.15, f32[1,32,32,128]{3,2,1,0:T(8,128)S(1)} %get-tuple-element.13, bf16[1,32,32,128]{3,2,1,0:T(8,128)(2,1)S(1)} %copy-done.3, ...), kind=kOutput, calls=%fused_computation.42 | convolution fusion | flops 35913728 | bytes 4464640 | tf_op jit(solution)/shard_map/nmvs,nmrs->nmvr/dot_general | solution.py:42
  40.4 1.9 %collective-permute-start.7 = (bf16[1,1,32,128]{3,2,1,0:T(8,128)(2,1)S(1)}, bf16[1,1,32,128]{3,2,1,0:T(8,128)(2,1)S(1)}, u32[]{:S(2)}, u32[]{:S(2)}) collective-permute-start(bf16[1,1,32,128]{3,2,1,0:T(8,128)(2,1)S(1)} %get-tuple-element.5), channel_id=1, source_target_pairs={{0,1},{1,2},{2,3},{3,4},{4,5},{5,6},{6,7},{8,9},{9,10},{10,11},{11... | collective-permute-start | bytes 24584 | tf_op jit(solution)/shard_map/ppermute | solution.py:16
  42.7 3.6 %collective-permute-start.8 = (bf16[1,1,32,128]{3,2,1,0:T(8,128)(2,1)S(1)}, bf16[1,1,32,128]{3,2,1,0:T(8,128)(2,1)S(1)}, u32[]{:S(2)}, u32[]{:S(2)}) collective-permute-start(bf16[1,1,32,128]{3,2,1,0:T(8,128)(2,1)S(1)} %get-tuple-element.4), channel_id=1, source_target_pairs={{1,0},{2,1},{3,2},{4,3},{5,4},{6,5},{7,6},{9,8},{10,9},{11,10},{12... | collective-permute-start | bytes 24584 | tf_op jit(solution)/shard_map/ppermute | solution.py:17
  48.6 2.0 %collective-permute-start.9 = (bf16[2,32,128]{2,1,0:T(8,128)(2,1)S(1)}, bf16[2,32,128]{2,1,0:T(8,128)(2,1)S(1)}, u32[]{:S(2)}, u32[]{:S(2)}) collective-permute-start(bf16[2,32,128]{2,1,0:T(8,128)(2,1)S(1)} %convert_element_type.42), channel_id=1, source_target_pairs={{0,1},{1,0},{2,3},{3,2},{4,5},{5,4},{6,7},{7,6},{8,9},{9,8},{10,11... | collective-permute-start | bytes 49160 | tf_op jit(solution)/shard_map/ppermute | solution.py:31
  50.6 1.1 collective-permute-done.9
  52.0 3.7 %collective-permute-start.10 = (bf16[2,32,128]{2,1,0:T(8,128)(2,1)S(1)}, bf16[2,32,128]{2,1,0:T(8,128)(2,1)S(1)}, u32[]{:S(2)}, u32[]{:S(2)}) collective-permute-start(bf16[2,32,128]{2,1,0:T(8,128)(2,1)S(1)} %get-tuple-element.17), channel_id=1, source_target_pairs={{0,2},{1,3},{2,0},{3,1},{4,6},{5,7},{6,4},{7,5},{8,10},{9,11},{10,... | collective-permute-start | bytes 49160 | tf_op jit(solution)/shard_map/ppermute | solution.py:31
  55.6 2.0 %collective-permute-done.10 = bf16[2,32,128]{2,1,0:T(8,128)(2,1)S(1)} collective-permute-done((bf16[2,32,128]{2,1,0:T(8,128)(2,1)S(1)}, bf16[2,32,128]{2,1,0:T(8,128)(2,1)S(1)}, u32[]{:S(2)}, u32[]{:S(2)}) %collective-permute-start.10) | collective-permute-done | bytes 16416 | tf_op jit(solution)/shard_map/ppermute | solution.py:31
  57.8 1.9 %collective-permute-start.11 = (bf16[2,32,128]{2,1,0:T(8,128)(2,1)S(1)}, bf16[2,32,128]{2,1,0:T(8,128)(2,1)S(1)}, u32[]{:S(2)}, u32[]{:S(2)}) collective-permute-start(bf16[2,32,128]{2,1,0:T(8,128)(2,1)S(1)} %get-tuple-element.19), channel_id=1, source_target_pairs={{0,4},{1,5},{2,6},{3,7},{4,0},{5,1},{6,2},{7,3},{8,12},{9,13},{10,... | collective-permute-start | bytes 49160 | tf_op jit(solution)/shard_map/ppermute | solution.py:31
  59.8 5.2 %collective-permute-done.11 = bf16[2,32,128]{2,1,0:T(8,128)(2,1)S(1)} collective-permute-done((bf16[2,32,128]{2,1,0:T(8,128)(2,1)S(1)}, bf16[2,32,128]{2,1,0:T(8,128)(2,1)S(1)}, u32[]{:S(2)}, u32[]{:S(2)}) %collective-permute-start.11) | collective-permute-done | bytes 16416 | tf_op jit(solution)/shard_map/ppermute | solution.py:31
  65.2 1.9 %collective-permute-start.12 = (f32[2,32,128]{2,1,0:T(8,128)S(1)}, f32[2,32,128]{2,1,0:T(8,128)S(1)}, u32[]{:S(2)}, u32[]{:S(2)}) collective-permute-start(f32[2,32,128]{2,1,0:T(8,128)S(1)} %fusion.79), channel_id=1, source_target_pairs={{0,8},{8,0},{16,24},{24,16},{32,40},{40,32},{48,56},{56,48},{64,72... | collective-permute-start | bytes 98312 | tf_op jit(solution)/shard_map/ppermute | solution.py:31
  67.1 3.9 %collective-permute-done.12 = f32[2,32,128]{2,1,0:T(8,128)S(1)} collective-permute-done((f32[2,32,128]{2,1,0:T(8,128)S(1)}, f32[2,32,128]{2,1,0:T(8,128)S(1)}, u32[]{:S(2)}, u32[]{:S(2)}) %collective-permute-start.12) | collective-permute-done | bytes 32800 | tf_op jit(solution)/shard_map/ppermute | solution.py:31
  71.2 1.9 %collective-permute-start.13 = (f32[2,32,128]{2,1,0:T(8,128)S(1)}, f32[2,32,128]{2,1,0:T(8,128)S(1)}, u32[]{:S(2)}, u32[]{:S(2)}) collective-permute-start(f32[2,32,128]{2,1,0:T(8,128)S(1)} %fusion.76), channel_id=1, source_target_pairs={{0,16},{8,24},{16,0},{24,8},{32,48},{40,56},{48,32},{56,40},{64,80... | collective-permute-start | bytes 98312 | tf_op jit(solution)/shard_map/ppermute | solution.py:31
  73.2 4.8 %collective-permute-done.13 = f32[2,32,128]{2,1,0:T(8,128)S(1)} collective-permute-done((f32[2,32,128]{2,1,0:T(8,128)S(1)}, f32[2,32,128]{2,1,0:T(8,128)S(1)}, u32[]{:S(2)}, u32[]{:S(2)}) %collective-permute-start.13) | collective-permute-done | bytes 32800 | tf_op jit(solution)/shard_map/ppermute | solution.py:31
  78.2 4.6 %collective-permute-start.14 = (f32[2,32,128]{2,1,0:T(8,128)S(1)}, f32[2,32,128]{2,1,0:T(8,128)S(1)}, u32[]{:S(2)}, u32[]{:S(2)}) collective-permute-start(f32[2,32,128]{2,1,0:T(8,128)S(1)} %fusion.73), channel_id=1, source_target_pairs={{0,32},{8,40},{16,48},{24,56},{32,0},{40,8},{48,16},{56,24},{64,96... | collective-permute-start | bytes 98312 | tf_op jit(solution)/shard_map/ppermute | solution.py:31
  82.7 5.3 %collective-permute-done.14 = f32[2,32,128]{2,1,0:T(8,128)S(1)} collective-permute-done((f32[2,32,128]{2,1,0:T(8,128)S(1)}, f32[2,32,128]{2,1,0:T(8,128)S(1)}, u32[]{:S(2)}, u32[]{:S(2)}) %collective-permute-start.14) | collective-permute-done | bytes 32800 | tf_op jit(solution)/shard_map/ppermute | solution.py:31
  88.3 11.2 %collective-permute-start.15 = (f32[2,32,128]{2,1,0:T(8,128)S(1)}, f32[2,32,128]{2,1,0:T(8,128)S(1)}, u32[]{:S(2)}, u32[]{:S(2)}) collective-permute-start(f32[2,32,128]{2,1,0:T(8,128)S(1)} %fusion.70), channel_id=1, source_target_pairs={{0,64},{8,72},{16,80},{24,88},{32,96},{40,104},{48,112},{56,120},{... | collective-permute-start | bytes 98312 | tf_op jit(solution)/shard_map/ppermute | solution.py:31
  99.5 3.3 %collective-permute-done.15 = f32[2,32,128]{2,1,0:T(8,128)S(1)} collective-permute-done((f32[2,32,128]{2,1,0:T(8,128)S(1)}, f32[2,32,128]{2,1,0:T(8,128)S(1)}, u32[]{:S(2)}, u32[]{:S(2)}) %collective-permute-start.15) | collective-permute-done | bytes 32800 | tf_op jit(solution)/shard_map/ppermute | solution.py:31
  103.0 2.2 %collective-permute-start.16 = (f32[2,32,128]{2,1,0:T(8,128)S(1)}, f32[2,32,128]{2,1,0:T(8,128)S(1)}, u32[]{:S(2)}, u32[]{:S(2)}) collective-permute-start(f32[2,32,128]{2,1,0:T(8,128)S(1)} %fusion.67), channel_id=1, source_target_pairs={{0,128},{8,136},{16,144},{24,152},{32,160},{40,168},{48,176},{56,1... | collective-permute-start | bytes 98312 | tf_op jit(solution)/shard_map/ppermute | solution.py:31
  105.2 3.6 %collective-permute-done.16 = f32[2,32,128]{2,1,0:T(8,128)S(1)} collective-permute-done((f32[2,32,128]{2,1,0:T(8,128)S(1)}, f32[2,32,128]{2,1,0:T(8,128)S(1)}, u32[]{:S(2)}, u32[]{:S(2)}) %collective-permute-start.16) | collective-permute-done | bytes 32800 | tf_op jit(solution)/shard_map/ppermute | solution.py:31
  109.0 3.3 %collective-permute-start.17 = (f32[2,32,128]{2,1,0:T(8,128)S(1)}, f32[2,32,128]{2,1,0:T(8,128)S(1)}, u32[]{:S(2)}, u32[]{:S(2)}) collective-permute-start(f32[2,32,128]{2,1,0:T(8,128)S(1)} %fusion.64), channel_id=1, source_target_pairs={{0,256},{8,264},{16,272},{24,280},{32,288},{40,296},{48,304},{56,3... | collective-permute-start | bytes 98312 | tf_op jit(solution)/shard_map/ppermute | solution.py:31
  112.4 4.3 %collective-permute-done.17 = f32[2,32,128]{2,1,0:T(8,128)S(1)} collective-permute-done((f32[2,32,128]{2,1,0:T(8,128)S(1)}, f32[2,32,128]{2,1,0:T(8,128)S(1)}, u32[]{:S(2)}, u32[]{:S(2)}) %collective-permute-start.17) | collective-permute-done | bytes 32800 | tf_op jit(solution)/shard_map/ppermute | solution.py:31
  116.9 6.0 %collective-permute-start.18 = (f32[2,32,128]{2,1,0:T(8,128)S(1)}, f32[2,32,128]{2,1,0:T(8,128)S(1)}, u32[]{:S(2)}, u32[]{:S(2)}) collective-permute-start(f32[2,32,128]{2,1,0:T(8,128)S(1)} %fusion.61), channel_id=1, source_target_pairs={{0,512},{8,520},{16,528},{24,536},{32,544},{40,552},{48,560},{56,5... | collective-permute-start | bytes 98312 | tf_op jit(solution)/shard_map/ppermute | solution.py:31
  122.9 3.7 %collective-permute-done.18 = f32[2,32,128]{2,1,0:T(8,128)S(1)} collective-permute-done((f32[2,32,128]{2,1,0:T(8,128)S(1)}, f32[2,32,128]{2,1,0:T(8,128)S(1)}, u32[]{:S(2)}, u32[]{:S(2)}) %collective-permute-start.18) | collective-permute-done | bytes 32800 | tf_op jit(solution)/shard_map/ppermute | solution.py:31
  (50 shorter events, 12.4 us)
Async XLA Ops:
  0.6 9.7 %copy-start = (bf16[1,32,128,128]{3,2,1,0:T(8,128)(2,1)S(1)}, bf16[1,32,128,128]{3,2,1,0:T(8,128)(2,1)}, u32[]{:S(2)}) copy-start(bf16[1,32,128,128]{3,2,1,0:T(8,128)(2,1)} %param.7) | copy-start | bytes 3145732
  1.5 8.8 %copy-start.3 = (bf16[1,32,32,128]{3,2,1,0:T(8,128)(2,1)S(1)}, bf16[1,32,32,128]{3,2,1,0:T(8,128)(2,1)}, u32[]{:S(2)}) copy-start(bf16[1,32,32,128]{3,2,1,0:T(8,128)(2,1)} %param.6) | copy-start | bytes 786436
  1.5 21.0 %collective-permute-start.1 = (bf16[1,1,128,128]{3,2,1,0:T(8,128)(2,1)S(1)}, bf16[1,1,128,128]{3,2,1,0:T(8,128)(2,1)S(1)}, u32[]{:S(2)}, u32[]{:S(2)}) collective-permute-start(bf16[1,1,128,128]{3,2,1,0:T(8,128)(2,1)S(1)} %slice.64), channel_id=1, source_target_pairs={{0,1},{1,2},{2,3},{3,4},{4,5},{5,6},{6,7},{8,9},{9,10},{10,11},{11... | collective-permute-start | bytes 98312 | tf_op jit(solution)/shard_map/ppermute | solution.py:25
  4.6 6.1 %copy-start.1 = (bf16[1,32,128,128]{3,2,1,0:T(8,128)(2,1)S(1)}, bf16[1,32,128,128]{3,2,1,0:T(8,128)(2,1)}, u32[]{:S(2)}) copy-start(bf16[1,32,128,128]{3,2,1,0:T(8,128)(2,1)} %param.8) | copy-start | bytes 3145732
  4.6 18.4 %collective-permute-start.2 = (bf16[1,1,32,128]{3,2,1,0:T(8,128)(2,1)S(1)}, bf16[1,1,32,128]{3,2,1,0:T(8,128)(2,1)S(1)}, u32[]{:S(2)}, u32[]{:S(2)}) collective-permute-start(bf16[1,1,32,128]{3,2,1,0:T(8,128)(2,1)S(1)} %get-tuple-element.10), channel_id=1, source_target_pairs={{1,0},{2,1},{3,2},{4,3},{5,4},{6,5},{7,6},{9,8},{10,9},{11,10},{12... | collective-permute-start | bytes 24584 | tf_op jit(solution)/shard_map/ppermute | solution.py:17
  8.4 14.2 %collective-permute-start = (bf16[1,1,32,128]{3,2,1,0:T(8,128)(2,1)S(1)}, bf16[1,1,32,128]{3,2,1,0:T(8,128)(2,1)S(1)}, u32[]{:S(2)}, u32[]{:S(2)}) collective-permute-start(bf16[1,1,32,128]{3,2,1,0:T(8,128)(2,1)S(1)} %get-tuple-element.11), channel_id=1, source_target_pairs={{0,1},{1,2},{2,3},{3,4},{4,5},{5,6},{6,7},{8,9},{9,10},{10,11},{11... | collective-permute-start | bytes 24584 | tf_op jit(solution)/shard_map/ppermute | solution.py:16
  23.6 6.0 %collective-permute-start.3 = (bf16[1,1,32,128]{3,2,1,0:T(8,128)(2,1)S(1)}, bf16[1,1,32,128]{3,2,1,0:T(8,128)(2,1)S(1)}, u32[]{:S(2)}, u32[]{:S(2)}) collective-permute-start(bf16[1,1,32,128]{3,2,1,0:T(8,128)(2,1)S(1)} %get-tuple-element.9), channel_id=1, source_target_pairs={{0,1},{1,2},{2,3},{3,4},{4,5},{5,6},{6,7},{8,9},{9,10},{10,11},{11... | collective-permute-start | bytes 24584 | tf_op jit(solution)/shard_map/ppermute | solution.py:16
  25.9 5.0 %collective-permute-start.4 = (bf16[1,1,32,128]{3,2,1,0:T(8,128)(2,1)S(1)}, bf16[1,1,32,128]{3,2,1,0:T(8,128)(2,1)S(1)}, u32[]{:S(2)}, u32[]{:S(2)}) collective-permute-start(bf16[1,1,32,128]{3,2,1,0:T(8,128)(2,1)S(1)} %get-tuple-element.8), channel_id=1, source_target_pairs={{1,0},{2,1},{3,2},{4,3},{5,4},{6,5},{7,6},{9,8},{10,9},{11,10},{12... | collective-permute-start | bytes 24584 | tf_op jit(solution)/shard_map/ppermute | solution.py:17
  31.6 6.0 %collective-permute-start.5 = (bf16[1,1,32,128]{3,2,1,0:T(8,128)(2,1)S(1)}, bf16[1,1,32,128]{3,2,1,0:T(8,128)(2,1)S(1)}, u32[]{:S(2)}, u32[]{:S(2)}) collective-permute-start(bf16[1,1,32,128]{3,2,1,0:T(8,128)(2,1)S(1)} %get-tuple-element.7), channel_id=1, source_target_pairs={{0,1},{1,2},{2,3},{3,4},{4,5},{5,6},{6,7},{8,9},{9,10},{10,11},{11... | collective-permute-start | bytes 24584 | tf_op jit(solution)/shard_map/ppermute | solution.py:16
  33.9 5.0 %collective-permute-start.6 = (bf16[1,1,32,128]{3,2,1,0:T(8,128)(2,1)S(1)}, bf16[1,1,32,128]{3,2,1,0:T(8,128)(2,1)S(1)}, u32[]{:S(2)}, u32[]{:S(2)}) collective-permute-start(bf16[1,1,32,128]{3,2,1,0:T(8,128)(2,1)S(1)} %get-tuple-element.6), channel_id=1, source_target_pairs={{1,0},{2,1},{3,2},{4,3},{5,4},{6,5},{7,6},{9,8},{10,9},{11,10},{12... | collective-permute-start | bytes 24584 | tf_op jit(solution)/shard_map/ppermute | solution.py:17
  40.4 6.0 %collective-permute-start.7 = (bf16[1,1,32,128]{3,2,1,0:T(8,128)(2,1)S(1)}, bf16[1,1,32,128]{3,2,1,0:T(8,128)(2,1)S(1)}, u32[]{:S(2)}, u32[]{:S(2)}) collective-permute-start(bf16[1,1,32,128]{3,2,1,0:T(8,128)(2,1)S(1)} %get-tuple-element.5), channel_id=1, source_target_pairs={{0,1},{1,2},{2,3},{3,4},{4,5},{5,6},{6,7},{8,9},{9,10},{10,11},{11... | collective-permute-start | bytes 24584 | tf_op jit(solution)/shard_map/ppermute | solution.py:16
  42.7 5.0 %collective-permute-start.8 = (bf16[1,1,32,128]{3,2,1,0:T(8,128)(2,1)S(1)}, bf16[1,1,32,128]{3,2,1,0:T(8,128)(2,1)S(1)}, u32[]{:S(2)}, u32[]{:S(2)}) collective-permute-start(bf16[1,1,32,128]{3,2,1,0:T(8,128)(2,1)S(1)} %get-tuple-element.4), channel_id=1, source_target_pairs={{1,0},{2,1},{3,2},{4,3},{5,4},{6,5},{7,6},{9,8},{10,9},{11,10},{12... | collective-permute-start | bytes 24584 | tf_op jit(solution)/shard_map/ppermute | solution.py:17
  47.7 0.8 copy-start.5
  48.4 3.3 %copy-start.2 = (f32[2,128,128]{2,1,0:T(8,128)S(1)}, f32[2,128,128]{2,1,0:T(8,128)}, u32[]{:S(2)}) copy-start(f32[2,128,128]{2,1,0:T(8,128)} %param.10) | copy-start | bytes 393220
  48.6 3.1 %collective-permute-start.9 = (bf16[2,32,128]{2,1,0:T(8,128)(2,1)S(1)}, bf16[2,32,128]{2,1,0:T(8,128)(2,1)S(1)}, u32[]{:S(2)}, u32[]{:S(2)}) collective-permute-start(bf16[2,32,128]{2,1,0:T(8,128)(2,1)S(1)} %convert_element_type.42), channel_id=1, source_target_pairs={{0,1},{1,0},{2,3},{3,2},{4,5},{5,4},{6,7},{7,6},{8,9},{9,8},{10,11... | collective-permute-start | bytes 49160 | tf_op jit(solution)/shard_map/ppermute | solution.py:31
  52.0 5.6 %collective-permute-start.10 = (bf16[2,32,128]{2,1,0:T(8,128)(2,1)S(1)}, bf16[2,32,128]{2,1,0:T(8,128)(2,1)S(1)}, u32[]{:S(2)}, u32[]{:S(2)}) collective-permute-start(bf16[2,32,128]{2,1,0:T(8,128)(2,1)S(1)} %get-tuple-element.17), channel_id=1, source_target_pairs={{0,2},{1,3},{2,0},{3,1},{4,6},{5,7},{6,4},{7,5},{8,10},{9,11},{10,... | collective-permute-start | bytes 49160 | tf_op jit(solution)/shard_map/ppermute | solution.py:31
  57.8 7.1 %collective-permute-start.11 = (bf16[2,32,128]{2,1,0:T(8,128)(2,1)S(1)}, bf16[2,32,128]{2,1,0:T(8,128)(2,1)S(1)}, u32[]{:S(2)}, u32[]{:S(2)}) collective-permute-start(bf16[2,32,128]{2,1,0:T(8,128)(2,1)S(1)} %get-tuple-element.19), channel_id=1, source_target_pairs={{0,4},{1,5},{2,6},{3,7},{4,0},{5,1},{6,2},{7,3},{8,12},{9,13},{10,... | collective-permute-start | bytes 49160 | tf_op jit(solution)/shard_map/ppermute | solution.py:31
  65.2 5.8 %collective-permute-start.12 = (f32[2,32,128]{2,1,0:T(8,128)S(1)}, f32[2,32,128]{2,1,0:T(8,128)S(1)}, u32[]{:S(2)}, u32[]{:S(2)}) collective-permute-start(f32[2,32,128]{2,1,0:T(8,128)S(1)} %fusion.79), channel_id=1, source_target_pairs={{0,8},{8,0},{16,24},{24,16},{32,40},{40,32},{48,56},{56,48},{64,72... | collective-permute-start | bytes 98312 | tf_op jit(solution)/shard_map/ppermute | solution.py:31
  71.2 6.7 %collective-permute-start.13 = (f32[2,32,128]{2,1,0:T(8,128)S(1)}, f32[2,32,128]{2,1,0:T(8,128)S(1)}, u32[]{:S(2)}, u32[]{:S(2)}) collective-permute-start(f32[2,32,128]{2,1,0:T(8,128)S(1)} %fusion.76), channel_id=1, source_target_pairs={{0,16},{8,24},{16,0},{24,8},{32,48},{40,56},{48,32},{56,40},{64,80... | collective-permute-start | bytes 98312 | tf_op jit(solution)/shard_map/ppermute | solution.py:31
  78.2 9.9 %collective-permute-start.14 = (f32[2,32,128]{2,1,0:T(8,128)S(1)}, f32[2,32,128]{2,1,0:T(8,128)S(1)}, u32[]{:S(2)}, u32[]{:S(2)}) collective-permute-start(f32[2,32,128]{2,1,0:T(8,128)S(1)} %fusion.73), channel_id=1, source_target_pairs={{0,32},{8,40},{16,48},{24,56},{32,0},{40,8},{48,16},{56,24},{64,96... | collective-permute-start | bytes 98312 | tf_op jit(solution)/shard_map/ppermute | solution.py:31
  88.3 14.5 %collective-permute-start.15 = (f32[2,32,128]{2,1,0:T(8,128)S(1)}, f32[2,32,128]{2,1,0:T(8,128)S(1)}, u32[]{:S(2)}, u32[]{:S(2)}) collective-permute-start(f32[2,32,128]{2,1,0:T(8,128)S(1)} %fusion.70), channel_id=1, source_target_pairs={{0,64},{8,72},{16,80},{24,88},{32,96},{40,104},{48,112},{56,120},{... | collective-permute-start | bytes 98312 | tf_op jit(solution)/shard_map/ppermute | solution.py:31
  103.0 5.8 %collective-permute-start.16 = (f32[2,32,128]{2,1,0:T(8,128)S(1)}, f32[2,32,128]{2,1,0:T(8,128)S(1)}, u32[]{:S(2)}, u32[]{:S(2)}) collective-permute-start(f32[2,32,128]{2,1,0:T(8,128)S(1)} %fusion.67), channel_id=1, source_target_pairs={{0,128},{8,136},{16,144},{24,152},{32,160},{40,168},{48,176},{56,1... | collective-permute-start | bytes 98312 | tf_op jit(solution)/shard_map/ppermute | solution.py:31
  109.0 17.8 %copy-start.4 = (f32[256,256]{1,0:T(8,128)S(1)}, f32[256,256]{1,0:T(8,128)}, u32[]{:S(2)}) copy-start(f32[256,256]{1,0:T(8,128)} %param.11) | copy-start | bytes 786436
  109.0 7.6 %collective-permute-start.17 = (f32[2,32,128]{2,1,0:T(8,128)S(1)}, f32[2,32,128]{2,1,0:T(8,128)S(1)}, u32[]{:S(2)}, u32[]{:S(2)}) collective-permute-start(f32[2,32,128]{2,1,0:T(8,128)S(1)} %fusion.64), channel_id=1, source_target_pairs={{0,256},{8,264},{16,272},{24,280},{32,288},{40,296},{48,304},{56,3... | collective-permute-start | bytes 98312 | tf_op jit(solution)/shard_map/ppermute | solution.py:31
  116.9 9.7 %collective-permute-start.18 = (f32[2,32,128]{2,1,0:T(8,128)S(1)}, f32[2,32,128]{2,1,0:T(8,128)S(1)}, u32[]{:S(2)}, u32[]{:S(2)}) collective-permute-start(f32[2,32,128]{2,1,0:T(8,128)S(1)} %fusion.61), channel_id=1, source_target_pairs={{0,512},{8,520},{16,528},{24,536},{32,544},{40,552},{48,560},{56,5... | collective-permute-start | bytes 98312 | tf_op jit(solution)/shard_map/ppermute | solution.py:31
where the time goes:
time: 128 us
  starting transfers between devices  63.1 us (49%)
  waiting for transfers between devices  51.7 us (40%)
  matrix products  9.89 us (8%)
    ppermute x10, starting transfers between devices, from_partner(): return lax.ppermute(value, axis, pairs)  38.7 us
    ppermute x10, waiting for transfers between devices, from_partner(): return lax.ppermute(value, axis, pairs)  37.1 us
    ppermute x4, starting transfers between devices, extended(): after = lax.ppermute(initial, axis, down)  14.7 us
    ppermute x4, waiting for transfers between devices, extended(): before = lax.ppermute(last, axis, up)  11.7 us
    ppermute x4, starting transfers between devices, extended(): before = lax.ppermute(last, axis, up)  7.67 us
    dot_general x4, matrix products, apply_local(): jnp.einsum('nmvs,nmrs->nmvr', next_vals, link_blocks, preferred_element_t...  3.45 us
    ppermute x4, waiting for transfers between devices, extended(): after = lax.ppermute(initial, axis, down)  2.83 us
  transfers between devices with their start and end apart: 19, of which 14 were waited for; matrix products, arithmetic and copies ran while one was open for 3% of the time, Pallas kernels for 0%

commit v1 on v0

v1 whole, which is shorter than its diff:
```python
import functools
import math

import jax
import jax.numpy as jnp
from jax import lax
from jax.experimental import pallas as pl
from jax.experimental.pallas import tpu as pltpu
from jax.sharding import Mesh
from jax.sharding import PartitionSpec as P

TILES = 32
VECS = 32
ROWS = 128
STEPS = 4
HALF = TILES // 2


def coefficients():
    theta, delta = 2.0, 1.7
    sigma = theta / delta
    rho = 1.0 / sigma
    out = []
    for _ in range(STEPS - 1):
        rho_new = 1.0 / (2.0 * sigma - rho)
        out.append((rho_new * rho, 2.0 * rho_new / delta))
        rho = rho_new
    return out


COEFS = coefficients()


def times(a, b):
    return jnp.dot(a, b, preferred_element_type=jnp.float32)


def times_t(a, b):
    return lax.dot_general(a, b, (((1,), (1,)), ((), ())), preferred_element_type=jnp.float32)


def inner_kernel(rhs, diag, link, rel, state, near, sums, resid, direc, dirb):
    for t in range(TILES):
        r = rhs[t].astype(jnp.float32)
        resid[t] = r
        d = r * 0.5
        direc[t] = d
        rel[t] = d
        dirb[0, t] = d.astype(jnp.bfloat16)
    totals = [jnp.zeros((VECS, ROWS), jnp.float32) for _ in range(2)]
    for k in range(1, STEPS + 1):
        now, later = (k - 1) % 2, k % 2
        near[k - 1] = dirb[now, k]
        near[STEPS + k - 1] = dirb[now, TILES - 1 - k]
        for t in range(k, TILES - k):
            a = times(dirb[now, t], diag[t])
            a = a + times(dirb[now, t - 1], link[t - 1])
            a = a + times_t(dirb[now, t + 1], link[t])
            r = resid[t] - a
            resid[t] = r
            if k < STEPS:
                c0, c1 = COEFS[k - 1]
                d = c0 * direc[t] + c1 * r
                direc[t] = d
                rel[t] = rel[t] + d
                dirb[later, t] = d.astype(jnp.bfloat16)
            else:
                totals[t // HALF] += r.astype(jnp.bfloat16).astype(jnp.float32)
    for i, t in enumerate((0, 1, 2, 3, 31, 30, 29, 28)):
        state[0, i] = resid[t]
        state[1, i] = direc[t]
        state[2, i] = rel[t]
    for c in range(2):
        sums[c] = totals[c]


def edge_kernel(flag, lo, hi, diag_lo, link_lo, diag_hi, link_hi, state, near, sums_in, edge, sums):
    def blocks(ref, base, count, height):
        return [ref[base + i * height : base + (i + 1) * height, :] for i in range(count)]

    def sweep_side(rhs, diag, fwd, near_base, state_base, mirrored):
        res, dirs, rel = {}, {}, {}
        for p in range(4):
            r = rhs[p].astype(jnp.float32)
            res[p] = r
            dirs[p] = r * 0.5
        for i in range(4):
            res[4 + i] = state[0, state_base + i]
            dirs[4 + i] = state[1, state_base + i]
            rel[4 + i] = state[2, state_base + i]
        outward = times if mirrored else times_t
        inward = times_t if mirrored else times
        for k in range(1, STEPS + 1):
            bf = {p: dirs[p].astype(jnp.bfloat16) for p in range(k - 1, k + 4)}
            bf[k + 4] = near[near_base + k - 1]
            for p in range(k, k + 4):
                a = times(bf[p], diag[p])
                a = a + inward(bf[p - 1], fwd[p - 1])
                a = a + outward(bf[p + 1], fwd[p])
                r = res[p] - a
                res[p] = r
                if k < STEPS:
                    c0, c1 = COEFS[k - 1]
                    dirs[p] = c0 * dirs[p] + c1 * r
                    if p >= 4:
                        rel[p] = rel[p] + dirs[p]
        total = jnp.zeros((VECS, ROWS), jnp.float32)
        for i in range(4):
            total = total + res[4 + i].astype(jnp.bfloat16).astype(jnp.float32)
            edge[state_base + i] = rel[4 + i]
        return total

    n = 4 * VECS
    rhs_l = blocks(lo, 0, 4, VECS)
    diag_l = [None] + blocks(lo, n, 3, ROWS) + [diag_lo[i] for i in range(4)]
    fwd_l = blocks(lo, n + 3 * ROWS, 4, ROWS) + [link_lo[i] for i in range(4)]
    total_l = sweep_side(rhs_l, diag_l, fwd_l, 0, 0, False)
    sums[0] = sums_in[0] + total_l
    rhs_r = blocks(hi, 0, 4, VECS)[::-1]
    diag_r = [None] + blocks(hi, n, 3, ROWS)[::-1] + [diag_hi[3 - i] for i in range(4)]
    last = link_hi[4]
    last = jnp.where(flag[0] > 0, last, jnp.zeros_like(last))
    fwd_r = blocks(hi, n + 3 * ROWS, 3, ROWS)[::-1] + [last] + [link_hi[3 - i] for i in range(4)]
    total_r = sweep_side(rhs_r, diag_r, fwd_r, 4, 4, True)
    sums[1] = sums_in[1] + total_r


def map_kernel(restrict, level, inverse, out):
    def dot(a, b):
        return jnp.dot(a, b, precision=lax.Precision.HIGHEST, preferred_element_type=jnp.float32)

    scale = 2.0**-5
    r = restrict[...].astype(jnp.float32) * scale
    for c in range(2):
        one = level[c]
        two = dot(one, one)
        four = dot(two, two)
        eight = dot(four, four)
        head = dot(r, two)
        tail = dot(eight, inverse[c * ROWS : (c + 1) * ROWS, :])
        out[c] = dot(head, tail)


def solve_kernel(s, m, out):
    acc = jnp.zeros((VECS, 2 * ROWS), jnp.float32)
    for c in range(2):
        acc = acc + jnp.dot(
            s[c], m[c], precision=lax.Precision.HIGHEST, preferred_element_type=jnp.float32
        )
    out[...] = acc


VMEM = pl.BlockSpec(memory_space=pltpu.VMEM)
SMEM = pl.BlockSpec(memory_space=pltpu.SMEM)
f32 = functools.partial(jax.ShapeDtypeStruct, dtype=jnp.float32)
bf16 = functools.partial(jax.ShapeDtypeStruct, dtype=jnp.bfloat16)


def direct_sum(piece, axis):
    count = lax.axis_size(axis)
    copies = jnp.broadcast_to(piece.astype(jnp.bfloat16)[None], (count,) + piece.shape)
    got = lax.all_to_all(copies, axis, 0, 0, tiled=True)
    return jnp.sum(got.astype(jnp.float32), axis=0)


def total_of(sums):
    sub = ("x", "core")
    flat = sums.reshape(8, 8, ROWS).astype(jnp.bfloat16)
    piece = jnp.sum(lax.all_to_all(flat, sub, 0, 0, tiled=True).astype(jnp.float32), axis=0)
    piece = direct_sum(piece, "y")
    piece = direct_sum(piece, "z")
    copies = jnp.broadcast_to(piece[None], (8,) + piece.shape)
    return lax.all_to_all(copies, sub, 0, 0, tiled=True).reshape(2, VECS, ROWS)


def shards(right_side, diag_blocks, link_blocks, restrict_map, level_map, coarse_inverse):
    rhs, diag, link = right_side[0], diag_blocks[0], link_blocks[0]
    sub = ("x", "core")

    def packed(r, d, k):
        return jnp.concatenate([a.reshape(-1, ROWS) for a in (r, d, k)], axis=0)

    up = [(i, i + 1) for i in range(7)]
    down = [(i + 1, i) for i in range(7)]
    lo = lax.ppermute(packed(rhs[28:], diag[29:], link[28:]), sub, up)
    hi = lax.ppermute(packed(rhs[:4], diag[:3], link[:3]), sub, down)

    rel, state, near, sums = pl.pallas_call(
        inner_kernel,
        out_shape=(
            f32((TILES, VECS, ROWS)),
            f32((3, 8, VECS, ROWS)),
            bf16((8, VECS, ROWS)),
            f32((2, VECS, ROWS)),
        ),
        in_specs=[VMEM] * 3,
        out_specs=(VMEM,) * 4,
        scratch_shapes=[
            pltpu.VMEM((TILES, VECS, ROWS), jnp.float32),
            pltpu.VMEM((TILES, VECS, ROWS), jnp.float32),
            pltpu.VMEM((2, TILES, VECS, ROWS), jnp.bfloat16),
        ],
        compiler_params=pltpu.CompilerParams(vmem_limit_bytes=24 << 20),
        cost_estimate=pl.CostEstimate(flops=4 * 10**8, bytes_accessed=3 << 20, transcendentals=0),
    )(rhs, diag, link)

    maps = pl.pallas_call(
        map_kernel,
        out_shape=f32((2, ROWS, 2 * ROWS)),
        in_specs=[VMEM] * 3,
        out_specs=VMEM,
        compiler_params=pltpu.CompilerParams(vmem_limit_bytes=8 << 20),
        cost_estimate=pl.CostEstimate(flops=4 * 10**8, bytes_accessed=1 << 19, transcendentals=0),
    )(restrict_map, level_map, coarse_inverse)

    j = lax.axis_index("x") * 2 + lax.axis_index("core")
    flag = (j < 7).astype(jnp.int32).reshape(1)
    edge, sums = pl.pallas_call(
        edge_kernel,
        out_shape=(f32((8, VECS, ROWS)), f32((2, VECS, ROWS))),
        in_specs=[SMEM] + [VMEM] * 9,
        out_specs=(VMEM, VMEM),
        compiler_params=pltpu.CompilerParams(vmem_limit_bytes=16 << 20),
        cost_estimate=pl.CostEstimate(flops=10**8, bytes_accessed=1 << 20, transcendentals=0),
    )(flag, lo, hi, diag[:4], link[:4], diag[28:], link[27:], state, near, sums)

    rel = lax.dynamic_update_slice(rel, edge[:4], (0, 0, 0))
    rel = lax.dynamic_update_slice(rel, edge[4:][::-1], (28, 0, 0))

    total = total_of(sums)
    solved = pl.pallas_call(
        solve_kernel,
        out_shape=f32((VECS, 2 * ROWS)),
        in_specs=[VMEM] * 2,
        out_specs=VMEM,
        compiler_params=pltpu.CompilerParams(vmem_limit_bytes=8 << 20),
        cost_estimate=pl.CostEstimate(flops=10**7, bytes_accessed=1 << 18, transcendentals=0),
    )(total, maps)
    return (rel[None], solved[None, None])


def solution(mesh):
    fine = Mesh(mesh.devices.reshape(8, 16, 4, 2), ("y", "z", "x", "core"))
    node, sub = ("y", "z"), ("x", "core")
    big = P(node, sub, None, None)
    return jax.shard_map(
        shards,
        mesh=fine,
        in_specs=(big, big, big, P(), P(), P()),
        out_specs=(big, big),
        check_vma=False,
    )
```

time: 128 us -> 85.8 us (0.67)
  the two profiles are of different devices: /device:TPU:2 before, /device:TPU:1 now
where the time goes in v1:
time: 85.8 us; the launch traced here: 85.4 us
  starting transfers between devices  41.8 us (49%)
  waiting for transfers between devices  19.2 us (22%)
  Pallas kernels  9.29 us (11%)
  blocking collectives  6.52 us (8%)
  local copies, waits for them, and re-layouts  6.26 us (7%)
  other arithmetic  1.47 us (2%)
    all_to_all x2, starting transfers between devices, direct_sum(): got = lax.all_to_all(copies, axis, 0, 0, tiled=True)  17.5 us
    all_to_all x2, waiting for transfers between devices, direct_sum(): got = lax.all_to_all(copies, axis, 0, 0, tiled=True)  15.1 us
    ppermute x1, starting transfers between devices, shards(): hi = lax.ppermute(packed(rhs[:4], diag[:3], link[:3]), sub, down)  12.8 us
    all_to_all x1, starting transfers between devices, total_of(): return lax.all_to_all(copies, sub, 0, 0, tiled=True).reshape(2, VECS, ROWS)  6.81 us
    all_to_all x1, blocking collectives, total_of(): lax.all_to_all(flat, sub, 0, 0, tiled=True).astype(jnp.float32)  6.52 us
    ppermute x1, starting transfers between devices, shards(): lo = lax.ppermute(packed(rhs[28:], diag[29:], link[28:]), sub, up)  4.63 us
    pallas_call x1, Pallas kernels, shards(): pl.pallas_call(inner_kernel, out_shape=(f32((TILES, VECS, ROWS)), f32((3,...  4.62 us
    all_to_all x1, waiting for transfers between devices, total_of(): return lax.all_to_all(copies, sub, 0, 0, tiled=True).reshape(2, VECS, ROWS)  4.1 us
  transfers between devices with their start and end apart: 5, of which 3 were waited for; matrix products, arithmetic and copies ran while one was open for 3% of the time, Pallas kernels for 8%

profile of v1, /device:TPU:1, one launch (start us, length us, event | category | flops | bytes accessed | tf_op | source)
XLA Modules:
  0.0 85.4 jit_solution(8367760362732997135)
XLA Ops:
  0.6 0.0 copy-start.2
  0.6 1.0 %slice_bitcast_fusion.2 = (bf16[4,128,128]{2,1,0:T(8,128)(2,1)S(1)}, bf16[1,4,128,128]{3,2,1,0:T(8,128)(2,1)S(1)}) fusion(bf16[1,32,128,128]{3,2,1,0:T(8,128)(2,1)} %param.8), kind=kLoop, calls=%fused_computation.4 | loop fusion | bytes 524288 | tf_op jit(solution)/shard_map/slice | solution.py:225
  1.7 0.0 copy-start
  1.7 1.0 %fusion = (bf16[1,3,128,128]{3,2,1,0:T(8,128)(2,1)S(1)}, bf16[1,3,128,128]{3,2,1,0:T(8,128)(2,1)S(1)}) fusion(bf16[1,32,128,128]{3,2,1,0:T(8,128)(2,1)} %param.7), kind=kLoop, calls=%fused_computation.9 | loop fusion | bytes 393216 | tf_op jit(solution)/shard_map/slice | solution.py:186
  2.7 0.0 copy-done.2
  2.8 0.7 pad_maximum_fusion
  3.5 4.6 %collective-permute-start = (bf16[1024,128]{1,0:T(8,128)(2,1)}, bf16[1024,128]{1,0:T(8,128)(2,1)S(1)}, u32[]{:S(2)}, u32[]{:S(2)}) collective-permute-start(bf16[1024,128]{1,0:T(8,128)(2,1)} %pad_maximum_fusion), channel_id=1, source_target_pairs={{0,1},{1,2},{2,3},{3,4},{4,5},{5,6},{6,7},{8,9},{9,10},{10,11},{11... | collective-permute-start | bytes 786440 | tf_op jit(solution)/shard_map/ppermute | solution.py:185
  8.1 0.0 slice-done
  8.1 0.7 pad_maximum_fusion.1
  8.8 12.8 %collective-permute-start.1 = (bf16[896,128]{1,0:T(8,128)(2,1)}, bf16[896,128]{1,0:T(8,128)(2,1)S(1)}, u32[]{:S(2)}, u32[]{:S(2)}) collective-permute-start(bf16[896,128]{1,0:T(8,128)(2,1)} %pad_maximum_fusion.1), channel_id=1, source_target_pairs={{1,0},{2,1},{3,2},{4,3},{5,4},{6,5},{7,6},{9,8},{10,9},{11,10},{12... | collective-permute-start | bytes 688136 | tf_op jit(solution)/shard_map/ppermute | solution.py:186
  21.7 1.0 %slice_bitcast_fusion.1 = (bf16[4,128,128]{2,1,0:T(8,128)(2,1)S(1)}, bf16[4,128,128]{2,1,0:T(8,128)(2,1)S(1)}) fusion(bf16[1,32,128,128]{3,2,1,0:T(8,128)(2,1)} %param.7), kind=kLoop, calls=%fused_computation.3 | loop fusion | bytes 524288 | tf_op jit(solution)/shard_map/slice | solution.py:225
  22.7 4.6 %shard_map.77 = (f32[32,32,128]{2,1,0:T(8,128)}, f32[3,8,32,128]{3,2,1,0:T(8,128)S(1)}, bf16[8,32,128]{2,1,0:T(8,128)(2,1)S(1)}, f32[2,32,128]{2,1,0:T(8,128)S(1)}) custom-call(bf16[32,32,128]{2,1,0:T(8,128)(2,1)S(1)} %bitcast.29, bf16[32,128,128]{2,1,0:T(8,128)(2,1)S(1)} %bitcast.28, bf16[32,128,128]{2,1,0:T(8,128)(2,1)S(1)} %bitcast.26), custom_call_target="tpu_custom_call" | custom-call | flops 400000000 | bytes 3145728 | tf_op jit(solution)/shard_map/pallas_call | solution.py:188
  27.3 0.0 collective-permute-done.1.hi
  27.4 0.0 collective-permute-done.lo
  27.4 0.0 copy-start.3
  27.4 0.0 copy-start.5
  27.4 1.6 %shard_map.78 = (f32[8,32,128]{2,1,0:T(8,128)S(1)}, f32[2,32,128]{2,1,0:T(8,128)S(1)}) custom-call(s32[1]{0:T(128)} %bitcast.4.flag, bf16[1024,128]{1,0:T(8,128)(2,1)S(1)} %collective-permute-done.lo, bf16[896,128]{1,0:T(8,128)(2,1)S(1)} %collective-permute-done.1.hi, bf16[4,128,128]{2,1,0:T(8,128)(2,1)S(1)} %get-tuple-element.15.diag_lo, ...), custom_call_target="tpu_custom_call" | custom-call | flops 100000000 | bytes 1048576 | tf_op jit(solution)/shard_map/pallas_call | solution.py:218
  28.9 0.0 copy-start.4
  29.0 6.5 %all_to_all.20 = bf16[8,8,128]{2,1,0:T(8,128)(2,1)S(1)} all-to-all(bf16[8,8,128]{2,1,0:T(8,128)(2,1)S(1)} %bitcast.36), channel_id=1, replica_groups=mesh['y'=8,'z'=16,'x'=4,'core'=2] {'x','core'}, dimensions={0} | all-to-all | bytes 32768 | tf_op jit(solution)/shard_map/all_to_all | solution.py:169
  35.5 0.6 broadcast_in_dim.31
  36.1 3.3 %all-to-all-start.1 = ((bf16[8,8,128]{2,1,0:T(8,128)(2,1)}), bf16[8,8,128]{2,1,0:T(8,128)(2,1)S(1)}, u32[]{:S(2)}, u32[]{:S(2)}) async-start(bf16[8,8,128]{2,1,0:T(8,128)(2,1)} %broadcast_in_dim.31), calls=%async_computation.1 | async-start | bytes 32768 | tf_op jit(solution)/shard_map/all_to_all | solution.py:162
  39.5 2.2 %shard_map.79.m = f32[2,128,256]{2,1,0:T(8,128)S(1)} custom-call(bf16[128,128]{1,0:T(8,128)(2,1)S(1)} %copy-done.5, f32[2,128,128]{2,1,0:T(8,128)S(1)} %copy-done.4, f32[256,256]{1,0:T(8,128)S(1)} %copy-done.3), custom_call_target="tpu_custom_call" | custom-call | flops 400000000 | bytes 524288 | tf_op jit(solution)/shard_map/pallas_call | solution.py:207
  41.7 4.3 %all-to-all-done.1 = bf16[8,8,128]{2,1,0:T(8,128)(2,1)S(1)} async-done(((bf16[8,8,128]{2,1,0:T(8,128)(2,1)}), bf16[8,8,128]{2,1,0:T(8,128)(2,1)S(1)}, u32[]{:S(2)}, u32[]{:S(2)}) %all-to-all-start.1) | async-done | bytes 16416 | tf_op jit(solution)/shard_map/all_to_all | solution.py:162
  46.0 0.6 broadcast_in_dim.32
  46.7 14.2 %all-to-all-start.2 = ((bf16[16,8,128]{2,1,0:T(8,128)(2,1)}), bf16[16,8,128]{2,1,0:T(8,128)(2,1)S(1)}, u32[]{:S(2)}, u32[]{:S(2)}) async-start(bf16[16,8,128]{2,1,0:T(8,128)(2,1)} %broadcast_in_dim.32), calls=%async_computation.2 | async-start | bytes 65536 | tf_op jit(solution)/shard_map/all_to_all | solution.py:162
  60.9 0.6 bitcast_dynamic-update-slice_fusion.1
  61.5 10.8 %all-to-all-done.2 = bf16[16,8,128]{2,1,0:T(8,128)(2,1)S(1)} async-done(((bf16[16,8,128]{2,1,0:T(8,128)(2,1)}), bf16[16,8,128]{2,1,0:T(8,128)(2,1)S(1)}, u32[]{:S(2)}, u32[]{:S(2)}) %all-to-all-start.2) | async-done | bytes 32800 | tf_op jit(solution)/shard_map/all_to_all | solution.py:162
  72.3 0.6 broadcast_in_dim.33
  73.0 6.8 %all-to-all-start.3 = ((f32[8,8,128]{2,1,0:T(8,128)}), f32[8,8,128]{2,1,0:T(8,128)S(1)}, u32[]{:S(2)}, u32[]{:S(2)}) async-start(f32[8,8,128]{2,1,0:T(8,128)} %broadcast_in_dim.33), calls=%async_computation.3 | async-start | bytes 65536 | tf_op jit(solution)/shard_map/all_to_all | solution.py:173
  79.8 0.6 bitcast_dynamic-update-slice_fusion
  80.4 4.1 %all-to-all-done.3 = f32[8,8,128]{2,1,0:T(8,128)S(1)} async-done(((f32[8,8,128]{2,1,0:T(8,128)}), f32[8,8,128]{2,1,0:T(8,128)S(1)}, u32[]{:S(2)}, u32[]{:S(2)}) %all-to-all-start.3) | async-done | bytes 32800 | tf_op jit(solution)/shard_map/all_to_all | solution.py:173
  84.5 0.9 %shard_map.80 = f32[32,256]{1,0:T(8,128)} custom-call(f32[2,32,128]{2,1,0:T(8,128)S(1)} %bitcast.30, f32[2,128,256]{2,1,0:T(8,128)S(1)} %shard_map.79.m), custom_call_target="tpu_custom_call" | custom-call | flops 10000000 | bytes 262144 | tf_op jit(solution)/shard_map/pallas_call | solution.py:231
  (14 shorter events, 0.1 us)
Async XLA Ops:
  0.6 2.1 %copy-start.2 = (bf16[1,32,32,128]{3,2,1,0:T(8,128)(2,1)S(1)}, bf16[1,32,32,128]{3,2,1,0:T(8,128)(2,1)}, u32[]{:S(2)}) copy-start(bf16[1,32,32,128]{3,2,1,0:T(8,128)(2,1)} %param.6) | copy-start | bytes 786436
  1.7 21.0 %copy-start = (bf16[1,32,128,128]{3,2,1,0:T(8,128)(2,1)S(1)}, bf16[1,32,128,128]{3,2,1,0:T(8,128)(2,1)}, u32[]{:S(2)}) copy-start(bf16[1,32,128,128]{3,2,1,0:T(8,128)(2,1)} %param.8) | copy-start | bytes 3145732
  3.5 4.6 %slice-start = ((bf16[1,32,128,128]{3,2,1,0:T(8,128)(2,1)}), bf16[1,3,128,128]{3,2,1,0:T(8,128)(2,1)S(1)}, s32[]{:S(2)}) async-start(bf16[1,32,128,128]{3,2,1,0:T(8,128)(2,1)} %param.8), calls=%async_computation.4 | async-start | bytes 196608 | tf_op jit(solution)/shard_map/slice | solution.py:186
  3.5 19.2 %copy-start.1 = (bf16[1,32,128,128]{3,2,1,0:T(8,128)(2,1)S(1)}, bf16[1,32,128,128]{3,2,1,0:T(8,128)(2,1)}, u32[]{:S(2)}) copy-start(bf16[1,32,128,128]{3,2,1,0:T(8,128)(2,1)} %param.7) | copy-start | bytes 3145732
  3.5 23.9 %collective-permute-start = (bf16[1024,128]{1,0:T(8,128)(2,1)}, bf16[1024,128]{1,0:T(8,128)(2,1)S(1)}, u32[]{:S(2)}, u32[]{:S(2)}) collective-permute-start(bf16[1024,128]{1,0:T(8,128)(2,1)} %pad_maximum_fusion), channel_id=1, source_target_pairs={{0,1},{1,2},{2,3},{3,4},{4,5},{5,6},{6,7},{8,9},{9,10},{10,11},{11... | collective-permute-start | bytes 786440 | tf_op jit(solution)/shard_map/ppermute | solution.py:185
  8.8 18.5 %collective-permute-start.1 = (bf16[896,128]{1,0:T(8,128)(2,1)}, bf16[896,128]{1,0:T(8,128)(2,1)S(1)}, u32[]{:S(2)}, u32[]{:S(2)}) collective-permute-start(bf16[896,128]{1,0:T(8,128)(2,1)} %pad_maximum_fusion.1), channel_id=1, source_target_pairs={{1,0},{2,1},{3,2},{4,3},{5,4},{6,5},{7,6},{9,8},{10,9},{11,10},{12... | collective-permute-start | bytes 688136 | tf_op jit(solution)/shard_map/ppermute | solution.py:186
  27.4 12.1 %copy-start.3 = (f32[256,256]{1,0:T(8,128)S(1)}, f32[256,256]{1,0:T(8,128)}, u32[]{:S(2)}) copy-start(f32[256,256]{1,0:T(8,128)} %inverse.1) | copy-start | bytes 786436
  27.4 12.1 %copy-start.5 = (bf16[128,128]{1,0:T(8,128)(2,1)S(1)}, bf16[128,128]{1,0:T(8,128)(2,1)}, u32[]{:S(2)}) copy-start(bf16[128,128]{1,0:T(8,128)(2,1)} %restrict.1) | copy-start | bytes 98308
  28.9 10.5 %copy-start.4 = (f32[2,128,128]{2,1,0:T(8,128)S(1)}, f32[2,128,128]{2,1,0:T(8,128)}, u32[]{:S(2)}) copy-start(f32[2,128,128]{2,1,0:T(8,128)} %level.1) | copy-start | bytes 393220
  36.1 9.9 %all-to-all-start.1 = ((bf16[8,8,128]{2,1,0:T(8,128)(2,1)}), bf16[8,8,128]{2,1,0:T(8,128)(2,1)S(1)}, u32[]{:S(2)}, u32[]{:S(2)}) async-start(bf16[8,8,128]{2,1,0:T(8,128)(2,1)} %broadcast_in_dim.31), calls=%async_computation.1 | async-start | bytes 32768 | tf_op jit(solution)/shard_map/all_to_all | solution.py:162
  46.7 25.7 %all-to-all-start.2 = ((bf16[16,8,128]{2,1,0:T(8,128)(2,1)}), bf16[16,8,128]{2,1,0:T(8,128)(2,1)S(1)}, u32[]{:S(2)}, u32[]{:S(2)}) async-start(bf16[16,8,128]{2,1,0:T(8,128)(2,1)} %broadcast_in_dim.32), calls=%async_computation.2 | async-start | bytes 65536 | tf_op jit(solution)/shard_map/all_to_all | solution.py:162
  73.0 11.6 %all-to-all-start.3 = ((f32[8,8,128]{2,1,0:T(8,128)}), f32[8,8,128]{2,1,0:T(8,128)S(1)}, u32[]{:S(2)}, u32[]{:S(2)}) async-start(f32[8,8,128]{2,1,0:T(8,128)} %broadcast_in_dim.33), calls=%async_computation.3 | async-start | bytes 65536 | tf_op jit(solution)/shard_map/all_to_all | solution.py:173

commit v2 on v0

v2 whole, which is shorter than its diff:
```python
import functools

import jax
import jax.numpy as jnp
from jax import lax
from jax.experimental import pallas as pl
from jax.experimental.pallas import tpu as pltpu
from jax.sharding import Mesh
from jax.sharding import PartitionSpec as P

TILES = 32
VECS = 32
ROWS = 128
STEPS = 4
HALF = TILES // 2
BF16, F32 = jnp.bfloat16, jnp.float32


def coefficients():
    theta, delta = 2.0, 1.7
    sigma = theta / delta
    rho = 1.0 / sigma
    out = []
    for _ in range(STEPS - 1):
        rho_new = 1.0 / (2.0 * sigma - rho)
        out.append((rho_new * rho, 2.0 * rho_new / delta))
        rho = rho_new
    return out


COEFS = coefficients()
VMEM = pl.BlockSpec(memory_space=pltpu.VMEM)
SMEM = pl.BlockSpec(memory_space=pltpu.SMEM)
HBM = pl.BlockSpec(memory_space=pltpu.HBM)
f32 = functools.partial(jax.ShapeDtypeStruct, dtype=F32)
bf16 = functools.partial(jax.ShapeDtypeStruct, dtype=BF16)


def call(kernel, out_shape, in_specs, out_specs, args, scratch=(), mib=8, cost=(0, 0), **kw):
    return pl.pallas_call(
        kernel,
        out_shape=out_shape,
        in_specs=in_specs,
        out_specs=out_specs,
        scratch_shapes=list(scratch),
        compiler_params=pltpu.CompilerParams(vmem_limit_bytes=int(mib * 2**20)),
        cost_estimate=pl.CostEstimate(flops=cost[0], bytes_accessed=cost[1], transcendentals=0),
        **kw,
    )(*args)


def times(a, b):
    return jnp.dot(a, b, preferred_element_type=F32)


def exact(a, b):
    return jnp.dot(a, b, precision=lax.Precision.HIGHEST, preferred_element_type=F32)


def pack_kernel(info, rhs, diag, link, chip, core, sems):
    def send(up, down):
        parts = (
            (rhs.at[7:8], up.at[0:1]),
            (diag.at[29:32], up.at[1:4]),
            (link.at[28:32], up.at[4:8]),
            (rhs.at[0:1], down.at[0:1]),
            (diag.at[0:3], down.at[1:4]),
            (link.at[0:4], down.at[4:8]),
        )
        copies = [pltpu.make_async_copy(a, b, sems.at[i]) for i, (a, b) in enumerate(parts)]
        for c in copies:
            c.start()
        for c in copies:
            c.wait()

    @pl.when(info[0] == 0)
    def _():
        send(core, chip)

    @pl.when(info[0] != 0)
    def _():
        send(chip, core)


def inner_kernel(rhs, diag, link, rel, state, near, sums, resid, direc, dirb, stack):
    for t in range(1, TILES - 1):
        stack[t, 0:ROWS] = link[t - 1]
        stack[t, ROWS : 2 * ROWS] = diag[t]
        stack[t, 2 * ROWS :] = link[t].T
    for t in (0, TILES - 1):
        r = rhs[t].astype(F32)
        resid[t] = r
        direc[t] = r * 0.5
        rel[t] = r * 0.5
    totals = [jnp.zeros((VECS, ROWS), F32) for _ in range(2)]
    for k in range(1, STEPS + 1):
        now, later = (k - 1) % 2, k % 2

        def moved(t):
            return rhs[t] if k == 1 else dirb[now, t]

        near[k - 1] = moved(k) * BF16(0.5) if k == 1 else moved(k)
        near[STEPS + k - 1] = moved(TILES - 1 - k) * BF16(0.5) if k == 1 else moved(TILES - 1 - k)
        for t in range(k, TILES - k):
            v = jnp.concatenate([moved(t - 1), moved(t), moved(t + 1)], axis=1)
            a = times(v, stack[t])
            if k == 1:
                before = rhs[t].astype(F32)
                r = before - 0.5 * a
                d = before * 0.5
                total = d
            else:
                r = resid[t] - a
                d = direc[t] if k < STEPS else None
                total = rel[t] if k < STEPS else None
            if k < STEPS:
                c0, c1 = COEFS[k - 1]
                d = c0 * d + c1 * r
                rel[t] = total + d
                dirb[later, t] = d.astype(BF16)
                resid[t] = r
                if k < STEPS - 1 or t == k or t == TILES - 1 - k:
                    direc[t] = d
            else:
                totals[t // HALF] += r.astype(BF16).astype(F32)
    for i, t in enumerate((0, 1, 2, 3, 31, 30, 29, 28)):
        state[0, i] = resid[t]
        state[1, i] = direc[t]
        state[2, i] = rel[t]
    for c in range(2):
        sums[c] = totals[c]


def edge_kernel(info, chip, core, diag, link, state, near, sums_in, edge, keep, give, stack, rhs):
    mid, end = slice(ROWS, 2 * ROWS), slice(2 * ROWS, 3 * ROWS)

    def fill(lo, hi):
        for i in range(4):
            rhs[0, i] = lo[0, i * VECS : (i + 1) * VECS, :]
            rhs[1, i] = hi[0, (3 - i) * VECS : (4 - i) * VECS, :]
        for p in (1, 2, 3):
            stack[0, p, 0:ROWS] = lo[4 + p - 1]
            stack[0, p, mid] = lo[p]
            stack[0, p, end] = lo[4 + p].T
            stack[1, p, mid] = hi[4 - p]
            stack[1, p, end] = hi[4 + 3 - p].T
        stack[0, 4, 0:ROWS] = lo[7]
        for p in (1, 2):
            stack[1, p, 0:ROWS] = hi[4 + 2 - p]

    @pl.when(info[0] == 0)
    def _():
        fill(chip, core)

    @pl.when(info[0] != 0)
    def _():
        fill(core, chip)

    last = link[TILES - 1]
    stack[1, 3, 0:ROWS] = jnp.where(info[1] > 0, last, jnp.zeros_like(last))
    for p in range(4, 8):
        if p > 4:
            stack[0, p, 0:ROWS] = link[p - 5]
        stack[0, p, mid] = diag[p - 4]
        stack[0, p, end] = link[p - 4].T
        stack[1, p, 0:ROWS] = link[34 - p]
        stack[1, p, mid] = diag[35 - p]
        stack[1, p, end] = link[35 - p].T

    res, dirs, rel = [{}, {}], [{}, {}], [{}, {}]
    for s in range(2):
        for p in range(4):
            r = rhs[s, p].astype(F32)
            res[s][p] = r
            dirs[s][p] = r * 0.5
        for i in range(4):
            res[s][4 + i] = state[0, 4 * s + i]
            dirs[s][4 + i] = state[1, 4 * s + i]
            rel[s][4 + i] = state[2, 4 * s + i]
    for k in range(1, STEPS + 1):
        bf = [{p: dirs[s][p].astype(BF16) for p in range(k - 1, k + 4)} for s in range(2)]
        for s in range(2):
            bf[s][k + 4] = near[4 * s + k - 1]
        for p in range(k, k + 4):
            for s in range(2):
                order = (p - 1, p, p + 1) if s == 0 else (p + 1, p, p - 1)
                v = jnp.concatenate([bf[s][q] for q in order], axis=1)
                r = res[s][p] - times(v, stack[s, p])
                res[s][p] = r
                if k < STEPS:
                    c0, c1 = COEFS[k - 1]
                    dirs[s][p] = c0 * dirs[s][p] + c1 * r
                    if p >= 4:
                        rel[s][p] = rel[s][p] + dirs[s][p]
    totals = []
    for s in range(2):
        total = sums_in[s]
        for i in range(4):
            total = total + res[s][4 + i].astype(BF16).astype(F32)
            edge[4 * s + (i if s == 0 else 3 - i)] = rel[s][4 + i]
        totals.append(total)
    own = info[0] == 0
    keep[...] = jnp.where(own, totals[0], totals[1])
    give[...] = jnp.where(own, totals[1], totals[0]).astype(BF16)


def place_kernel(edge, inner, rel, sems):
    parts = ((edge.at[0:4], rel.at[0:4]), (inner.at[4:28], rel.at[4:28]), (edge.at[4:8], rel.at[28:32]))
    copies = [pltpu.make_async_copy(a, b, sems.at[i]) for i, (a, b) in enumerate(parts)]
    for c in copies:
        c.start()
    for c in copies:
        c.wait()


def spread_kernel(count, a, b, out):
    s = (a[...] + b[...].astype(F32)).astype(BF16)
    for i in range(count):
        out[i] = s


def sum_of(ref):
    parts = [ref[i].astype(F32) for i in range(ref.shape[0])]
    while len(parts) > 1:
        parts = [parts[i] + parts[i + 1] for i in range(0, len(parts), 2)]
    return parts[0]


def merge_kernel(count, got, out):
    s = sum_of(got).astype(BF16)
    for i in range(count):
        out[i] = s


def total_kernel(got, out):
    out[...] = sum_of(got)


def halves(a):
    top = a.astype(BF16)
    return top, (a - top.astype(F32)).astype(BF16)


def map_kernel(restrict, level, inverse, top, rest):
    r = restrict[...].astype(F32) * 2.0**-5
    for c in range(2):
        one = level[c]
        two = exact(one, one)
        four = exact(two, two)
        eight = exact(four, four)
        head = exact(r, two)
        tail = exact(eight, inverse[c * ROWS : (c + 1) * ROWS, :])
        top[c], rest[c] = halves(exact(head, tail))


def mapped(x, top, rest):
    x_top, x_rest = halves(x)
    return times(x_top, top) + (times(x_top, rest) + times(x_rest, top))


def own_kernel(info, mine, top, rest, out):
    c = info[0]
    out[...] = mapped(mine[...], top[c], rest[c])


def solve_kernel(info, part, other, top, rest, out):
    c = 1 - info[0]
    out[...] = part[...] + mapped(other[...], top[c], rest[c])


def shards(right_side, diag_blocks, link_blocks, restrict_map, level_map, coarse_inverse):
    rhs, diag, link = right_side[0], diag_blocks[0], link_blocks[0]
    tile, pack = (VECS, ROWS), (8, ROWS, ROWS)
    half = lax.axis_index("core")
    j = lax.axis_index("x") * 2 + half
    info = jnp.stack([half, (j < 7).astype(jnp.int32)]).astype(jnp.int32)

    to_chip, to_core = call(
        pack_kernel,
        (bf16(pack), bf16(pack)),
        [SMEM] + [HBM] * 3,
        (VMEM, VMEM),
        (info, rhs.reshape(8, ROWS, ROWS), diag, link),
        scratch=[pltpu.SemaphoreType.DMA((6,))],
        mib=53.25,
        cost=(0, 1 << 20),
    )
    across = [(1, 2), (2, 1), (3, 4), (4, 3), (5, 6), (6, 5)]
    swap = [(0, 1), (1, 0)]
    chip = lax.ppermute(to_chip, ("x", "core"), across)
    core = lax.ppermute(to_core, "core", swap)

    rel, state, near, sums = call(
        inner_kernel,
        (f32((TILES,) + tile), f32((3, 8) + tile), bf16((8,) + tile), f32((2,) + tile)),
        [VMEM] * 3,
        (VMEM,) * 4,
        (rhs, diag, link),
        scratch=[
            pltpu.VMEM((TILES,) + tile, F32),
            pltpu.VMEM((TILES,) + tile, F32),
            pltpu.VMEM((2, TILES) + tile, BF16),
            pltpu.VMEM((TILES, 3 * ROWS, ROWS), BF16),
        ],
        mib=24,
        cost=(4 * 10**8, 3 << 20),
    )
    edge, keep, give = call(
        edge_kernel,
        (f32((8,) + tile), f32(tile), bf16(tile)),
        [SMEM] + [VMEM] * 7,
        (VMEM,) * 3,
        (info, chip, core, diag, link, state, near, sums),
        scratch=[pltpu.VMEM((2, 8, 3 * ROWS, ROWS), BF16), pltpu.VMEM((2, 4) + tile, BF16)],
        mib=16,
        cost=(10**8, 1 << 20),
    )

    got = lax.ppermute(give, "core", swap)
    copies = call(
        functools.partial(spread_kernel, 32), bf16((32,) + tile), [VMEM] * 2, VMEM, (keep, got), cost=(0, 1 << 18)
    )
    copies = lax.all_to_all(copies, ("y", "x"), 0, 0, tiled=True)
    copies = call(functools.partial(merge_kernel, 16), bf16((16,) + tile), [VMEM], VMEM, (copies,), cost=(0, 1 << 18))
    copies, restrict_map, edge = lax.optimization_barrier((copies, restrict_map, edge))
    copies = lax.all_to_all(copies, "z", 0, 0, tiled=True)
    top, rest = call(
        map_kernel,
        (bf16((2, ROWS, 2 * ROWS)),) * 2,
        [VMEM] * 3,
        (VMEM,) * 2,
        (restrict_map, level_map, coarse_inverse),
        cost=(4 * 10**8, 1 << 19),
    )
    rel = call(
        place_kernel,
        f32((TILES,) + tile),
        [VMEM, VMEM],
        HBM,
        (edge, rel),
        scratch=[pltpu.SemaphoreType.DMA((3,))],
        cost=(0, 1 << 20),
    )
    mine = call(total_kernel, f32(tile), [VMEM], VMEM, (copies,), cost=(0, 1 << 17))
    mine, top, rest, rel = lax.optimization_barrier((mine, top, rest, rel))
    other = lax.ppermute(mine, "core", swap)
    wide = f32((VECS, 2 * ROWS))
    part = call(own_kernel, wide, [SMEM] + [VMEM] * 3, VMEM, (info, mine, top, rest), cost=(10**7, 1 << 17))
    solved = call(
        solve_kernel, wide, [SMEM] + [VMEM] * 4, VMEM, (info, part, other, top, rest), cost=(10**7, 1 << 17)
    )
    return (rel[None], solved[None, None])


def solution(mesh):
    fine = Mesh(mesh.devices.reshape(8, 16, 4, 2), ("y", "z", "x", "core"))
    big = P(("y", "z"), ("x", "core"), None, None)
    return jax.shard_map(
        shards,
        mesh=fine,
        in_specs=(big, big, big, P(), P(), P()),
        out_specs=(big, big),
        check_vma=False,
    )
```

time: 128 us -> 76.8 us (0.60)
  the two profiles are of different devices: /device:TPU:2 before, /device:TPU:1 now
where the time goes in v2:
time: 76.8 us; the launch traced here: 76.4 us
  starting transfers between devices  38.9 us (51%)
  blocking collectives  15.1 us (20%)
  Pallas kernels  11.4 us (15%)
  waiting for transfers between devices  9.85 us (13%)
  between operations  0.79 us (1%)
    all_to_all x1, blocking collectives, shards(): copies = lax.all_to_all(copies, ('y', 'x'), 0, 0, tiled=True)  15.1 us
    all_to_all x1, starting transfers between devices, shards(): copies = lax.all_to_all(copies, 'z', 0, 0, tiled=True)  14.3 us
    ppermute x1, starting transfers between devices, shards(): core = lax.ppermute(to_core, 'core', swap)  12.2 us
    pallas_call x10, Pallas kernels, call(): pl.pallas_call(kernel, out_shape=out_shape, in_specs=in_specs, out_specs=...  11.4 us
    all_to_all x1, waiting for transfers between devices, shards(): copies = lax.all_to_all(copies, 'z', 0, 0, tiled=True)  8.57 us
    ppermute x1, starting transfers between devices, shards(): other = lax.ppermute(mine, 'core', swap)  5.86 us
    ppermute x1, starting transfers between devices, shards(): chip = lax.ppermute(to_chip, ('x', 'core'), across)  4.51 us
    ppermute x1, starting transfers between devices, shards(): got = lax.ppermute(give, 'core', swap)  1.92 us
  transfers between devices with their start and end apart: 5, of which 3 were waited for; matrix products, arithmetic and copies ran while one was open for 0% of the time, Pallas kernels for 8%

profile of v2, /device:TPU:1, one launch (start us, length us, event | category | flops | bytes accessed | tf_op | source)
XLA Modules:
  0.0 76.4 jit_solution(17424393842685467020)
XLA Ops:
  0.6 0.1 pad_add_fusion.info
  0.7 0.0 copy-start
  0.7 0.0 copy-start.1
  0.7 0.0 copy-start.2
  0.7 1.8 %shard_map.77 = (bf16[8,128,128]{2,1,0:T(8,128)(2,1)S(1)}, bf16[8,128,128]{2,1,0:T(8,128)(2,1)S(1)}) custom-call(s32[2]{0:T(128)S(1)} %pad_add_fusion.info, bf16[8,128,128]{2,1,0:T(8,128)(2,1)} %bitcast.14, bf16[32,128,128]{2,1,0:T(8,128)(2,1)} %bitcast.8, bf16[32,128,128]{2,1,0:T(8,128)(2,1)} %bitcast.11), custom_call_target="tpu_custom_call" | custom-call | bytes 1048576 | tf_op jit(solution)/shard_map/pallas_call | solution.py:40
  2.6 4.5 %collective-permute-start = (bf16[8,128,128]{2,1,0:T(8,128)(2,1)S(1)}, bf16[8,128,128]{2,1,0:T(8,128)(2,1)S(1)}, u32[]{:S(2)}, u32[]{:S(2)}) collective-permute-start(bf16[8,128,128]{2,1,0:T(8,128)(2,1)S(1)} %get-tuple-element.20), channel_id=1, source_target_pairs={{1,2},{2,1},{3,4},{4,3},{5,6},{6,5},{9,10},{10,9},{11,12},{12,11},... | collective-permute-start | bytes 786440 | tf_op jit(solution)/shard_map/ppermute | solution.py:290
  7.1 12.2 %collective-permute-start.1 = (bf16[8,128,128]{2,1,0:T(8,128)(2,1)S(1)}, bf16[8,128,128]{2,1,0:T(8,128)(2,1)S(1)}, u32[]{:S(2)}, u32[]{:S(2)}) collective-permute-start(bf16[8,128,128]{2,1,0:T(8,128)(2,1)S(1)} %get-tuple-element.21), channel_id=1, source_target_pairs={{0,1},{1,0},{2,3},{3,2},{4,5},{5,4},{6,7},{7,6},{8,9},{9,8},{10,11... | collective-permute-start | bytes 786440 | tf_op jit(solution)/shard_map/ppermute | solution.py:291
  19.3 0.0 copy-done
  19.3 0.0 copy-done.1
  19.4 0.0 copy-done.2
  19.4 2.3 %shard_map.78 = (f32[32,32,128]{2,1,0:T(8,128)S(1)}, f32[3,8,32,128]{3,2,1,0:T(8,128)S(1)}, bf16[8,32,128]{2,1,0:T(8,128)(2,1)S(1)}, f32[2,32,128]{2,1,0:T(8,128)S(1)}) custom-call(bf16[32,32,128]{2,1,0:T(8,128)(2,1)S(1)} %bitcast.15, bf16[32,128,128]{2,1,0:T(8,128)(2,1)S(1)} %bitcast.9, bf16[32,128,128]{2,1,0:T(8,128)(2,1)S(1)} %bitcast.12), custom_call_target="tpu_custom_call" | custom-call | flops 400000000 | bytes 3145728 | tf_op jit(solution)/shard_map/pallas_call | solution.py:40
  21.6 0.0 collective-permute-done.chip
  21.7 0.0 collective-permute-done.1.core
  21.7 1.5 %shard_map.79 = (f32[8,32,128]{2,1,0:T(8,128)S(1)}, f32[32,128]{1,0:T(8,128)S(1)}, bf16[32,128]{1,0:T(8,128)(2,1)S(1)}) custom-call(s32[2]{0:T(128)S(1)} %pad_add_fusion.info, bf16[8,128,128]{2,1,0:T(8,128)(2,1)S(1)} %collective-permute-done.chip, bf16[8,128,128]{2,1,0:T(8,128)(2,1)S(1)} %collective-permute-done.1.core, bf16[32,128,128]{2,1,0:T(8,128)(2,1)S(1)} %bitcast.10, ...), custom_call_target="tpu_custom_call" | custom-call | flops 100000000 | bytes 1048576 | tf_op jit(solution)/shard_map/pallas_call | solution.py:40
  23.2 1.9 %collective-permute-start.2 = (bf16[32,128]{1,0:T(8,128)(2,1)S(1)}, bf16[32,128]{1,0:T(8,128)(2,1)S(1)}, u32[]{:S(2)}, u32[]{:S(2)}) collective-permute-start(bf16[32,128]{1,0:T(8,128)(2,1)S(1)} %get-tuple-element.26), channel_id=1, source_target_pairs={{0,1},{1,0},{2,3},{3,2},{4,5},{5,4},{6,7},{7,6},{8,9},{9,8},{10,11... | collective-permute-start | bytes 24584 | tf_op jit(solution)/shard_map/ppermute | solution.py:319
  25.1 1.1 %collective-permute-done.2.b = bf16[32,128]{1,0:T(8,128)(2,1)S(1)} collective-permute-done((bf16[32,128]{1,0:T(8,128)(2,1)S(1)}, bf16[32,128]{1,0:T(8,128)(2,1)S(1)}, u32[]{:S(2)}, u32[]{:S(2)}) %collective-permute-start.2) | collective-permute-done | bytes 8224 | tf_op jit(solution)/shard_map/ppermute | solution.py:319
  26.3 15.1 %all_to_all.10.got = bf16[32,32,128]{2,1,0:T(8,128)(2,1)S(1)} all-to-all(bf16[32,32,128]{2,1,0:T(8,128)(2,1)S(1)} %shard_map.80), channel_id=1, replica_groups=mesh['y'=8,'z'=16,'x'=4,'core'=2] {'y','x'}, dimensions={0} | all-to-all | bytes 524288 | tf_op jit(solution)/shard_map/all_to_all | solution.py:323
  41.4 0.7 shard_map.81
  42.1 14.3 %all-to-all-start.1 = ((bf16[16,32,128]{2,1,0:T(8,128)(2,1)}), bf16[16,32,128]{2,1,0:T(8,128)(2,1)S(1)}, u32[]{:S(2)}, u32[]{:S(2)}) async-start(bf16[16,32,128]{2,1,0:T(8,128)(2,1)} %shard_map.81), calls=%async_computation.1 | async-start | bytes 262144 | tf_op jit(solution)/shard_map/all_to_all | solution.py:326
  56.4 0.0 copy-start.3
  56.4 0.0 copy-start.4
  56.4 0.0 copy-start.5
  56.4 0.8 %shard_map.84 = f32[32,32,128]{2,1,0:T(8,128)} custom-call(f32[8,32,128]{2,1,0:T(8,128)S(1)} %get-tuple-element.32.edge, f32[32,32,128]{2,1,0:T(8,128)S(1)} %get-tuple-element.33.inner), custom_call_target="tpu_custom_call" | custom-call | bytes 1048576 | tf_op jit(solution)/shard_map/pallas_call | solution.py:40
  57.3 0.2 copy-done.3
  57.4 0.1 copy-done.4
  57.6 0.0 copy-done.5
  57.6 2.2 %shard_map.83 = (bf16[2,128,256]{2,1,0:T(8,128)(2,1)S(1)}, bf16[2,128,256]{2,1,0:T(8,128)(2,1)S(1)}) custom-call(bf16[128,128]{1,0:T(8,128)(2,1)S(1)} %copy-done.5, f32[2,128,128]{2,1,0:T(8,128)S(1)} %copy-done.4, f32[256,256]{1,0:T(8,128)S(1)} %copy-done.3), custom_call_target="tpu_custom_call" | custom-call | flops 400000000 | bytes 524288 | tf_op jit(solution)/shard_map/pallas_call | solution.py:40
  59.8 8.6 %all-to-all-done.1.got = bf16[16,32,128]{2,1,0:T(8,128)(2,1)S(1)} async-done(((bf16[16,32,128]{2,1,0:T(8,128)(2,1)}), bf16[16,32,128]{2,1,0:T(8,128)(2,1)S(1)}, u32[]{:S(2)}, u32[]{:S(2)}) %all-to-all-start.1) | async-done | bytes 131104 | tf_op jit(solution)/shard_map/all_to_all | solution.py:326
  68.4 5.9 %collective-permute-start.3 = (f32[32,128]{1,0:T(8,128)S(1)}, f32[32,128]{1,0:T(8,128)S(1)}, u32[]{:S(2)}, u32[]{:S(2)}) collective-permute-start(f32[32,128]{1,0:T(8,128)S(1)} %shard_map.82.mine), channel_id=1, source_target_pairs={{0,1},{1,0},{2,3},{3,2},{4,5},{5,4},{6,7},{7,6},{8,9},{9,8},{10,11... | collective-permute-start | bytes 49160 | tf_op jit(solution)/shard_map/ppermute | solution.py:346
  74.3 0.7 shard_map.85.part
  75.0 0.1 collective-permute-done.3.other
  75.1 1.3 %shard_map.86 = f32[32,256]{1,0:T(8,128)} custom-call(s32[2]{0:T(128)S(1)} %pad_add_fusion.info, f32[32,256]{1,0:T(8,128)S(1)} %shard_map.85.part, f32[32,128]{1,0:T(8,128)S(1)} %collective-permute-done.3.other, bf16[2,128,256]{2,1,0:T(8,128)(2,1)S(1)} %get-tuple-element.36.top, bf16[2,128,256]{2,1,0:T(8,128)(2,1)S(1)} %get-tuple-element.37.rest), custom_call_target="tpu_custom_call" | custom-call | flops 10000000 | bytes 131072 | tf_op jit(solution)/shard_map/pallas_call | solution.py:40
  (2 shorter events, 0.0 us)
Async XLA Ops:
  0.7 18.6 %copy-start = (bf16[1,32,128,128]{3,2,1,0:T(8,128)(2,1)S(1)}, bf16[1,32,128,128]{3,2,1,0:T(8,128)(2,1)}, u32[]{:S(2)}) copy-start(bf16[1,32,128,128]{3,2,1,0:T(8,128)(2,1)} %param.7) | copy-start | bytes 3145732
  0.7 18.6 %copy-start.1 = (bf16[1,32,128,128]{3,2,1,0:T(8,128)(2,1)S(1)}, bf16[1,32,128,128]{3,2,1,0:T(8,128)(2,1)}, u32[]{:S(2)}) copy-start(bf16[1,32,128,128]{3,2,1,0:T(8,128)(2,1)} %param.8) | copy-start | bytes 3145732
  0.7 18.6 %copy-start.2 = (bf16[1,32,32,128]{3,2,1,0:T(8,128)(2,1)S(1)}, bf16[1,32,32,128]{3,2,1,0:T(8,128)(2,1)}, u32[]{:S(2)}) copy-start(bf16[1,32,32,128]{3,2,1,0:T(8,128)(2,1)} %param.6) | copy-start | bytes 786436
  2.6 19.1 %collective-permute-start = (bf16[8,128,128]{2,1,0:T(8,128)(2,1)S(1)}, bf16[8,128,128]{2,1,0:T(8,128)(2,1)S(1)}, u32[]{:S(2)}, u32[]{:S(2)}) collective-permute-start(bf16[8,128,128]{2,1,0:T(8,128)(2,1)S(1)} %get-tuple-element.20), channel_id=1, source_target_pairs={{1,2},{2,1},{3,4},{4,3},{5,6},{6,5},{9,10},{10,9},{11,12},{12,11},... | collective-permute-start | bytes 786440 | tf_op jit(solution)/shard_map/ppermute | solution.py:290
  7.1 14.6 %collective-permute-start.1 = (bf16[8,128,128]{2,1,0:T(8,128)(2,1)S(1)}, bf16[8,128,128]{2,1,0:T(8,128)(2,1)S(1)}, u32[]{:S(2)}, u32[]{:S(2)}) collective-permute-start(bf16[8,128,128]{2,1,0:T(8,128)(2,1)S(1)} %get-tuple-element.21), channel_id=1, source_target_pairs={{0,1},{1,0},{2,3},{3,2},{4,5},{5,4},{6,7},{7,6},{8,9},{9,8},{10,11... | collective-permute-start | bytes 786440 | tf_op jit(solution)/shard_map/ppermute | solution.py:291
  23.2 3.1 %collective-permute-start.2 = (bf16[32,128]{1,0:T(8,128)(2,1)S(1)}, bf16[32,128]{1,0:T(8,128)(2,1)S(1)}, u32[]{:S(2)}, u32[]{:S(2)}) collective-permute-start(bf16[32,128]{1,0:T(8,128)(2,1)S(1)} %get-tuple-element.26), channel_id=1, source_target_pairs={{0,1},{1,0},{2,3},{3,2},{4,5},{5,4},{6,7},{7,6},{8,9},{9,8},{10,11... | collective-permute-start | bytes 24584 | tf_op jit(solution)/shard_map/ppermute | solution.py:319
  42.1 26.3 %all-to-all-start.1 = ((bf16[16,32,128]{2,1,0:T(8,128)(2,1)}), bf16[16,32,128]{2,1,0:T(8,128)(2,1)S(1)}, u32[]{:S(2)}, u32[]{:S(2)}) async-start(bf16[16,32,128]{2,1,0:T(8,128)(2,1)} %shard_map.81), calls=%async_computation.1 | async-start | bytes 262144 | tf_op jit(solution)/shard_map/all_to_all | solution.py:326
  56.4 1.0 %copy-start.3 = (f32[256,256]{1,0:T(8,128)S(1)}, f32[256,256]{1,0:T(8,128)}, u32[]{:S(2)}) copy-start(f32[256,256]{1,0:T(8,128)} %inverse.1) | copy-start | bytes 786436
  56.4 1.2 %copy-start.4 = (f32[2,128,128]{2,1,0:T(8,128)S(1)}, f32[2,128,128]{2,1,0:T(8,128)}, u32[]{:S(2)}) copy-start(f32[2,128,128]{2,1,0:T(8,128)} %level.1) | copy-start | bytes 393220
  56.4 1.2 %copy-start.5 = (bf16[128,128]{1,0:T(8,128)(2,1)S(1)}, bf16[128,128]{1,0:T(8,128)(2,1)}, u32[]{:S(2)}) copy-start(bf16[128,128]{1,0:T(8,128)(2,1)} %restrict) | copy-start | bytes 98308
  68.4 6.7 %collective-permute-start.3 = (f32[32,128]{1,0:T(8,128)S(1)}, f32[32,128]{1,0:T(8,128)S(1)}, u32[]{:S(2)}, u32[]{:S(2)}) collective-permute-start(f32[32,128]{1,0:T(8,128)S(1)} %shard_map.82.mine), channel_id=1, source_target_pairs={{0,1},{1,0},{2,3},{3,2},{4,5},{5,4},{6,7},{7,6},{8,9},{9,8},{10,11... | collective-permute-start | bytes 49160 | tf_op jit(solution)/shard_map/ppermute | solution.py:346

commit v3 on v2

--- a/solution.py
+++ b/solution.py
@@ -57,32 +57,30 @@
     return jnp.dot(a, b, precision=lax.Precision.HIGHEST, preferred_element_type=F32)
 
 
-def pack_kernel(info, rhs, diag, link, chip, core, sems):
-    def send(up, down):
-        parts = (
-            (rhs.at[7:8], up.at[0:1]),
-            (diag.at[29:32], up.at[1:4]),
-            (link.at[28:32], up.at[4:8]),
-            (rhs.at[0:1], down.at[0:1]),
-            (diag.at[0:3], down.at[1:4]),
-            (link.at[0:4], down.at[4:8]),
-        )
-        copies = [pltpu.make_async_copy(a, b, sems.at[i]) for i, (a, b) in enumerate(parts)]
-        for c in copies:
-            c.start()
-        for c in copies:
-            c.wait()
-
-    @pl.when(info[0] == 0)
-    def _():
-        send(core, chip)
-
-    @pl.when(info[0] != 0)
-    def _():
-        send(chip, core)
-
-
-def inner_kernel(rhs, diag, link, rel, state, near, sums, resid, direc, dirb, stack):
+def pack_kernel(info, rhs, diag, link, out, sems):
+    c = info[0]
+    parts = (
+        (rhs.at[pl.ds(7 * c, 1)], out.at[0:1]),
+        (diag.at[pl.ds(29 * c, 3)], out.at[1:4]),
+        (link.at[pl.ds(28 * c, 4)], out.at[4:8]),
+    )
+    copies = [pltpu.make_async_copy(src, dst, sems.at[i]) for i, (src, dst) in enumerate(parts)]
+    for copy in copies:
+        copy.start()
+    for copy in copies:
+        copy.wait()
+
+
+def halves(a):
+    top = a.astype(BF16)
+    return top, (a - top.astype(F32)).astype(BF16)
+
+
+def rows(i):
+    return slice(i * VECS, (i + 1) * VECS)
+
+
+def inner_kernel(info, rhs, diag, link, rel, state, near, sums, pass_on, resid, direc, dirb, stack):
     for t in range(1, TILES - 1):
         stack[t, 0:ROWS] = link[t - 1]
         stack[t, ROWS : 2 * ROWS] = diag[t]
@@ -130,93 +128,182 @@
     for c in range(2):
         sums[c] = totals[c]
 
-
-def edge_kernel(info, chip, core, diag, link, state, near, sums_in, edge, keep, give, stack, rhs):
-    mid, end = slice(ROWS, 2 * ROWS), slice(2 * ROWS, 3 * ROWS)
-
-    def fill(lo, hi):
-        for i in range(4):
-            rhs[0, i] = lo[0, i * VECS : (i + 1) * VECS, :]
-            rhs[1, i] = hi[0, (3 - i) * VECS : (4 - i) * VECS, :]
+    def fill(diag0, link0, near0, order, group):
+        for i in range(4):
+            pass_on[i] = diag[diag0 + i]
+        for i in range(5):
+            pass_on[4 + i] = link[link0 + i]
+        for i in range(4):
+            pass_on[9, rows(i), :] = near[near0 + i]
+            for which in range(2):
+                top, rest = halves(state[which, order[i]])
+                pass_on[10 + 2 * which, rows(i), :] = top
+                pass_on[11 + 2 * which, rows(i), :] = rest
+        top, rest = halves(totals[group])
+        for i in range(2):
+            pass_on[14, rows(2 * i), :] = top
+            pass_on[14, rows(2 * i + 1), :] = rest
+
+    @pl.when(info[0] == 0)
+    def _():
+        fill(28, 27, 4, (7, 6, 5, 4), 1)
+
+    @pl.when(info[0] != 0)
+    def _():
+        fill(0, 0, 0, (0, 1, 2, 3), 0)
+
+
+def sweep(k, span, stack, res, dirs, rel, bf):
+    for p in span:
+        v = jnp.concatenate([bf[p - 1], bf[p], bf[p + 1]], axis=1)
+        r = res[p] - times(v, stack[p])
+        res[p] = r
+        if k < STEPS:
+            c0, c1 = COEFS[k - 1]
+            dirs[p] = c0 * dirs[p] + c1 * r
+            if p in rel:
+                rel[p] = rel[p] + dirs[p]
+
+
+def total(res, span):
+    parts = [res[p].astype(BF16).astype(F32) for p in span]
+    return (parts[0] + parts[1]) + (parts[2] + parts[3])
+
+
+ONE, TWO, THREE = slice(0, ROWS), slice(ROWS, 2 * ROWS), slice(2 * ROWS, 3 * ROWS)
+
+
+def outer_kernel(info, chip, diag, link, state, near, edge, part, stack, rhs):
+    @pl.when(info[0] == 0)
+    def _():
+        for i in range(4):
+            rhs[i] = chip[0, rows(i), :]
         for p in (1, 2, 3):
-            stack[0, p, 0:ROWS] = lo[4 + p - 1]
-            stack[0, p, mid] = lo[p]
-            stack[0, p, end] = lo[4 + p].T
-            stack[1, p, mid] = hi[4 - p]
-            stack[1, p, end] = hi[4 + 3 - p].T
-        stack[0, 4, 0:ROWS] = lo[7]
-        for p in (1, 2):
-            stack[1, p, 0:ROWS] = hi[4 + 2 - p]
+            stack[p, ONE] = chip[3 + p]
+            stack[p, TWO] = chip[p]
+            stack[p, THREE] = chip[4 + p].T
+        for i in range(4):
+            stack[4 + i, ONE] = chip[7] if i == 0 else link[i - 1]
+            stack[4 + i, TWO] = diag[i]
+            stack[4 + i, THREE] = link[i].T
+
+    @pl.when(info[0] != 0)
+    def _():
+        last = link[TILES - 1]
+        last = jnp.where(info[1] > 0, last, jnp.zeros_like(last))
+        for i in range(4):
+            rhs[i] = chip[0, rows(3 - i), :]
+        for p in (1, 2, 3):
+            stack[p, ONE] = chip[7 - p].T
+            stack[p, TWO] = chip[4 - p]
+            stack[p, THREE] = last if p == 3 else chip[6 - p]
+        for i in range(4):
+            stack[4 + i, ONE] = link[31 - i].T
+            stack[4 + i, TWO] = diag[31 - i]
+            stack[4 + i, THREE] = link[30 - i]
+
+    c = info[0]
+    res, dirs, rel = {}, {}, {}
+    for p in range(8):
+        if p < 4:
+            res[p] = rhs[p].astype(F32)
+            dirs[p] = res[p] * 0.5
+        else:
+            res[p] = state[0, 4 * c + (p - 4)]
+            dirs[p] = state[1, 4 * c + (p - 4)]
+            rel[p] = state[2, 4 * c + (p - 4)]
+    for k in range(1, STEPS + 1):
+        bf = {p: dirs[p].astype(BF16) for p in range(k - 1, k + 4)}
+        bf[k + 4] = near[4 * c + (k - 1)]
+        sweep(k, range(k, k + 4), stack, res, dirs, rel, bf)
+    part[...] = total(res, range(4, 8))
+
+    @pl.when(c == 0)
+    def _():
+        for i in range(4):
+            edge[i] = rel[4 + i]
+
+    @pl.when(c != 0)
+    def _():
+        for i in range(4):
+            edge[3 - i] = rel[4 + i]
+
+
+def middle_kernel(info, core, diag, link, state, near, sums_in, part, edge, copies, stack, mid, ends):
+    def received(block, i):
+        return core[block, rows(i), :].astype(F32) + core[block + 1, rows(i), :].astype(F32)
 
     @pl.when(info[0] == 0)
     def _():
-        fill(chip, core)
+        for i in range(4):
+            stack[i, ONE] = link[27 + i]
+            stack[i, TWO] = diag[28 + i]
+            stack[i, THREE] = link[28 + i].T
+            stack[4 + i, ONE] = link[31] if i == 0 else core[3 + i]
+            stack[4 + i, TWO] = core[i]
+            stack[4 + i, THREE] = core[4 + i].T
+            for which in range(2):
+                mid[which, i] = state[which, 7 - i]
+                mid[which, 4 + i] = received(10 + 2 * which, i)
+            mid[2, i] = state[2, 7 - i]
+            mid[2, 4 + i] = jnp.zeros((VECS, ROWS), F32)
+            ends[0, i] = near[4 + i]
+            ends[1, i] = core[9, rows(i), :]
 
     @pl.when(info[0] != 0)
     def _():
-        fill(core, chip)
-
-    last = link[TILES - 1]
-    stack[1, 3, 0:ROWS] = jnp.where(info[1] > 0, last, jnp.zeros_like(last))
-    for p in range(4, 8):
-        if p > 4:
-            stack[0, p, 0:ROWS] = link[p - 5]
-        stack[0, p, mid] = diag[p - 4]
-        stack[0, p, end] = link[p - 4].T
-        stack[1, p, 0:ROWS] = link[34 - p]
-        stack[1, p, mid] = diag[35 - p]
-        stack[1, p, end] = link[35 - p].T
-
-    res, dirs, rel = [{}, {}], [{}, {}], [{}, {}]
-    for s in range(2):
-        for p in range(4):
-            r = rhs[s, p].astype(F32)
-            res[s][p] = r
-            dirs[s][p] = r * 0.5
-        for i in range(4):
-            res[s][4 + i] = state[0, 4 * s + i]
-            dirs[s][4 + i] = state[1, 4 * s + i]
-            rel[s][4 + i] = state[2, 4 * s + i]
+        for i in range(4):
+            stack[i, ONE] = core[4 + i]
+            stack[i, TWO] = core[i]
+            stack[i, THREE] = core[5 + i].T
+            stack[4 + i, ONE] = core[8] if i == 0 else link[i - 1]
+            stack[4 + i, TWO] = diag[i]
+            stack[4 + i, THREE] = link[i].T
+            for which in range(2):
+                mid[which, i] = received(10 + 2 * which, i)
+                mid[which, 4 + i] = state[which, i]
+            mid[2, i] = jnp.zeros((VECS, ROWS), F32)
+            mid[2, 4 + i] = state[2, i]
+            ends[0, i] = core[9, rows(i), :]
+            ends[1, i] = near[i]
+
+    c = info[0]
+    res, dirs, rel = ({p: mid[which, p] for p in range(8)} for which in range(3))
     for k in range(1, STEPS + 1):
-        bf = [{p: dirs[s][p].astype(BF16) for p in range(k - 1, k + 4)} for s in range(2)]
-        for s in range(2):
-            bf[s][k + 4] = near[4 * s + k - 1]
-        for p in range(k, k + 4):
-            for s in range(2):
-                order = (p - 1, p, p + 1) if s == 0 else (p + 1, p, p - 1)
-                v = jnp.concatenate([bf[s][q] for q in order], axis=1)
-                r = res[s][p] - times(v, stack[s, p])
-                res[s][p] = r
-                if k < STEPS:
-                    c0, c1 = COEFS[k - 1]
-                    dirs[s][p] = c0 * dirs[s][p] + c1 * r
-                    if p >= 4:
-                        rel[s][p] = rel[s][p] + dirs[s][p]
-    totals = []
-    for s in range(2):
-        total = sums_in[s]
-        for i in range(4):
-            total = total + res[s][4 + i].astype(BF16).astype(F32)
-            edge[4 * s + (i if s == 0 else 3 - i)] = rel[s][4 + i]
-        totals.append(total)
-    own = info[0] == 0
-    keep[...] = jnp.where(own, totals[0], totals[1])
-    give[...] = jnp.where(own, totals[1], totals[0]).astype(BF16)
-
-
-def place_kernel(edge, inner, rel, sems):
-    parts = ((edge.at[0:4], rel.at[0:4]), (inner.at[4:28], rel.at[4:28]), (edge.at[4:8], rel.at[28:32]))
+        span = range(4 - k, 4 + k)
+        bf = {p: dirs[p].astype(BF16) for p in span}
+        bf[3 - k] = ends[0, k - 1]
+        bf[4 + k] = ends[1, k - 1]
+        sweep(k, span, stack, res, dirs, rel, bf)
+    beside = jnp.where(c == 0, total(res, range(4, 8)), total(res, range(4)))
+    other = core[14, rows(0), :].astype(F32) + core[14, rows(1), :].astype(F32)
+    whole = ((sums_in[c] + other) + (part[...] + beside)).astype(BF16)
+    for i in range(copies.shape[0]):
+        copies[i] = whole
+
+    @pl.when(c == 0)
+    def _():
+        for i in range(4):
+            edge[i] = rel[i]
+
+    @pl.when(c != 0)
+    def _():
+        for i in range(4):
+            edge[i] = rel[4 + i]
+
+
+def place_kernel(info, outer, middle, inner, rel, sems):
+    c = info[0]
+    parts = (
+        (outer, rel.at[pl.ds(28 * c, 4)]),
+        (inner.at[4:28], rel.at[4:28]),
+        (middle, rel.at[pl.ds(28 - 28 * c, 4)]),
+    )
     copies = [pltpu.make_async_copy(a, b, sems.at[i]) for i, (a, b) in enumerate(parts)]
-    for c in copies:
-        c.start()
-    for c in copies:
-        c.wait()
-
-
-def spread_kernel(count, a, b, out):
-    s = (a[...] + b[...].astype(F32)).astype(BF16)
-    for i in range(count):
-        out[i] = s
+    for copy in copies:
+        copy.start()
+    for copy in copies:
+        copy.wait()
 
 
 def sum_of(ref):
@@ -234,11 +321,6 @@
 
 def total_kernel(got, out):
     out[...] = sum_of(got)
-
-
-def halves(a):
-    top = a.astype(BF16)
-    return top, (a - top.astype(F32)).astype(BF16)
 
 
 def map_kernel(restrict, level, inverse, top, rest):
@@ -275,27 +357,33 @@
     j = lax.axis_index("x") * 2 + half
     info = jnp.stack([half, (j < 7).astype(jnp.int32)]).astype(jnp.int32)
 
-    to_chip, to_core = call(
+    to_chip = call(
         pack_kernel,
-        (bf16(pack), bf16(pack)),
+        bf16(pack),
         [SMEM] + [HBM] * 3,
-        (VMEM, VMEM),
+        VMEM,
         (info, rhs.reshape(8, ROWS, ROWS), diag, link),
-        scratch=[pltpu.SemaphoreType.DMA((6,))],
-        mib=53.25,
-        cost=(0, 1 << 20),
+        scratch=[pltpu.SemaphoreType.DMA((3,))],
+        mib=53.5,
+        cost=(0, 1 << 19),
     )
     across = [(1, 2), (2, 1), (3, 4), (4, 3), (5, 6), (6, 5)]
     swap = [(0, 1), (1, 0)]
+    to_chip, later = lax.optimization_barrier((to_chip, info))
     chip = lax.ppermute(to_chip, ("x", "core"), across)
-    core = lax.ppermute(to_core, "core", swap)
-
-    rel, state, near, sums = call(
+
+    rel, state, near, sums, pass_on = call(
         inner_kernel,
-        (f32((TILES,) + tile), f32((3, 8) + tile), bf16((8,) + tile), f32((2,) + tile)),
-        [VMEM] * 3,
-        (VMEM,) * 4,
-        (rhs, diag, link),
+        (
+            f32((TILES,) + tile),
+            f32((3, 8) + tile),
+            bf16((8,) + tile),
+            f32((2,) + tile),
+            bf16((15, ROWS, ROWS)),
+        ),
+        [SMEM] + [VMEM] * 3,
+        (VMEM,) * 5,
+        (later, rhs, diag, link),
         scratch=[
             pltpu.VMEM((TILES,) + tile, F32),
             pltpu.VMEM((TILES,) + tile, F32),
@@ -305,24 +393,34 @@
         mib=24,
         cost=(4 * 10**8, 3 << 20),
     )
-    edge, keep, give = call(
-        edge_kernel,
-        (f32((8,) + tile), f32(tile), bf16(tile)),
+    core = lax.ppermute(pass_on, "core", swap)
+    outer, part = call(
+        outer_kernel,
+        (f32((4,) + tile), f32(tile)),
+        [SMEM] + [VMEM] * 5,
+        (VMEM,) * 2,
+        (info, chip, diag, link, state, near),
+        scratch=[pltpu.VMEM((8, 3 * ROWS, ROWS), BF16), pltpu.VMEM((4,) + tile, BF16)],
+        mib=16,
+        cost=(5 * 10**9, 1 << 20),
+    )
+    middle, copies = call(
+        middle_kernel,
+        (f32((4,) + tile), bf16((32,) + tile)),
         [SMEM] + [VMEM] * 7,
-        (VMEM,) * 3,
-        (info, chip, core, diag, link, state, near, sums),
-        scratch=[pltpu.VMEM((2, 8, 3 * ROWS, ROWS), BF16), pltpu.VMEM((2, 4) + tile, BF16)],
+        (VMEM,) * 2,
+        (info, core, diag, link, state, near, sums, part),
+        scratch=[
+            pltpu.VMEM((8, 3 * ROWS, ROWS), BF16),
+            pltpu.VMEM((3, 8) + tile, F32),
+            pltpu.VMEM((2, 4) + tile, BF16),
+        ],
         mib=16,
         cost=(10**8, 1 << 20),
     )
-
-    got = lax.ppermute(give, "core", swap)
-    copies = call(
-        functools.partial(spread_kernel, 32), bf16((32,) + tile), [VMEM] * 2, VMEM, (keep, got), cost=(0, 1 << 18)
-    )
     copies = lax.all_to_all(copies, ("y", "x"), 0, 0, tiled=True)
     copies = call(functools.partial(merge_kernel, 16), bf16((16,) + tile), [VMEM], VMEM, (copies,), cost=(0, 1 << 18))
-    copies, restrict_map, edge = lax.optimization_barrier((copies, restrict_map, edge))
+    copies, restrict_map, outer = lax.optimization_barrier((copies, restrict_map, outer))
     copies = lax.all_to_all(copies, "z", 0, 0, tiled=True)
     top, rest = call(
         map_kernel,
@@ -335,9 +433,9 @@
     rel = call(
         place_kernel,
         f32((TILES,) + tile),
-        [VMEM, VMEM],
+        [SMEM] + [VMEM] * 3,
         HBM,
-        (edge, rel),
+        (info, outer, middle, rel),
         scratch=[pltpu.SemaphoreType.DMA((3,))],
         cost=(0, 1 << 20),
     )

time: 76.8 us -> 75.4 us (0.982)
  Pallas kernels: 11.4 us -> 13.5 us
  starting transfers between devices: 38.9 us -> 37.3 us
  waiting for transfers between devices: 9.85 us -> 8.59 us
    pallas_call x10, Pallas kernels: 11.4 us -> 13.5 us  [call(): pl.pallas_call(kernel, out_shape=out_shape, in_specs=in_specs, out_specs=...]
    ppermute x2 -> x1, starting transfers between devices: 14.2 us -> 12.2 us  [shards(): core = lax.ppermute(pass_on, 'core', swap)]
    ppermute x2 -> x1, waiting for transfers between devices: 1.14 us -> 0.11 us  [shards(): core = lax.ppermute(pass_on, 'core', swap)]
  transfers between devices with their start and end apart: 5 -> 4, of which waited for: 3 -> 3; matrix products, arithmetic and copies ran while one was open for 0% -> 0% of each run, Pallas kernels for 8% -> 11%
where the time goes in v3:
time: 75.4 us; the launch traced here: 75.1 us
  starting transfers between devices  37.3 us (49%)
  blocking collectives  14.8 us (20%)
  Pallas kernels  13.5 us (18%)
  waiting for transfers between devices  8.59 us (11%)
  between operations  0.81 us (1%)
    all_to_all x1, blocking collectives, shards(): copies = lax.all_to_all(copies, ('y', 'x'), 0, 0, tiled=True)  14.8 us
    all_to_all x1, starting transfers between devices, shards(): copies = lax.all_to_all(copies, 'z', 0, 0, tiled=True)  14.8 us
    pallas_call x10, Pallas kernels, call(): pl.pallas_call(kernel, out_shape=out_shape, in_specs=in_specs, out_specs=...  13.5 us
    ppermute x1, starting transfers between devices, shards(): core = lax.ppermute(pass_on, 'core', swap)  12.2 us
    all_to_all x1, waiting for transfers between devices, shards(): copies = lax.all_to_all(copies, 'z', 0, 0, tiled=True)  8.35 us
    ppermute x1, starting transfers between devices, shards(): other = lax.ppermute(mine, 'core', swap)  5.7 us
    ppermute x1, starting transfers between devices, shards(): chip = lax.ppermute(to_chip, ('x', 'core'), across)  4.51 us
  transfers between devices with their start and end apart: 4, of which 3 were waited for; matrix products, arithmetic and copies ran while one was open for 0% of the time, Pallas kernels for 11%

profile of v3, /device:TPU:1, one launch (start us, length us, event | category | flops | bytes accessed | tf_op | source)
XLA Modules:
  0.0 75.1 jit_solution(14377065218378874503)
XLA Ops:
  0.6 0.1 pad_add_fusion.info
  0.7 0.0 copy-start
  0.7 0.0 copy-start.1
  0.7 0.0 copy-start.2
  0.7 1.7 %shard_map.77 = bf16[8,128,128]{2,1,0:T(8,128)(2,1)S(1)} custom-call(s32[2]{0:T(128)S(1)} %pad_add_fusion.info, bf16[8,128,128]{2,1,0:T(8,128)(2,1)} %bitcast.16, bf16[32,128,128]{2,1,0:T(8,128)(2,1)} %bitcast.8, bf16[32,128,128]{2,1,0:T(8,128)(2,1)} %bitcast.12), custom_call_target="tpu_custom_call" | custom-call | bytes 524288 | tf_op jit(solution)/shard_map/pallas_call | solution.py:40
  2.4 4.5 %collective-permute-start.1 = (bf16[8,128,128]{2,1,0:T(8,128)(2,1)S(1)}, bf16[8,128,128]{2,1,0:T(8,128)(2,1)S(1)}, u32[]{:S(2)}, u32[]{:S(2)}) collective-permute-start(bf16[8,128,128]{2,1,0:T(8,128)(2,1)S(1)} %shard_map.77), channel_id=1, source_target_pairs={{1,2},{2,1},{3,4},{4,3},{5,6},{6,5},{9,10},{10,9},{11,12},{12,11},... | collective-permute-start | bytes 786440 | tf_op jit(solution)/shard_map/ppermute | solution.py:373
  6.9 0.0 copy-done
  7.0 0.0 copy-done.1
  7.0 0.0 copy-done.2
  7.0 2.9 %shard_map.78 = (f32[32,32,128]{2,1,0:T(8,128)S(1)}, f32[3,8,32,128]{3,2,1,0:T(8,128)S(1)}, bf16[8,32,128]{2,1,0:T(8,128)(2,1)S(1)}, f32[2,32,128]{2,1,0:T(8,128)S(1)}, bf16[15,128,128]{2,1,0:T(8,128)(2,1)S(1)}) custom-call(s32[2]{0:T(128)S(1)} %pad_add_fusion.info, bf16[32,32,128]{2,1,0:T(8,128)(2,1)S(1)} %bitcast.17, bf16[32,128,128]{2,1,0:T(8,128)(2,1)S(1)} %bitcast.9, ...), custom_call_target="tpu_custom_call" | custom-call | flops 400000000 | bytes 3145728 | tf_op jit(solution)/shard_map/pallas_call | solution.py:40
  9.8 12.2 %collective-permute-start = (bf16[15,128,128]{2,1,0:T(8,128)(2,1)S(1)}, bf16[15,128,128]{2,1,0:T(8,128)(2,1)S(1)}, u32[]{:S(2)}, u32[]{:S(2)}) collective-permute-start(bf16[15,128,128]{2,1,0:T(8,128)(2,1)S(1)} %get-tuple-element.23), channel_id=1, source_target_pairs={{0,1},{1,0},{2,3},{3,2},{4,5},{5,4},{6,7},{7,6},{8,9},{9,8},{10,11... | collective-permute-start | bytes 1474568 | tf_op jit(solution)/shard_map/ppermute | solution.py:396
  22.1 0.0 collective-permute-done.1.chip
  22.1 1.3 %shard_map.79 = (f32[4,32,128]{2,1,0:T(8,128)S(1)}, f32[32,128]{1,0:T(8,128)S(1)}) custom-call(s32[2]{0:T(128)S(1)} %pad_add_fusion.info, bf16[8,128,128]{2,1,0:T(8,128)(2,1)S(1)} %collective-permute-done.1.chip, bf16[32,128,128]{2,1,0:T(8,128)(2,1)S(1)} %bitcast.10, bf16[32,128,128]{2,1,0:T(8,128)(2,1)S(1)} %bitcast.14, ...), custom_call_target="tpu_custom_call" | custom-call | flops 5000000000 | bytes 1048576 | tf_op jit(solution)/shard_map/pallas_call | solution.py:40
  23.4 0.1 collective-permute-done.core
  23.5 1.3 %shard_map.80 = (f32[4,32,128]{2,1,0:T(8,128)S(1)}, bf16[32,32,128]{2,1,0:T(8,128)(2,1)S(1)}) custom-call(s32[2]{0:T(128)S(1)} %pad_add_fusion.info, bf16[15,128,128]{2,1,0:T(8,128)(2,1)S(1)} %collective-permute-done.core, bf16[32,128,128]{2,1,0:T(8,128)(2,1)S(1)} %bitcast.11, bf16[32,128,128]{2,1,0:T(8,128)(2,1)S(1)} %bitcast.15, ...), custom_call_target="tpu_custom_call" | custom-call | flops 100000000 | bytes 1048576 | tf_op jit(solution)/shard_map/pallas_call | solution.py:40
  24.9 14.8 %all_to_all.10.got = bf16[32,32,128]{2,1,0:T(8,128)(2,1)S(1)} all-to-all(bf16[32,32,128]{2,1,0:T(8,128)(2,1)S(1)} %get-tuple-element.29), channel_id=1, replica_groups=mesh['y'=8,'z'=16,'x'=4,'core'=2] {'y','x'}, dimensions={0} | all-to-all | bytes 524288 | tf_op jit(solution)/shard_map/all_to_all | solution.py:421
  39.7 0.7 shard_map.81
  40.4 14.8 %all-to-all-start.1 = ((bf16[16,32,128]{2,1,0:T(8,128)(2,1)}), bf16[16,32,128]{2,1,0:T(8,128)(2,1)S(1)}, u32[]{:S(2)}, u32[]{:S(2)}) async-start(bf16[16,32,128]{2,1,0:T(8,128)(2,1)} %shard_map.81), calls=%async_computation.1 | async-start | bytes 262144 | tf_op jit(solution)/shard_map/all_to_all | solution.py:424
  55.2 0.0 copy-start.3
  55.2 0.0 copy-start.4
  55.3 0.0 copy-start.5
  55.3 1.4 %shard_map.84 = f32[32,32,128]{2,1,0:T(8,128)} custom-call(s32[2]{0:T(128)S(1)} %pad_add_fusion.info, f32[4,32,128]{2,1,0:T(8,128)S(1)} %get-tuple-element.35.outer, f32[4,32,128]{2,1,0:T(8,128)S(1)} %get-tuple-element.36.middle, f32[32,32,128]{2,1,0:T(8,128)S(1)} %get-tuple-element.37.inner), custom_call_target="tpu_custom_call" | custom-call | bytes 1048576 | tf_op jit(solution)/shard_map/pallas_call | solution.py:40
  56.6 0.0 copy-done.3
  56.6 0.0 copy-done.4
  56.6 0.0 copy-done.5
  56.7 2.2 %shard_map.83 = (bf16[2,128,256]{2,1,0:T(8,128)(2,1)S(1)}, bf16[2,128,256]{2,1,0:T(8,128)(2,1)S(1)}) custom-call(bf16[128,128]{1,0:T(8,128)(2,1)S(1)} %copy-done.5, f32[2,128,128]{2,1,0:T(8,128)S(1)} %copy-done.4, f32[256,256]{1,0:T(8,128)S(1)} %copy-done.3), custom_call_target="tpu_custom_call" | custom-call | flops 400000000 | bytes 524288 | tf_op jit(solution)/shard_map/pallas_call | solution.py:40
  58.9 8.3 %all-to-all-done.1.got = bf16[16,32,128]{2,1,0:T(8,128)(2,1)S(1)} async-done(((bf16[16,32,128]{2,1,0:T(8,128)(2,1)}), bf16[16,32,128]{2,1,0:T(8,128)(2,1)S(1)}, u32[]{:S(2)}, u32[]{:S(2)}) %all-to-all-start.1) | async-done | bytes 131104 | tf_op jit(solution)/shard_map/all_to_all | solution.py:424
  67.3 5.7 %collective-permute-start.2 = (f32[32,128]{1,0:T(8,128)S(1)}, f32[32,128]{1,0:T(8,128)S(1)}, u32[]{:S(2)}, u32[]{:S(2)}) collective-permute-start(f32[32,128]{1,0:T(8,128)S(1)} %shard_map.82.mine), channel_id=1, source_target_pairs={{0,1},{1,0},{2,3},{3,2},{4,5},{5,4},{6,7},{7,6},{8,9},{9,8},{10,11... | collective-permute-start | bytes 49160 | tf_op jit(solution)/shard_map/ppermute | solution.py:444
  73.0 0.7 shard_map.85.part
  73.7 0.1 collective-permute-done.2.other
  73.8 1.3 %shard_map.86 = f32[32,256]{1,0:T(8,128)} custom-call(s32[2]{0:T(128)S(1)} %pad_add_fusion.info, f32[32,256]{1,0:T(8,128)S(1)} %shard_map.85.part, f32[32,128]{1,0:T(8,128)S(1)} %collective-permute-done.2.other, bf16[2,128,256]{2,1,0:T(8,128)(2,1)S(1)} %get-tuple-element.40.top, bf16[2,128,256]{2,1,0:T(8,128)(2,1)S(1)} %get-tuple-element.41.rest), custom_call_target="tpu_custom_call" | custom-call | flops 10000000 | bytes 131072 | tf_op jit(solution)/shard_map/pallas_call | solution.py:40
  (1 shorter events, 0.0 us)
Async XLA Ops:
  0.7 6.2 %copy-start = (bf16[1,32,128,128]{3,2,1,0:T(8,128)(2,1)S(1)}, bf16[1,32,128,128]{3,2,1,0:T(8,128)(2,1)}, u32[]{:S(2)}) copy-start(bf16[1,32,128,128]{3,2,1,0:T(8,128)(2,1)} %param.7) | copy-start | bytes 3145732
  0.7 6.2 %copy-start.1 = (bf16[1,32,128,128]{3,2,1,0:T(8,128)(2,1)S(1)}, bf16[1,32,128,128]{3,2,1,0:T(8,128)(2,1)}, u32[]{:S(2)}) copy-start(bf16[1,32,128,128]{3,2,1,0:T(8,128)(2,1)} %param.8) | copy-start | bytes 3145732
  0.7 6.2 %copy-start.2 = (bf16[1,32,32,128]{3,2,1,0:T(8,128)(2,1)S(1)}, bf16[1,32,32,128]{3,2,1,0:T(8,128)(2,1)}, u32[]{:S(2)}) copy-start(bf16[1,32,32,128]{3,2,1,0:T(8,128)(2,1)} %param.6) | copy-start | bytes 786436
  2.4 19.6 %collective-permute-start.1 = (bf16[8,128,128]{2,1,0:T(8,128)(2,1)S(1)}, bf16[8,128,128]{2,1,0:T(8,128)(2,1)S(1)}, u32[]{:S(2)}, u32[]{:S(2)}) collective-permute-start(bf16[8,128,128]{2,1,0:T(8,128)(2,1)S(1)} %shard_map.77), channel_id=1, source_target_pairs={{1,2},{2,1},{3,4},{4,3},{5,6},{6,5},{9,10},{10,9},{11,12},{12,11},... | collective-permute-start | bytes 786440 | tf_op jit(solution)/shard_map/ppermute | solution.py:373
  9.8 13.7 %collective-permute-start = (bf16[15,128,128]{2,1,0:T(8,128)(2,1)S(1)}, bf16[15,128,128]{2,1,0:T(8,128)(2,1)S(1)}, u32[]{:S(2)}, u32[]{:S(2)}) collective-permute-start(bf16[15,128,128]{2,1,0:T(8,128)(2,1)S(1)} %get-tuple-element.23), channel_id=1, source_target_pairs={{0,1},{1,0},{2,3},{3,2},{4,5},{5,4},{6,7},{7,6},{8,9},{9,8},{10,11... | collective-permute-start | bytes 1474568 | tf_op jit(solution)/shard_map/ppermute | solution.py:396
  40.4 26.8 %all-to-all-start.1 = ((bf16[16,32,128]{2,1,0:T(8,128)(2,1)}), bf16[16,32,128]{2,1,0:T(8,128)(2,1)S(1)}, u32[]{:S(2)}, u32[]{:S(2)}) async-start(bf16[16,32,128]{2,1,0:T(8,128)(2,1)} %shard_map.81), calls=%async_computation.1 | async-start | bytes 262144 | tf_op jit(solution)/shard_map/all_to_all | solution.py:424
  55.2 1.4 %copy-start.3 = (f32[256,256]{1,0:T(8,128)S(1)}, f32[256,256]{1,0:T(8,128)}, u32[]{:S(2)}) copy-start(f32[256,256]{1,0:T(8,128)} %inverse.1) | copy-start | bytes 786436
  55.2 1.4 %copy-start.4 = (f32[2,128,128]{2,1,0:T(8,128)S(1)}, f32[2,128,128]{2,1,0:T(8,128)}, u32[]{:S(2)}) copy-start(f32[2,128,128]{2,1,0:T(8,128)} %level.1) | copy-start | bytes 393220
  55.3 1.4 %copy-start.5 = (bf16[128,128]{1,0:T(8,128)(2,1)S(1)}, bf16[128,128]{1,0:T(8,128)(2,1)}, u32[]{:S(2)}) copy-start(bf16[128,128]{1,0:T(8,128)(2,1)} %restrict) | copy-start | bytes 98308
  67.3 6.5 %collective-permute-start.2 = (f32[32,128]{1,0:T(8,128)S(1)}, f32[32,128]{1,0:T(8,128)S(1)}, u32[]{:S(2)}, u32[]{:S(2)}) collective-permute-start(f32[32,128]{1,0:T(8,128)S(1)} %shard_map.82.mine), channel_id=1, source_target_pairs={{0,1},{1,0},{2,3},{3,2},{4,5},{5,4},{6,7},{7,6},{8,9},{9,8},{10,11... | collective-permute-start | bytes 49160 | tf_op jit(solution)/shard_map/ppermute | solution.py:444

commit v4 on v3

--- a/solution.py
+++ b/solution.py
@@ -30,7 +30,6 @@
 
 COEFS = coefficients()
 VMEM = pl.BlockSpec(memory_space=pltpu.VMEM)
-SMEM = pl.BlockSpec(memory_space=pltpu.SMEM)
 HBM = pl.BlockSpec(memory_space=pltpu.HBM)
 f32 = functools.partial(jax.ShapeDtypeStruct, dtype=F32)
 bf16 = functools.partial(jax.ShapeDtypeStruct, dtype=BF16)
@@ -49,6 +48,10 @@
     )(*args)
 
 
+def core_index():
+    return lax.axis_index("core")
+
+
 def times(a, b):
     return jnp.dot(a, b, preferred_element_type=F32)
 
@@ -57,8 +60,8 @@
     return jnp.dot(a, b, precision=lax.Precision.HIGHEST, preferred_element_type=F32)
 
 
-def pack_kernel(info, rhs, diag, link, out, sems):
-    c = info[0]
+def pack_kernel(rhs, diag, link, out, sems):
+    c = core_index()
     parts = (
         (rhs.at[pl.ds(7 * c, 1)], out.at[0:1]),
         (diag.at[pl.ds(29 * c, 3)], out.at[1:4]),
@@ -80,7 +83,7 @@
     return slice(i * VECS, (i + 1) * VECS)
 
 
-def inner_kernel(info, rhs, diag, link, rel, state, near, sums, pass_on, resid, direc, dirb, stack):
+def inner_kernel(rhs, diag, link, rel, state, near, sums, pass_on, resid, direc, dirb, stack):
     for t in range(1, TILES - 1):
         stack[t, 0:ROWS] = link[t - 1]
         stack[t, ROWS : 2 * ROWS] = diag[t]
@@ -144,11 +147,11 @@
             pass_on[14, rows(2 * i), :] = top
             pass_on[14, rows(2 * i + 1), :] = rest
 
-    @pl.when(info[0] == 0)
+    @pl.when(core_index() == 0)
     def _():
         fill(28, 27, 4, (7, 6, 5, 4), 1)
 
-    @pl.when(info[0] != 0)
+    @pl.when(core_index() != 0)
     def _():
         fill(0, 0, 0, (0, 1, 2, 3), 0)
 
@@ -173,8 +176,8 @@
 ONE, TWO, THREE = slice(0, ROWS), slice(ROWS, 2 * ROWS), slice(2 * ROWS, 3 * ROWS)
 
 
-def outer_kernel(info, chip, diag, link, state, near, edge, part, stack, rhs):
-    @pl.when(info[0] == 0)
+def outer_kernel(chip, diag, link, state, near, edge, part, stack, rhs):
+    @pl.when(core_index() == 0)
     def _():
         for i in range(4):
             rhs[i] = chip[0, rows(i), :]
@@ -187,10 +190,10 @@
             stack[4 + i, TWO] = diag[i]
             stack[4 + i, THREE] = link[i].T
 
-    @pl.when(info[0] != 0)
+    @pl.when(core_index() != 0)
     def _():
         last = link[TILES - 1]
-        last = jnp.where(info[1] > 0, last, jnp.zeros_like(last))
+        last = jnp.where(lax.axis_index("x") * 2 + core_index() < 7, last, jnp.zeros_like(last))
         for i in range(4):
             rhs[i] = chip[0, rows(3 - i), :]
         for p in (1, 2, 3):
@@ -202,7 +205,7 @@
             stack[4 + i, TWO] = diag[31 - i]
             stack[4 + i, THREE] = link[30 - i]
 
-    c = info[0]
+    c = core_index()
     res, dirs, rel = {}, {}, {}
     for p in range(8):
         if p < 4:
@@ -229,11 +232,11 @@
             edge[3 - i] = rel[4 + i]
 
 
-def middle_kernel(info, core, diag, link, state, near, sums_in, part, edge, copies, stack, mid, ends):
+def middle_kernel(core, diag, link, state, near, sums_in, part, edge, copies, stack, mid, ends):
     def received(block, i):
         return core[block, rows(i), :].astype(F32) + core[block + 1, rows(i), :].astype(F32)
 
-    @pl.when(info[0] == 0)
+    @pl.when(core_index() == 0)
     def _():
         for i in range(4):
             stack[i, ONE] = link[27 + i]
@@ -250,7 +253,7 @@
             ends[0, i] = near[4 + i]
             ends[1, i] = core[9, rows(i), :]
 
-    @pl.when(info[0] != 0)
+    @pl.when(core_index() != 0)
     def _():
         for i in range(4):
             stack[i, ONE] = core[4 + i]
@@ -267,7 +270,7 @@
             ends[0, i] = core[9, rows(i), :]
             ends[1, i] = near[i]
 
-    c = info[0]
+    c = core_index()
     res, dirs, rel = ({p: mid[which, p] for p in range(8)} for which in range(3))
     for k in range(1, STEPS + 1):
         span = range(4 - k, 4 + k)
@@ -292,8 +295,8 @@
             edge[i] = rel[4 + i]
 
 
-def place_kernel(info, outer, middle, inner, rel, sems):
-    c = info[0]
+def place_kernel(outer, middle, inner, rel, sems):
+    c = core_index()
     parts = (
         (outer, rel.at[pl.ds(28 * c, 4)]),
         (inner.at[4:28], rel.at[4:28]),
@@ -340,36 +343,32 @@
     return times(x_top, top) + (times(x_top, rest) + times(x_rest, top))
 
 
-def own_kernel(info, mine, top, rest, out):
-    c = info[0]
+def own_kernel(mine, top, rest, out):
+    c = core_index()
     out[...] = mapped(mine[...], top[c], rest[c])
 
 
-def solve_kernel(info, part, other, top, rest, out):
-    c = 1 - info[0]
+def solve_kernel(part, other, top, rest, out):
+    c = 1 - core_index()
     out[...] = part[...] + mapped(other[...], top[c], rest[c])
 
 
 def shards(right_side, diag_blocks, link_blocks, restrict_map, level_map, coarse_inverse):
     rhs, diag, link = right_side[0], diag_blocks[0], link_blocks[0]
     tile, pack = (VECS, ROWS), (8, ROWS, ROWS)
-    half = lax.axis_index("core")
-    j = lax.axis_index("x") * 2 + half
-    info = jnp.stack([half, (j < 7).astype(jnp.int32)]).astype(jnp.int32)
-
     to_chip = call(
         pack_kernel,
         bf16(pack),
-        [SMEM] + [HBM] * 3,
+        [HBM] * 3,
         VMEM,
-        (info, rhs.reshape(8, ROWS, ROWS), diag, link),
+        (rhs.reshape(8, ROWS, ROWS), diag, link),
         scratch=[pltpu.SemaphoreType.DMA((3,))],
         mib=53.5,
         cost=(0, 1 << 19),
     )
     across = [(1, 2), (2, 1), (3, 4), (4, 3), (5, 6), (6, 5)]
     swap = [(0, 1), (1, 0)]
-    to_chip, later = lax.optimization_barrier((to_chip, info))
+    to_chip, later = lax.optimization_barrier((to_chip, rhs))
     chip = lax.ppermute(to_chip, ("x", "core"), across)
 
     rel, state, near, sums, pass_on = call(
@@ -381,9 +380,9 @@
             f32((2,) + tile),
             bf16((15, ROWS, ROWS)),
         ),
-        [SMEM] + [VMEM] * 3,
+        [VMEM] * 3,
         (VMEM,) * 5,
-        (later, rhs, diag, link),
+        (later, diag, link),
         scratch=[
             pltpu.VMEM((TILES,) + tile, F32),
             pltpu.VMEM((TILES,) + tile, F32),
@@ -397,9 +396,9 @@
     outer, part = call(
         outer_kernel,
         (f32((4,) + tile), f32(tile)),
-        [SMEM] + [VMEM] * 5,
+        [VMEM] * 5,
         (VMEM,) * 2,
-        (info, chip, diag, link, state, near),
+        (chip, diag, link, state, near),
         scratch=[pltpu.VMEM((8, 3 * ROWS, ROWS), BF16), pltpu.VMEM((4,) + tile, BF16)],
         mib=16,
         cost=(5 * 10**9, 1 << 20),
@@ -407,9 +406,9 @@
     middle, copies = call(
         middle_kernel,
         (f32((4,) + tile), bf16((32,) + tile)),
-        [SMEM] + [VMEM] * 7,
+        [VMEM] * 7,
         (VMEM,) * 2,
-        (info, core, diag, link, state, near, sums, part),
+        (core, diag, link, state, near, sums, part),
         scratch=[
             pltpu.VMEM((8, 3 * ROWS, ROWS), BF16),
             pltpu.VMEM((3, 8) + tile, F32),
@@ -433,9 +432,9 @@
     rel = call(
         place_kernel,
         f32((TILES,) + tile),
-        [SMEM] + [VMEM] * 3,
+        [VMEM] * 3,
         HBM,
-        (info, outer, middle, rel),
+        (outer, middle, rel),
         scratch=[pltpu.SemaphoreType.DMA((3,))],
         cost=(0, 1 << 20),
     )
@@ -443,9 +442,9 @@
     mine, top, rest, rel = lax.optimization_barrier((mine, top, rest, rel))
     other = lax.ppermute(mine, "core", swap)
     wide = f32((VECS, 2 * ROWS))
-    part = call(own_kernel, wide, [SMEM] + [VMEM] * 3, VMEM, (info, mine, top, rest), cost=(10**7, 1 << 17))
+    part = call(own_kernel, wide, [VMEM] * 3, VMEM, (mine, top, rest), cost=(10**7, 1 << 17))
     solved = call(
-        solve_kernel, wide, [SMEM] + [VMEM] * 4, VMEM, (info, part, other, top, rest), cost=(10**7, 1 << 17)
+        solve_kernel, wide, [VMEM] * 4, VMEM, (part, other, top, rest), cost=(10**7, 1 << 17)
     )
     return (rel[None], solved[None, None])
 

time: 75.4 us -> 73.2 us (0.971)
  Pallas kernels: 13.5 us -> 9.69 us
  waiting for transfers between devices: 8.59 us -> 9.93 us
    pallas_call x10, Pallas kernels: 13.5 us -> 9.69 us  [call(): pl.pallas_call(kernel, out_shape=out_shape, in_specs=in_specs, out_specs=...]
  transfers between devices with their start and end apart: 4 -> 4, of which waited for: 3 -> 3; matrix products, arithmetic and copies ran while one was open for 0% -> 0% of each run, Pallas kernels for 11% -> 9%
where the time goes in v4:
time: 73.2 us; the launch traced here: 72.9 us
  starting transfers between devices  37.3 us (51%)
  blocking collectives  14.8 us (20%)
  waiting for transfers between devices  9.93 us (14%)
  Pallas kernels  9.69 us (13%)
  between operations  0.81 us (1%)
    all_to_all x1, starting transfers between devices, shards(): copies = lax.all_to_all(copies, 'z', 0, 0, tiled=True)  14.8 us
    all_to_all x1, blocking collectives, shards(): copies = lax.all_to_all(copies, ('y', 'x'), 0, 0, tiled=True)  14.8 us
    ppermute x1, starting transfers between devices, shards(): core = lax.ppermute(pass_on, 'core', swap)  12.2 us
    pallas_call x10, Pallas kernels, call(): pl.pallas_call(kernel, out_shape=out_shape, in_specs=in_specs, out_specs=...  9.69 us
    all_to_all x1, waiting for transfers between devices, shards(): copies = lax.all_to_all(copies, 'z', 0, 0, tiled=True)  8.6 us
    ppermute x1, starting transfers between devices, shards(): other = lax.ppermute(mine, 'core', swap)  5.7 us
    ppermute x1, starting transfers between devices, shards(): chip = lax.ppermute(to_chip, ('x', 'core'), across)  4.51 us
  transfers between devices with their start and end apart: 4, of which 3 were waited for; matrix products, arithmetic and copies ran while one was open for 0% of the time, Pallas kernels for 9%

profile of v4, /device:TPU:1, one launch (start us, length us, event | category | flops | bytes accessed | tf_op | source)
XLA Modules:
  0.0 72.9 jit_solution(4101222607677642354)
XLA Ops:
  0.6 0.0 copy-start
  0.6 0.0 copy-start.1
  0.6 0.0 copy-start.2
  0.7 1.2 %shard_map.77 = bf16[8,128,128]{2,1,0:T(8,128)(2,1)S(1)} custom-call(bf16[8,128,128]{2,1,0:T(8,128)(2,1)} %bitcast.14, bf16[32,128,128]{2,1,0:T(8,128)(2,1)} %bitcast.6, bf16[32,128,128]{2,1,0:T(8,128)(2,1)} %bitcast.10), custom_call_target="tpu_custom_call" | custom-call | bytes 524288 | tf_op jit(solution)/shard_map/pallas_call | solution.py:39
  1.8 4.5 %collective-permute-start.1 = (bf16[8,128,128]{2,1,0:T(8,128)(2,1)S(1)}, bf16[8,128,128]{2,1,0:T(8,128)(2,1)S(1)}, u32[]{:S(2)}, u32[]{:S(2)}) collective-permute-start(bf16[8,128,128]{2,1,0:T(8,128)(2,1)S(1)} %shard_map.77), channel_id=1, source_target_pairs={{1,2},{2,1},{3,4},{4,3},{5,6},{6,5},{9,10},{10,9},{11,12},{12,11},... | collective-permute-start | bytes 786440 | tf_op jit(solution)/shard_map/ppermute | solution.py:372
  6.3 0.0 copy-done
  6.3 0.0 copy-done.1
  6.4 0.0 copy-done.2
  6.4 2.3 %shard_map.78 = (f32[32,32,128]{2,1,0:T(8,128)S(1)}, f32[3,8,32,128]{3,2,1,0:T(8,128)S(1)}, bf16[8,32,128]{2,1,0:T(8,128)(2,1)S(1)}, f32[2,32,128]{2,1,0:T(8,128)S(1)}, bf16[15,128,128]{2,1,0:T(8,128)(2,1)S(1)}) custom-call(bf16[32,32,128]{2,1,0:T(8,128)(2,1)S(1)} %bitcast.15, bf16[32,128,128]{2,1,0:T(8,128)(2,1)S(1)} %bitcast.7, ...), custom_call_target="tpu_custom_call" | custom-call | flops 400000000 | bytes 3145728 | tf_op jit(solution)/shard_map/pallas_call | solution.py:39
  8.7 12.2 %collective-permute-start = (bf16[15,128,128]{2,1,0:T(8,128)(2,1)S(1)}, bf16[15,128,128]{2,1,0:T(8,128)(2,1)S(1)}, u32[]{:S(2)}, u32[]{:S(2)}) collective-permute-start(bf16[15,128,128]{2,1,0:T(8,128)(2,1)S(1)} %get-tuple-element.23), channel_id=1, source_target_pairs={{0,1},{1,0},{2,3},{3,2},{4,5},{5,4},{6,7},{7,6},{8,9},{9,8},{10,11... | collective-permute-start | bytes 1474568 | tf_op jit(solution)/shard_map/ppermute | solution.py:395
  20.9 0.0 collective-permute-done.1.chip
  20.9 0.8 %shard_map.79 = (f32[4,32,128]{2,1,0:T(8,128)S(1)}, f32[32,128]{1,0:T(8,128)S(1)}) custom-call(bf16[8,128,128]{2,1,0:T(8,128)(2,1)S(1)} %collective-permute-done.1.chip, bf16[32,128,128]{2,1,0:T(8,128)(2,1)S(1)} %bitcast.8, bf16[32,128,128]{2,1,0:T(8,128)(2,1)S(1)} %bitcast.12, f32[3,8,32,128]{3,2,1,0:T(8,128)S(1)} %get-tuple-element.24.state, ...), custom_call_target="tpu_custom_call" | custom-call | flops 5000000000 | bytes 1048576 | tf_op jit(solution)/shard_map/pallas_call | solution.py:39
  21.7 0.7 collective-permute-done.core
  22.4 0.8 %shard_map.80 = (f32[4,32,128]{2,1,0:T(8,128)S(1)}, bf16[32,32,128]{2,1,0:T(8,128)(2,1)S(1)}) custom-call(bf16[15,128,128]{2,1,0:T(8,128)(2,1)S(1)} %collective-permute-done.core, bf16[32,128,128]{2,1,0:T(8,128)(2,1)S(1)} %bitcast.9, bf16[32,128,128]{2,1,0:T(8,128)(2,1)S(1)} %bitcast.13, f32[3,8,32,128]{3,2,1,0:T(8,128)S(1)} %get-tuple-element.24.state, ...), custom_call_target="tpu_custom_call" | custom-call | flops 100000000 | bytes 1048576 | tf_op jit(solution)/shard_map/pallas_call | solution.py:39
  23.2 14.8 %all_to_all.10.got = bf16[32,32,128]{2,1,0:T(8,128)(2,1)S(1)} all-to-all(bf16[32,32,128]{2,1,0:T(8,128)(2,1)S(1)} %get-tuple-element.29), channel_id=1, replica_groups=mesh['y'=8,'z'=16,'x'=4,'core'=2] {'y','x'}, dimensions={0} | all-to-all | bytes 524288 | tf_op jit(solution)/shard_map/all_to_all | solution.py:420
  38.0 0.7 shard_map.81
  38.7 14.8 %all-to-all-start.1 = ((bf16[16,32,128]{2,1,0:T(8,128)(2,1)}), bf16[16,32,128]{2,1,0:T(8,128)(2,1)S(1)}, u32[]{:S(2)}, u32[]{:S(2)}) async-start(bf16[16,32,128]{2,1,0:T(8,128)(2,1)} %shard_map.81), calls=%async_computation.1 | async-start | bytes 262144 | tf_op jit(solution)/shard_map/all_to_all | solution.py:423
  53.5 0.0 copy-start.3
  53.5 0.0 copy-start.4
  53.5 0.0 copy-start.5
  53.6 0.8 %shard_map.84 = f32[32,32,128]{2,1,0:T(8,128)} custom-call(f32[4,32,128]{2,1,0:T(8,128)S(1)} %get-tuple-element.35.outer, f32[4,32,128]{2,1,0:T(8,128)S(1)} %get-tuple-element.36.middle, f32[32,32,128]{2,1,0:T(8,128)S(1)} %get-tuple-element.37.inner), custom_call_target="tpu_custom_call" | custom-call | bytes 1048576 | tf_op jit(solution)/shard_map/pallas_call | solution.py:39
  54.4 0.1 copy-done.3
  54.5 0.2 copy-done.4
  54.7 0.0 copy-done.5
  54.7 2.2 %shard_map.83 = (bf16[2,128,256]{2,1,0:T(8,128)(2,1)S(1)}, bf16[2,128,256]{2,1,0:T(8,128)(2,1)S(1)}) custom-call(bf16[128,128]{1,0:T(8,128)(2,1)S(1)} %copy-done.5, f32[2,128,128]{2,1,0:T(8,128)S(1)} %copy-done.4, f32[256,256]{1,0:T(8,128)S(1)} %copy-done.3), custom_call_target="tpu_custom_call" | custom-call | flops 400000000 | bytes 524288 | tf_op jit(solution)/shard_map/pallas_call | solution.py:39
  56.9 8.6 %all-to-all-done.1.got = bf16[16,32,128]{2,1,0:T(8,128)(2,1)S(1)} async-done(((bf16[16,32,128]{2,1,0:T(8,128)(2,1)}), bf16[16,32,128]{2,1,0:T(8,128)(2,1)S(1)}, u32[]{:S(2)}, u32[]{:S(2)}) %all-to-all-start.1) | async-done | bytes 131104 | tf_op jit(solution)/shard_map/all_to_all | solution.py:423
  65.5 5.7 %collective-permute-start.2 = (f32[32,128]{1,0:T(8,128)S(1)}, f32[32,128]{1,0:T(8,128)S(1)}, u32[]{:S(2)}, u32[]{:S(2)}) collective-permute-start(f32[32,128]{1,0:T(8,128)S(1)} %shard_map.82.mine), channel_id=1, source_target_pairs={{0,1},{1,0},{2,3},{3,2},{4,5},{5,4},{6,7},{7,6},{8,9},{9,8},{10,11... | collective-permute-start | bytes 49160 | tf_op jit(solution)/shard_map/ppermute | solution.py:443
  71.3 0.1 shard_map.85.part
  71.4 0.7 collective-permute-done.2.other
  72.1 0.8 %shard_map.86 = f32[32,256]{1,0:T(8,128)} custom-call(f32[32,256]{1,0:T(8,128)S(1)} %shard_map.85.part, f32[32,128]{1,0:T(8,128)S(1)} %collective-permute-done.2.other, bf16[2,128,256]{2,1,0:T(8,128)(2,1)S(1)} %get-tuple-element.40.top, bf16[2,128,256]{2,1,0:T(8,128)(2,1)S(1)} %get-tuple-element.41.rest), custom_call_target="tpu_custom_call" | custom-call | flops 10000000 | bytes 131072 | tf_op jit(solution)/shard_map/pallas_call | solution.py:39
  (1 shorter events, 0.0 us)
Async XLA Ops:
  0.6 5.7 %copy-start = (bf16[1,32,128,128]{3,2,1,0:T(8,128)(2,1)S(1)}, bf16[1,32,128,128]{3,2,1,0:T(8,128)(2,1)}, u32[]{:S(2)}) copy-start(bf16[1,32,128,128]{3,2,1,0:T(8,128)(2,1)} %param.7) | copy-start | bytes 3145732
  0.6 5.7 %copy-start.1 = (bf16[1,32,128,128]{3,2,1,0:T(8,128)(2,1)S(1)}, bf16[1,32,128,128]{3,2,1,0:T(8,128)(2,1)}, u32[]{:S(2)}) copy-start(bf16[1,32,128,128]{3,2,1,0:T(8,128)(2,1)} %param.8) | copy-start | bytes 3145732
  0.6 5.7 %copy-start.2 = (bf16[1,32,32,128]{3,2,1,0:T(8,128)(2,1)S(1)}, bf16[1,32,32,128]{3,2,1,0:T(8,128)(2,1)}, u32[]{:S(2)}) copy-start(bf16[1,32,32,128]{3,2,1,0:T(8,128)(2,1)} %param.6) | copy-start | bytes 786436
  1.8 19.1 %collective-permute-start.1 = (bf16[8,128,128]{2,1,0:T(8,128)(2,1)S(1)}, bf16[8,128,128]{2,1,0:T(8,128)(2,1)S(1)}, u32[]{:S(2)}, u32[]{:S(2)}) collective-permute-start(bf16[8,128,128]{2,1,0:T(8,128)(2,1)S(1)} %shard_map.77), channel_id=1, source_target_pairs={{1,2},{2,1},{3,4},{4,3},{5,6},{6,5},{9,10},{10,9},{11,12},{12,11},... | collective-permute-start | bytes 786440 | tf_op jit(solution)/shard_map/ppermute | solution.py:372
  8.7 13.7 %collective-permute-start = (bf16[15,128,128]{2,1,0:T(8,128)(2,1)S(1)}, bf16[15,128,128]{2,1,0:T(8,128)(2,1)S(1)}, u32[]{:S(2)}, u32[]{:S(2)}) collective-permute-start(bf16[15,128,128]{2,1,0:T(8,128)(2,1)S(1)} %get-tuple-element.23), channel_id=1, source_target_pairs={{0,1},{1,0},{2,3},{3,2},{4,5},{5,4},{6,7},{7,6},{8,9},{9,8},{10,11... | collective-permute-start | bytes 1474568 | tf_op jit(solution)/shard_map/ppermute | solution.py:395
  38.7 26.9 %all-to-all-start.1 = ((bf16[16,32,128]{2,1,0:T(8,128)(2,1)}), bf16[16,32,128]{2,1,0:T(8,128)(2,1)S(1)}, u32[]{:S(2)}, u32[]{:S(2)}) async-start(bf16[16,32,128]{2,1,0:T(8,128)(2,1)} %shard_map.81), calls=%async_computation.1 | async-start | bytes 262144 | tf_op jit(solution)/shard_map/all_to_all | solution.py:423
  53.5 1.0 %copy-start.3 = (f32[256,256]{1,0:T(8,128)S(1)}, f32[256,256]{1,0:T(8,128)}, u32[]{:S(2)}) copy-start(f32[256,256]{1,0:T(8,128)} %inverse.1) | copy-start | bytes 786436
  53.5 1.2 %copy-start.4 = (f32[2,128,128]{2,1,0:T(8,128)S(1)}, f32[2,128,128]{2,1,0:T(8,128)}, u32[]{:S(2)}) copy-start(f32[2,128,128]{2,1,0:T(8,128)} %level.1) | copy-start | bytes 393220
  53.5 1.2 %copy-start.5 = (bf16[128,128]{1,0:T(8,128)(2,1)S(1)}, bf16[128,128]{1,0:T(8,128)(2,1)}, u32[]{:S(2)}) copy-start(bf16[128,128]{1,0:T(8,128)(2,1)} %restrict) | copy-start | bytes 98308
  65.5 6.5 %collective-permute-start.2 = (f32[32,128]{1,0:T(8,128)S(1)}, f32[32,128]{1,0:T(8,128)S(1)}, u32[]{:S(2)}, u32[]{:S(2)}) collective-permute-start(f32[32,128]{1,0:T(8,128)S(1)} %shard_map.82.mine), channel_id=1, source_target_pairs={{0,1},{1,0},{2,3},{3,2},{4,5},{5,4},{6,7},{7,6},{8,9},{9,8},{10,11... | collective-permute-start | bytes 49160 | tf_op jit(solution)/shard_map/ppermute | solution.py:443

commit v5 on v4

--- a/solution.py
+++ b/solution.py
@@ -29,6 +29,8 @@
 
 
 COEFS = coefficients()
+PLANE = [(4 + y) % 8 * 4 + (2 + x) % 4 for y in range(8) for x in range(4)]
+COLUMN = [(12 + z) % 16 for z in range(16)]
 VMEM = pl.BlockSpec(memory_space=pltpu.VMEM)
 HBM = pl.BlockSpec(memory_space=pltpu.HBM)
 f32 = functools.partial(jax.ShapeDtypeStruct, dtype=F32)
@@ -417,10 +419,10 @@
         mib=16,
         cost=(10**8, 1 << 20),
     )
-    copies = lax.all_to_all(copies, ("y", "x"), 0, 0, tiled=True)
+    copies = lax.all_to_all(copies, ("y", "x"), 0, 0, axis_index_groups=[PLANE], tiled=True)
     copies = call(functools.partial(merge_kernel, 16), bf16((16,) + tile), [VMEM], VMEM, (copies,), cost=(0, 1 << 18))
     copies, restrict_map, outer = lax.optimization_barrier((copies, restrict_map, outer))
-    copies = lax.all_to_all(copies, "z", 0, 0, tiled=True)
+    copies = lax.all_to_all(copies, "z", 0, 0, axis_index_groups=[COLUMN], tiled=True)
     top, rest = call(
         map_kernel,
         (bf16((2, ROWS, 2 * ROWS)),) * 2,

time: 73.2 us -> 67.5 us (0.922)
  starting transfers between devices: 37.3 us -> 33 us
  waiting for transfers between devices: 9.93 us -> 7.7 us
  blocking collectives: 14.8 us -> 15.6 us
    all_to_all x1, starting transfers between devices: 14.8 us -> 11.8 us  [shards(): lax.all_to_all(copies, 'z', 0, 0, axis_index_groups=[COLUMN], tiled=True)]
    all_to_all x1, waiting for transfers between devices: 8.6 us -> 6.37 us  [shards(): lax.all_to_all(copies, 'z', 0, 0, axis_index_groups=[COLUMN], tiled=True)]
    ppermute x1, starting transfers between devices: 5.7 us -> 4.45 us  [shards(): other = lax.ppermute(mine, 'core', swap)]
    all_to_all x1, blocking collectives: 14.8 us -> 15.6 us  [shards(): lax.all_to_all(copies, ('y', 'x'), 0, 0, axis_index_groups=[PLANE], tiled...]
where the time goes in v5:
time: 67.5 us; the launch traced here: 67.1 us
  starting transfers between devices  33 us (49%)
  blocking collectives  15.6 us (23%)
  Pallas kernels  9.69 us (14%)
  waiting for transfers between devices  7.7 us (11%)
  between operations  0.8 us (1%)
    all_to_all x1, blocking collectives, shards(): lax.all_to_all(copies, ('y', 'x'), 0, 0, axis_index_groups=[PLANE], tiled...  15.6 us
    ppermute x1, starting transfers between devices, shards(): core = lax.ppermute(pass_on, 'core', swap)  12.2 us
    all_to_all x1, starting transfers between devices, shards(): lax.all_to_all(copies, 'z', 0, 0, axis_index_groups=[COLUMN], tiled=True)  11.8 us
    pallas_call x10, Pallas kernels, call(): pl.pallas_call(kernel, out_shape=out_shape, in_specs=in_specs, out_specs=...  9.69 us
    all_to_all x1, waiting for transfers between devices, shards(): lax.all_to_all(copies, 'z', 0, 0, axis_index_groups=[COLUMN], tiled=True)  6.37 us
    ppermute x1, starting transfers between devices, shards(): chip = lax.ppermute(to_chip, ('x', 'core'), across)  4.51 us
    ppermute x1, starting transfers between devices, shards(): other = lax.ppermute(mine, 'core', swap)  4.45 us
  transfers between devices with their start and end apart: 4, of which 3 were waited for; matrix products, arithmetic and copies ran while one was open for 0% of the time, Pallas kernels for 9%

profile of v5, /device:TPU:1, one launch (start us, length us, event | category | flops | bytes accessed | tf_op | source)
XLA Modules:
  0.0 67.1 jit_solution(14934482915719018462)
XLA Ops:
  0.6 0.0 copy-start
  0.6 0.0 copy-start.1
  0.6 0.0 copy-start.2
  0.7 1.2 %shard_map.77 = bf16[8,128,128]{2,1,0:T(8,128)(2,1)S(1)} custom-call(bf16[8,128,128]{2,1,0:T(8,128)(2,1)} %bitcast.14, bf16[32,128,128]{2,1,0:T(8,128)(2,1)} %bitcast.6, bf16[32,128,128]{2,1,0:T(8,128)(2,1)} %bitcast.10), custom_call_target="tpu_custom_call" | custom-call | bytes 524288 | tf_op jit(solution)/shard_map/pallas_call | solution.py:41
  1.8 4.5 %collective-permute-start.1 = (bf16[8,128,128]{2,1,0:T(8,128)(2,1)S(1)}, bf16[8,128,128]{2,1,0:T(8,128)(2,1)S(1)}, u32[]{:S(2)}, u32[]{:S(2)}) collective-permute-start(bf16[8,128,128]{2,1,0:T(8,128)(2,1)S(1)} %shard_map.77), channel_id=1, source_target_pairs={{1,2},{2,1},{3,4},{4,3},{5,6},{6,5},{9,10},{10,9},{11,12},{12,11},... | collective-permute-start | bytes 786440 | tf_op jit(solution)/shard_map/ppermute | solution.py:374
  6.3 0.0 copy-done
  6.3 0.0 copy-done.1
  6.4 0.0 copy-done.2
  6.4 2.3 %shard_map.78 = (f32[32,32,128]{2,1,0:T(8,128)S(1)}, f32[3,8,32,128]{3,2,1,0:T(8,128)S(1)}, bf16[8,32,128]{2,1,0:T(8,128)(2,1)S(1)}, f32[2,32,128]{2,1,0:T(8,128)S(1)}, bf16[15,128,128]{2,1,0:T(8,128)(2,1)S(1)}) custom-call(bf16[32,32,128]{2,1,0:T(8,128)(2,1)S(1)} %bitcast.15, bf16[32,128,128]{2,1,0:T(8,128)(2,1)S(1)} %bitcast.7, ...), custom_call_target="tpu_custom_call" | custom-call | flops 400000000 | bytes 3145728 | tf_op jit(solution)/shard_map/pallas_call | solution.py:41
  8.7 12.2 %collective-permute-start = (bf16[15,128,128]{2,1,0:T(8,128)(2,1)S(1)}, bf16[15,128,128]{2,1,0:T(8,128)(2,1)S(1)}, u32[]{:S(2)}, u32[]{:S(2)}) collective-permute-start(bf16[15,128,128]{2,1,0:T(8,128)(2,1)S(1)} %get-tuple-element.23), channel_id=1, source_target_pairs={{0,1},{1,0},{2,3},{3,2},{4,5},{5,4},{6,7},{7,6},{8,9},{9,8},{10,11... | collective-permute-start | bytes 1474568 | tf_op jit(solution)/shard_map/ppermute | solution.py:397
  20.9 0.0 collective-permute-done.1.chip
  20.9 0.8 %shard_map.79 = (f32[4,32,128]{2,1,0:T(8,128)S(1)}, f32[32,128]{1,0:T(8,128)S(1)}) custom-call(bf16[8,128,128]{2,1,0:T(8,128)(2,1)S(1)} %collective-permute-done.1.chip, bf16[32,128,128]{2,1,0:T(8,128)(2,1)S(1)} %bitcast.8, bf16[32,128,128]{2,1,0:T(8,128)(2,1)S(1)} %bitcast.12, f32[3,8,32,128]{3,2,1,0:T(8,128)S(1)} %get-tuple-element.24.state, ...), custom_call_target="tpu_custom_call" | custom-call | flops 5000000000 | bytes 1048576 | tf_op jit(solution)/shard_map/pallas_call | solution.py:41
  21.7 0.7 collective-permute-done.core
  22.4 0.8 %shard_map.80 = (f32[4,32,128]{2,1,0:T(8,128)S(1)}, bf16[32,32,128]{2,1,0:T(8,128)(2,1)S(1)}) custom-call(bf16[15,128,128]{2,1,0:T(8,128)(2,1)S(1)} %collective-permute-done.core, bf16[32,128,128]{2,1,0:T(8,128)(2,1)S(1)} %bitcast.9, bf16[32,128,128]{2,1,0:T(8,128)(2,1)S(1)} %bitcast.13, f32[3,8,32,128]{3,2,1,0:T(8,128)S(1)} %get-tuple-element.24.state, ...), custom_call_target="tpu_custom_call" | custom-call | flops 100000000 | bytes 1048576 | tf_op jit(solution)/shard_map/pallas_call | solution.py:41
  23.2 15.6 %all_to_all.10.got = bf16[32,32,128]{2,1,0:T(8,128)(2,1)S(1)} all-to-all(bf16[32,32,128]{2,1,0:T(8,128)(2,1)S(1)} %get-tuple-element.29), channel_id=1, replica_groups={{516,518,512,514,644,646,640,642,772,774,768,770,900,902,896,898,4,6,0,..., dimensions={0} | all-to-all | bytes 524288 | tf_op jit(solution)/shard_map/all_to_all | solution.py:422
  38.8 0.7 %shard_map.81 = bf16[16,32,128]{2,1,0:T(8,128)(2,1)} custom-call(bf16[32,32,128]{2,1,0:T(8,128)(2,1)S(1)} %all_to_all.10.got), custom_call_target="tpu_custom_call" | custom-call | bytes 262144 | tf_op jit(solution)/shard_map/pallas_call | solution.py:41
  39.5 11.8 %all-to-all-start.1 = ((bf16[16,32,128]{2,1,0:T(8,128)(2,1)}), bf16[16,32,128]{2,1,0:T(8,128)(2,1)S(1)}, u32[]{:S(2)}, u32[]{:S(2)}) async-start(bf16[16,32,128]{2,1,0:T(8,128)(2,1)} %shard_map.81), calls=%async_computation.1 | async-start | bytes 262144 | tf_op jit(solution)/shard_map/all_to_all | solution.py:425
  51.3 0.0 copy-start.3
  51.3 0.0 copy-start.4
  51.3 0.0 copy-start.5
  51.3 0.8 %shard_map.84 = f32[32,32,128]{2,1,0:T(8,128)} custom-call(f32[4,32,128]{2,1,0:T(8,128)S(1)} %get-tuple-element.35.outer, f32[4,32,128]{2,1,0:T(8,128)S(1)} %get-tuple-element.36.middle, f32[32,32,128]{2,1,0:T(8,128)S(1)} %get-tuple-element.37.inner), custom_call_target="tpu_custom_call" | custom-call | bytes 1048576 | tf_op jit(solution)/shard_map/pallas_call | solution.py:41
  52.1 0.1 copy-done.3
  52.3 0.2 copy-done.4
  52.5 0.0 copy-done.5
  52.5 2.2 %shard_map.83 = (bf16[2,128,256]{2,1,0:T(8,128)(2,1)S(1)}, bf16[2,128,256]{2,1,0:T(8,128)(2,1)S(1)}) custom-call(bf16[128,128]{1,0:T(8,128)(2,1)S(1)} %copy-done.5, f32[2,128,128]{2,1,0:T(8,128)S(1)} %copy-done.4, f32[256,256]{1,0:T(8,128)S(1)} %copy-done.3), custom_call_target="tpu_custom_call" | custom-call | flops 400000000 | bytes 524288 | tf_op jit(solution)/shard_map/pallas_call | solution.py:41
  54.7 6.4 %all-to-all-done.1.got = bf16[16,32,128]{2,1,0:T(8,128)(2,1)S(1)} async-done(((bf16[16,32,128]{2,1,0:T(8,128)(2,1)}), bf16[16,32,128]{2,1,0:T(8,128)(2,1)S(1)}, u32[]{:S(2)}, u32[]{:S(2)}) %all-to-all-start.1) | async-done | bytes 131104 | tf_op jit(solution)/shard_map/all_to_all | solution.py:425
  61.1 4.4 %collective-permute-start.2 = (f32[32,128]{1,0:T(8,128)S(1)}, f32[32,128]{1,0:T(8,128)S(1)}, u32[]{:S(2)}, u32[]{:S(2)}) collective-permute-start(f32[32,128]{1,0:T(8,128)S(1)} %shard_map.82.mine), channel_id=1, source_target_pairs={{0,1},{1,0},{2,3},{3,2},{4,5},{5,4},{6,7},{7,6},{8,9},{9,8},{10,11... | collective-permute-start | bytes 49160 | tf_op jit(solution)/shard_map/ppermute | solution.py:445
  65.5 0.1 shard_map.85.part
  65.7 0.7 %collective-permute-done.2.other = f32[32,128]{1,0:T(8,128)S(1)} collective-permute-done((f32[32,128]{1,0:T(8,128)S(1)}, f32[32,128]{1,0:T(8,128)S(1)}, u32[]{:S(2)}, u32[]{:S(2)}) %collective-permute-start.2) | collective-permute-done | bytes 16416 | tf_op jit(solution)/shard_map/ppermute | solution.py:445
  66.4 0.8 %shard_map.86 = f32[32,256]{1,0:T(8,128)} custom-call(f32[32,256]{1,0:T(8,128)S(1)} %shard_map.85.part, f32[32,128]{1,0:T(8,128)S(1)} %collective-permute-done.2.other, bf16[2,128,256]{2,1,0:T(8,128)(2,1)S(1)} %get-tuple-element.40.top, bf16[2,128,256]{2,1,0:T(8,128)(2,1)S(1)} %get-tuple-element.41.rest), custom_call_target="tpu_custom_call" | custom-call | flops 10000000 | bytes 131072 | tf_op jit(solution)/shard_map/pallas_call | solution.py:41
  (1 shorter events, 0.0 us)
Async XLA Ops:
  0.6 5.7 %copy-start = (bf16[1,32,128,128]{3,2,1,0:T(8,128)(2,1)S(1)}, bf16[1,32,128,128]{3,2,1,0:T(8,128)(2,1)}, u32[]{:S(2)}) copy-start(bf16[1,32,128,128]{3,2,1,0:T(8,128)(2,1)} %param.7) | copy-start | bytes 3145732
  0.6 5.7 %copy-start.1 = (bf16[1,32,128,128]{3,2,1,0:T(8,128)(2,1)S(1)}, bf16[1,32,128,128]{3,2,1,0:T(8,128)(2,1)}, u32[]{:S(2)}) copy-start(bf16[1,32,128,128]{3,2,1,0:T(8,128)(2,1)} %param.8) | copy-start | bytes 3145732
  0.6 5.7 %copy-start.2 = (bf16[1,32,32,128]{3,2,1,0:T(8,128)(2,1)S(1)}, bf16[1,32,32,128]{3,2,1,0:T(8,128)(2,1)}, u32[]{:S(2)}) copy-start(bf16[1,32,32,128]{3,2,1,0:T(8,128)(2,1)} %param.6) | copy-start | bytes 786436
  1.8 19.1 %collective-permute-start.1 = (bf16[8,128,128]{2,1,0:T(8,128)(2,1)S(1)}, bf16[8,128,128]{2,1,0:T(8,128)(2,1)S(1)}, u32[]{:S(2)}, u32[]{:S(2)}) collective-permute-start(bf16[8,128,128]{2,1,0:T(8,128)(2,1)S(1)} %shard_map.77), channel_id=1, source_target_pairs={{1,2},{2,1},{3,4},{4,3},{5,6},{6,5},{9,10},{10,9},{11,12},{12,11},... | collective-permute-start | bytes 786440 | tf_op jit(solution)/shard_map/ppermute | solution.py:374
  8.7 13.7 %collective-permute-start = (bf16[15,128,128]{2,1,0:T(8,128)(2,1)S(1)}, bf16[15,128,128]{2,1,0:T(8,128)(2,1)S(1)}, u32[]{:S(2)}, u32[]{:S(2)}) collective-permute-start(bf16[15,128,128]{2,1,0:T(8,128)(2,1)S(1)} %get-tuple-element.23), channel_id=1, source_target_pairs={{0,1},{1,0},{2,3},{3,2},{4,5},{5,4},{6,7},{7,6},{8,9},{9,8},{10,11... | collective-permute-start | bytes 1474568 | tf_op jit(solution)/shard_map/ppermute | solution.py:397
  39.5 21.6 %all-to-all-start.1 = ((bf16[16,32,128]{2,1,0:T(8,128)(2,1)}), bf16[16,32,128]{2,1,0:T(8,128)(2,1)S(1)}, u32[]{:S(2)}, u32[]{:S(2)}) async-start(bf16[16,32,128]{2,1,0:T(8,128)(2,1)} %shard_map.81), calls=%async_computation.1 | async-start | bytes 262144 | tf_op jit(solution)/shard_map/all_to_all | solution.py:425
  51.3 1.0 %copy-start.3 = (f32[256,256]{1,0:T(8,128)S(1)}, f32[256,256]{1,0:T(8,128)}, u32[]{:S(2)}) copy-start(f32[256,256]{1,0:T(8,128)} %inverse.1) | copy-start | bytes 786436
  51.3 1.2 %copy-start.4 = (f32[2,128,128]{2,1,0:T(8,128)S(1)}, f32[2,128,128]{2,1,0:T(8,128)}, u32[]{:S(2)}) copy-start(f32[2,128,128]{2,1,0:T(8,128)} %level.1) | copy-start | bytes 393220
  51.3 1.2 %copy-start.5 = (bf16[128,128]{1,0:T(8,128)(2,1)S(1)}, bf16[128,128]{1,0:T(8,128)(2,1)}, u32[]{:S(2)}) copy-start(bf16[128,128]{1,0:T(8,128)(2,1)} %restrict) | copy-start | bytes 98308
  61.1 5.3 %collective-permute-start.2 = (f32[32,128]{1,0:T(8,128)S(1)}, f32[32,128]{1,0:T(8,128)S(1)}, u32[]{:S(2)}, u32[]{:S(2)}) collective-permute-start(f32[32,128]{1,0:T(8,128)S(1)} %shard_map.82.mine), channel_id=1, source_target_pairs={{0,1},{1,0},{2,3},{3,2},{4,5},{5,4},{6,7},{7,6},{8,9},{9,8},{10,11... | collective-permute-start | bytes 49160 | tf_op jit(solution)/shard_map/ppermute | solution.py:445

commit v6 on v5

--- a/solution.py
+++ b/solution.py
@@ -12,6 +12,7 @@
 VECS = 32
 ROWS = 128
 STEPS = 4
+EARLY = 8
 HALF = TILES // 2
 BF16, F32 = jnp.bfloat16, jnp.float32
 
@@ -29,8 +30,8 @@
 
 
 COEFS = coefficients()
-PLANE = [(4 + y) % 8 * 4 + (2 + x) % 4 for y in range(8) for x in range(4)]
-COLUMN = [(12 + z) % 16 for z in range(16)]
+PLANE = [18] + [4 * y + x for y in (0, 1, 7, 2, 6, 3, 5, 4) for x in range(4) if (y, x) != (4, 2)]
+COLUMN = [12, 0, 1, 2, 3, 4, 5, 6, 7, 15, 14, 13, 11, 10, 9, 8]
 VMEM = pl.BlockSpec(memory_space=pltpu.VMEM)
 HBM = pl.BlockSpec(memory_space=pltpu.HBM)
 f32 = functools.partial(jax.ShapeDtypeStruct, dtype=F32)
@@ -178,7 +179,7 @@
 ONE, TWO, THREE = slice(0, ROWS), slice(ROWS, 2 * ROWS), slice(2 * ROWS, 3 * ROWS)
 
 
-def outer_kernel(chip, diag, link, state, near, edge, part, stack, rhs):
+def outer_kernel(chip, diag, link, state, near, restrict, level, inverse, edge, part, stack, rhs):
     @pl.when(core_index() == 0)
     def _():
         for i in range(4):
@@ -297,7 +298,7 @@
             edge[i] = rel[4 + i]
 
 
-def place_kernel(outer, middle, inner, rel, sems):
+def place_tiles(outer, middle, inner, rel, sems):
     c = core_index()
     parts = (
         (outer, rel.at[pl.ds(28 * c, 4)]),
@@ -328,7 +329,7 @@
     out[...] = sum_of(got)
 
 
-def map_kernel(restrict, level, inverse, top, rest):
+def make_maps(restrict, level, inverse, top, rest):
     r = restrict[...].astype(F32) * 2.0**-5
     for c in range(2):
         one = level[c]
@@ -338,6 +339,25 @@
         head = exact(r, two)
         tail = exact(eight, inverse[c * ROWS : (c + 1) * ROWS, :])
         top[c], rest[c] = halves(exact(head, tail))
+
+
+def aside_kernel(restrict, level, inverse, outer, middle, inner, top, rest, rel, sems):
+    @pl.when(lax.axis_index("z") < EARLY)
+    def _():
+        make_maps(restrict, level, inverse, top, rest)
+        place_tiles(outer, middle, inner, rel, sems)
+
+
+def late_kernel(restrict, level, inverse, outer, middle, inner, top_in, rest_in, rel_in, top, rest, rel, sems):
+    @pl.when(lax.axis_index("z") < EARLY)
+    def _():
+        top[...] = top_in[...]
+        rest[...] = rest_in[...]
+
+    @pl.when(lax.axis_index("z") >= EARLY)
+    def _():
+        make_maps(restrict, level, inverse, top, rest)
+        place_tiles(outer, middle, inner, rel, sems)
 
 
 def mapped(x, top, rest):
@@ -398,9 +418,9 @@
     outer, part = call(
         outer_kernel,
         (f32((4,) + tile), f32(tile)),
-        [VMEM] * 5,
+        [VMEM] * 8,
         (VMEM,) * 2,
-        (chip, diag, link, state, near),
+        (chip, diag, link, state, near, restrict_map, level_map, coarse_inverse),
         scratch=[pltpu.VMEM((8, 3 * ROWS, ROWS), BF16), pltpu.VMEM((4,) + tile, BF16)],
         mib=16,
         cost=(5 * 10**9, 1 << 20),
@@ -421,32 +441,39 @@
     )
     copies = lax.all_to_all(copies, ("y", "x"), 0, 0, axis_index_groups=[PLANE], tiled=True)
     copies = call(functools.partial(merge_kernel, 16), bf16((16,) + tile), [VMEM], VMEM, (copies,), cost=(0, 1 << 18))
-    copies, restrict_map, outer = lax.optimization_barrier((copies, restrict_map, outer))
+    wide, whole = bf16((2, ROWS, 2 * ROWS)), f32((TILES,) + tile)
+    sources = (restrict_map, level_map, coarse_inverse, outer, middle, rel)
+    copies, middle_later = lax.optimization_barrier((copies, middle))
+    sources = (restrict_map, level_map, coarse_inverse, outer, middle_later, rel)
+    top, rest, out = call(
+        aside_kernel,
+        (wide, wide, whole),
+        [VMEM] * 6,
+        (VMEM, VMEM, HBM),
+        sources,
+        scratch=[pltpu.SemaphoreType.DMA((3,))],
+        cost=(10**8, 1 << 20),
+    )
+    copies, top, rest, out = lax.optimization_barrier((copies, top, rest, out))
     copies = lax.all_to_all(copies, "z", 0, 0, axis_index_groups=[COLUMN], tiled=True)
-    top, rest = call(
-        map_kernel,
-        (bf16((2, ROWS, 2 * ROWS)),) * 2,
-        [VMEM] * 3,
-        (VMEM,) * 2,
-        (restrict_map, level_map, coarse_inverse),
-        cost=(4 * 10**8, 1 << 19),
-    )
-    rel = call(
-        place_kernel,
-        f32((TILES,) + tile),
-        [VMEM] * 3,
-        HBM,
-        (outer, middle, rel),
+    copies, late = lax.optimization_barrier((copies, sources))
+    top, rest, rel = call(
+        late_kernel,
+        (wide, wide, whole),
+        [VMEM] * 8 + [HBM],
+        (VMEM, VMEM, HBM),
+        late + (top, rest, out),
         scratch=[pltpu.SemaphoreType.DMA((3,))],
-        cost=(0, 1 << 20),
+        cost=(10**8, 1 << 20),
+        input_output_aliases={8: 2},
     )
     mine = call(total_kernel, f32(tile), [VMEM], VMEM, (copies,), cost=(0, 1 << 17))
     mine, top, rest, rel = lax.optimization_barrier((mine, top, rest, rel))
     other = lax.ppermute(mine, "core", swap)
-    wide = f32((VECS, 2 * ROWS))
-    part = call(own_kernel, wide, [VMEM] * 3, VMEM, (mine, top, rest), cost=(10**7, 1 << 17))
+    solution_shape = f32((VECS, 2 * ROWS))
+    part = call(own_kernel, solution_shape, [VMEM] * 3, VMEM, (mine, top, rest), cost=(10**7, 1 << 17))
     solved = call(
-        solve_kernel, wide, [VMEM] * 4, VMEM, (part, other, top, rest), cost=(10**7, 1 << 17)
+        solve_kernel, solution_shape, [VMEM] * 4, VMEM, (part, other, top, rest), cost=(10**7, 1 << 17)
     )
     return (rel[None], solved[None, None])
 

time: 67.5 us -> 66.9 us (level)
  blocking collectives: 15.6 us -> 35.3 us
  starting transfers between devices: 33 us -> 20.8 us
  waiting for transfers between devices: 7.7 us -> 1.3 us
  Pallas kernels: 9.69 us -> 8.38 us
    all_to_all x0 -> x1, blocking collectives: none -> 19.5 us  [shards(): lax.all_to_all(copies, 'z', 0, 0, axis_index_groups=[COLUMN], tiled=True)]
    all_to_all x1 -> x0, starting transfers between devices: 11.8 us -> none  [shards(): lax.all_to_all(copies, 'z', 0, 0, axis_index_groups=[COLUMN], tiled=True)]
    all_to_all x1 -> x0, waiting for transfers between devices: 6.37 us -> none  [shards(): lax.all_to_all(copies, 'z', 0, 0, axis_index_groups=[COLUMN], tiled=True)]
    pallas_call x10, Pallas kernels: 9.69 us -> 8.38 us  [call(): pl.pallas_call(kernel, out_shape=out_shape, in_specs=in_specs, out_specs=...]
  transfers between devices with their start and end apart: 4 -> 3, of which waited for: 3 -> 2; matrix products, arithmetic and copies ran while one was open for 0% -> 0% of each run, Pallas kernels for 9% -> 5%
where the time goes in v6:
time: 66.9 us; the launch traced here: 66.6 us
  blocking collectives  35.3 us (53%)
  starting transfers between devices  20.8 us (31%)
  Pallas kernels  8.38 us (13%)
  waiting for transfers between devices  1.3 us (2%)
  between operations  0.83 us (1%)
    all_to_all x1, blocking collectives, shards(): lax.all_to_all(copies, 'z', 0, 0, axis_index_groups=[COLUMN], tiled=True)  19.5 us
    all_to_all x1, blocking collectives, shards(): lax.all_to_all(copies, ('y', 'x'), 0, 0, axis_index_groups=[PLANE], tiled...  15.8 us
    ppermute x1, starting transfers between devices, shards(): core = lax.ppermute(pass_on, 'core', swap)  12.2 us
    pallas_call x10, Pallas kernels, call(): pl.pallas_call(kernel, out_shape=out_shape, in_specs=in_specs, out_specs=...  8.38 us
    ppermute x1, starting transfers between devices, shards(): chip = lax.ppermute(to_chip, ('x', 'core'), across)  4.64 us
    ppermute x1, starting transfers between devices, shards(): other = lax.ppermute(mine, 'core', swap)  3.9 us
  transfers between devices with their start and end apart: 3, of which 2 were waited for; matrix products, arithmetic and copies ran while one was open for 0% of the time, Pallas kernels for 5%

profile of v6, /device:TPU:1, one launch (start us, length us, event | category | flops | bytes accessed | tf_op | source)
XLA Modules:
  0.0 66.6 jit_solution(1773162971309795039)
XLA Ops:
  0.6 0.0 copy-start
  0.6 0.0 copy-start.1
  0.6 0.0 copy-start.2
  0.7 1.2 %shard_map.77 = bf16[8,128,128]{2,1,0:T(8,128)(2,1)S(1)} custom-call(bf16[8,128,128]{2,1,0:T(8,128)(2,1)} %bitcast.14, bf16[32,128,128]{2,1,0:T(8,128)(2,1)} %bitcast.6, bf16[32,128,128]{2,1,0:T(8,128)(2,1)} %bitcast.10), custom_call_target="tpu_custom_call" | custom-call | bytes 524288 | tf_op jit(solution)/shard_map/pallas_call | solution.py:42
  1.8 0.0 copy-start.3
  1.8 0.0 copy-start.4
  1.8 0.0 copy-start.5
  1.9 4.6 %collective-permute-start.1 = (bf16[8,128,128]{2,1,0:T(8,128)(2,1)S(1)}, bf16[8,128,128]{2,1,0:T(8,128)(2,1)S(1)}, u32[]{:S(2)}, u32[]{:S(2)}) collective-permute-start(bf16[8,128,128]{2,1,0:T(8,128)(2,1)S(1)} %shard_map.77), channel_id=1, source_target_pairs={{1,2},{2,1},{3,4},{4,3},{5,6},{6,5},{9,10},{10,9},{11,12},{12,11},... | collective-permute-start | bytes 786440 | tf_op jit(solution)/shard_map/ppermute | solution.py:394
  6.5 0.0 copy-done
  6.5 0.0 copy-done.1
  6.5 0.0 copy-done.2
  6.5 2.3 %shard_map.78 = (f32[32,32,128]{2,1,0:T(8,128)S(1)}, f32[3,8,32,128]{3,2,1,0:T(8,128)S(1)}, bf16[8,32,128]{2,1,0:T(8,128)(2,1)S(1)}, f32[2,32,128]{2,1,0:T(8,128)S(1)}, bf16[15,128,128]{2,1,0:T(8,128)(2,1)S(1)}) custom-call(bf16[32,32,128]{2,1,0:T(8,128)(2,1)S(1)} %bitcast.15, bf16[32,128,128]{2,1,0:T(8,128)(2,1)S(1)} %bitcast.7, ...), custom_call_target="tpu_custom_call" | custom-call | flops 400000000 | bytes 3145728 | tf_op jit(solution)/shard_map/pallas_call | solution.py:42
  8.8 12.2 %collective-permute-start = (bf16[15,128,128]{2,1,0:T(8,128)(2,1)S(1)}, bf16[15,128,128]{2,1,0:T(8,128)(2,1)S(1)}, u32[]{:S(2)}, u32[]{:S(2)}) collective-permute-start(bf16[15,128,128]{2,1,0:T(8,128)(2,1)S(1)} %get-tuple-element.37), channel_id=1, source_target_pairs={{0,1},{1,0},{2,3},{3,2},{4,5},{5,4},{6,7},{7,6},{8,9},{9,8},{10,11... | collective-permute-start | bytes 1474568 | tf_op jit(solution)/shard_map/ppermute | solution.py:417
  21.1 0.0 collective-permute-done.1.chip
  21.1 0.0 copy-done.3
  21.1 0.0 copy-done.4
  21.1 0.0 copy-done.5
  21.1 0.8 %shard_map.79 = (f32[4,32,128]{2,1,0:T(8,128)S(1)}, f32[32,128]{1,0:T(8,128)S(1)}) custom-call(bf16[8,128,128]{2,1,0:T(8,128)(2,1)S(1)} %collective-permute-done.1.chip, bf16[32,128,128]{2,1,0:T(8,128)(2,1)S(1)} %bitcast.8, bf16[32,128,128]{2,1,0:T(8,128)(2,1)S(1)} %bitcast.12, f32[3,8,32,128]{3,2,1,0:T(8,128)S(1)} %get-tuple-element.38.state, ...), custom_call_target="tpu_custom_call" | custom-call | flops 5000000000 | bytes 1048576 | tf_op jit(solution)/shard_map/pallas_call | solution.py:42
  21.9 0.6 collective-permute-done.core
  22.5 0.8 %shard_map.80 = (f32[4,32,128]{2,1,0:T(8,128)S(1)}, bf16[32,32,128]{2,1,0:T(8,128)(2,1)S(1)}) custom-call(bf16[15,128,128]{2,1,0:T(8,128)(2,1)S(1)} %collective-permute-done.core, bf16[32,128,128]{2,1,0:T(8,128)(2,1)S(1)} %bitcast.9, bf16[32,128,128]{2,1,0:T(8,128)(2,1)S(1)} %bitcast.13, f32[3,8,32,128]{3,2,1,0:T(8,128)S(1)} %get-tuple-element.38.state, ...), custom_call_target="tpu_custom_call" | custom-call | flops 100000000 | bytes 1048576 | tf_op jit(solution)/shard_map/pallas_call | solution.py:42
  23.3 15.8 %all_to_all.10.got = bf16[32,32,128]{2,1,0:T(8,128)(2,1)S(1)} all-to-all(bf16[32,32,128]{2,1,0:T(8,128)(2,1)S(1)} %get-tuple-element.43), channel_id=1, replica_groups={{516,0,2,4,6,128,130,132,134,896,898,900,902,256,258,260,262,768,770,77..., dimensions={0} | all-to-all | bytes 524288 | tf_op jit(solution)/shard_map/all_to_all | solution.py:442
  39.2 2.3 %shard_map.82 = (bf16[2,128,256]{2,1,0:T(8,128)(2,1)S(1)}, bf16[2,128,256]{2,1,0:T(8,128)(2,1)S(1)}, f32[32,32,128]{2,1,0:T(8,128)}) custom-call(bf16[128,128]{1,0:T(8,128)(2,1)S(1)} %copy-done.5, f32[2,128,128]{2,1,0:T(8,128)S(1)} %copy-done.4, f32[256,256]{1,0:T(8,128)S(1)} %copy-done.3, f32[4,32,128]{2,1,0:T(8,128)S(1)} %get-tuple-element.57.outer, ...), custom_call_target="tpu_custom_call" | custom-call | flops 100000000 | bytes 1048576 | tf_op jit(solution)/shard_map/pallas_call | solution.py:42
  41.5 19.5 %all_to_all.11.got = bf16[16,32,128]{2,1,0:T(8,128)(2,1)S(1)} all-to-all(bf16[16,32,128]{2,1,0:T(8,128)(2,1)S(1)} %shard_map.81), channel_id=1, replica_groups={{96,0,8,16,24,32,40,48,56,120,112,104,88,80,72,64},{97,1,9,17,25,33,41,..., dimensions={0} | all-to-all | bytes 262144 | tf_op jit(solution)/shard_map/all_to_all | solution.py:458
  61.0 0.1 shard_map.84
  61.1 3.9 %collective-permute-start.2 = (f32[32,128]{1,0:T(8,128)S(1)}, f32[32,128]{1,0:T(8,128)S(1)}, u32[]{:S(2)}, u32[]{:S(2)}) collective-permute-start(f32[32,128]{1,0:T(8,128)S(1)} %shard_map.83.mine), channel_id=1, source_target_pairs={{0,1},{1,0},{2,3},{3,2},{4,5},{5,4},{6,7},{7,6},{8,9},{9,8},{10,11... | collective-permute-start | bytes 49160 | tf_op jit(solution)/shard_map/ppermute | solution.py:472
  65.0 0.1 shard_map.85.part
  65.1 0.7 %collective-permute-done.2.other = f32[32,128]{1,0:T(8,128)S(1)} collective-permute-done((f32[32,128]{1,0:T(8,128)S(1)}, f32[32,128]{1,0:T(8,128)S(1)}, u32[]{:S(2)}, u32[]{:S(2)}) %collective-permute-start.2) | collective-permute-done | bytes 16416 | tf_op jit(solution)/shard_map/ppermute | solution.py:472
  65.8 0.8 %shard_map.86 = f32[32,256]{1,0:T(8,128)} custom-call(f32[32,256]{1,0:T(8,128)S(1)} %shard_map.85.part, f32[32,128]{1,0:T(8,128)S(1)} %collective-permute-done.2.other, bf16[2,128,256]{2,1,0:T(8,128)(2,1)S(1)} %get-tuple-element.68.top, bf16[2,128,256]{2,1,0:T(8,128)(2,1)S(1)} %get-tuple-element.69.rest), custom_call_target="tpu_custom_call" | custom-call | flops 10000000 | bytes 131072 | tf_op jit(solution)/shard_map/pallas_call | solution.py:42
  (2 shorter events, 0.1 us)
Async XLA Ops:
  0.6 5.9 %copy-start = (bf16[1,32,128,128]{3,2,1,0:T(8,128)(2,1)S(1)}, bf16[1,32,128,128]{3,2,1,0:T(8,128)(2,1)}, u32[]{:S(2)}) copy-start(bf16[1,32,128,128]{3,2,1,0:T(8,128)(2,1)} %param.7) | copy-start | bytes 3145732
  0.6 5.9 %copy-start.1 = (bf16[1,32,128,128]{3,2,1,0:T(8,128)(2,1)S(1)}, bf16[1,32,128,128]{3,2,1,0:T(8,128)(2,1)}, u32[]{:S(2)}) copy-start(bf16[1,32,128,128]{3,2,1,0:T(8,128)(2,1)} %param.8) | copy-start | bytes 3145732
  0.6 5.9 %copy-start.2 = (bf16[1,32,32,128]{3,2,1,0:T(8,128)(2,1)S(1)}, bf16[1,32,32,128]{3,2,1,0:T(8,128)(2,1)}, u32[]{:S(2)}) copy-start(bf16[1,32,32,128]{3,2,1,0:T(8,128)(2,1)} %param.6) | copy-start | bytes 786436
  1.8 19.3 %copy-start.3 = (f32[256,256]{1,0:T(8,128)S(1)}, f32[256,256]{1,0:T(8,128)}, u32[]{:S(2)}) copy-start(f32[256,256]{1,0:T(8,128)} %inverse.4) | copy-start | bytes 786436
  1.8 19.3 %copy-start.4 = (f32[2,128,128]{2,1,0:T(8,128)S(1)}, f32[2,128,128]{2,1,0:T(8,128)}, u32[]{:S(2)}) copy-start(f32[2,128,128]{2,1,0:T(8,128)} %level.4) | copy-start | bytes 393220
  1.8 19.3 %copy-start.5 = (bf16[128,128]{1,0:T(8,128)(2,1)S(1)}, bf16[128,128]{1,0:T(8,128)(2,1)}, u32[]{:S(2)}) copy-start(bf16[128,128]{1,0:T(8,128)(2,1)} %restrict.4) | copy-start | bytes 98308
  1.9 19.2 %collective-permute-start.1 = (bf16[8,128,128]{2,1,0:T(8,128)(2,1)S(1)}, bf16[8,128,128]{2,1,0:T(8,128)(2,1)S(1)}, u32[]{:S(2)}, u32[]{:S(2)}) collective-permute-start(bf16[8,128,128]{2,1,0:T(8,128)(2,1)S(1)} %shard_map.77), channel_id=1, source_target_pairs={{1,2},{2,1},{3,4},{4,3},{5,6},{6,5},{9,10},{10,9},{11,12},{12,11},... | collective-permute-start | bytes 786440 | tf_op jit(solution)/shard_map/ppermute | solution.py:394
  8.8 13.7 %collective-permute-start = (bf16[15,128,128]{2,1,0:T(8,128)(2,1)S(1)}, bf16[15,128,128]{2,1,0:T(8,128)(2,1)S(1)}, u32[]{:S(2)}, u32[]{:S(2)}) collective-permute-start(bf16[15,128,128]{2,1,0:T(8,128)(2,1)S(1)} %get-tuple-element.37), channel_id=1, source_target_pairs={{0,1},{1,0},{2,3},{3,2},{4,5},{5,4},{6,7},{7,6},{8,9},{9,8},{10,11... | collective-permute-start | bytes 1474568 | tf_op jit(solution)/shard_map/ppermute | solution.py:417
  61.1 4.7 %collective-permute-start.2 = (f32[32,128]{1,0:T(8,128)S(1)}, f32[32,128]{1,0:T(8,128)S(1)}, u32[]{:S(2)}, u32[]{:S(2)}) collective-permute-start(f32[32,128]{1,0:T(8,128)S(1)} %shard_map.83.mine), channel_id=1, source_target_pairs={{0,1},{1,0},{2,3},{3,2},{4,5},{5,4},{6,7},{7,6},{8,9},{9,8},{10,11... | collective-permute-start | bytes 49160 | tf_op jit(solution)/shard_map/ppermute | solution.py:472

commit v7 on v6

--- a/solution.py
+++ b/solution.py
@@ -284,8 +284,8 @@
     beside = jnp.where(c == 0, total(res, range(4, 8)), total(res, range(4)))
     other = core[14, rows(0), :].astype(F32) + core[14, rows(1), :].astype(F32)
     whole = ((sums_in[c] + other) + (part[...] + beside)).astype(BF16)
-    for i in range(copies.shape[0]):
-        copies[i] = whole
+    for i, place in enumerate(PLANE):
+        copies[i] = whole[: VECS // 2] if place % 2 == 0 else whole[VECS // 2 :]
 
     @pl.when(c == 0)
     def _():
@@ -326,7 +326,9 @@
 
 
 def total_kernel(got, out):
-    out[...] = sum_of(got)
+    whole = sum_of(got)
+    for i in range(out.shape[0]):
+        out[i] = whole
 
 
 def make_maps(restrict, level, inverse, top, rest):
@@ -365,19 +367,14 @@
     return times(x_top, top) + (times(x_top, rest) + times(x_rest, top))
 
 
-def own_kernel(mine, top, rest, out):
-    c = core_index()
-    out[...] = mapped(mine[...], top[c], rest[c])
-
-
-def solve_kernel(part, other, top, rest, out):
-    c = 1 - core_index()
-    out[...] = part[...] + mapped(other[...], top[c], rest[c])
+def solve_kernel(got, top, rest, out):
+    tiles = [jnp.concatenate([got[c], got[2 + c]], axis=0) for c in range(2)]
+    out[...] = mapped(tiles[0], top[0], rest[0]) + mapped(tiles[1], top[1], rest[1])
 
 
 def shards(right_side, diag_blocks, link_blocks, restrict_map, level_map, coarse_inverse):
     rhs, diag, link = right_side[0], diag_blocks[0], link_blocks[0]
-    tile, pack = (VECS, ROWS), (8, ROWS, ROWS)
+    tile, part_tile, pack = (VECS, ROWS), (VECS // 2, ROWS), (8, ROWS, ROWS)
     to_chip = call(
         pack_kernel,
         bf16(pack),
@@ -427,7 +424,7 @@
     )
     middle, copies = call(
         middle_kernel,
-        (f32((4,) + tile), bf16((32,) + tile)),
+        (f32((4,) + tile), bf16((32,) + part_tile)),
         [VMEM] * 7,
         (VMEM,) * 2,
         (core, diag, link, state, near, sums, part),
@@ -440,7 +437,7 @@
         cost=(10**8, 1 << 20),
     )
     copies = lax.all_to_all(copies, ("y", "x"), 0, 0, axis_index_groups=[PLANE], tiled=True)
-    copies = call(functools.partial(merge_kernel, 16), bf16((16,) + tile), [VMEM], VMEM, (copies,), cost=(0, 1 << 18))
+    copies = call(functools.partial(merge_kernel, 16), bf16((16,) + part_tile), [VMEM], VMEM, (copies,), cost=(0, 1 << 18))
     wide, whole = bf16((2, ROWS, 2 * ROWS)), f32((TILES,) + tile)
     sources = (restrict_map, level_map, coarse_inverse, outer, middle, rel)
     copies, middle_later = lax.optimization_barrier((copies, middle))
@@ -467,13 +464,11 @@
         cost=(10**8, 1 << 20),
         input_output_aliases={8: 2},
     )
-    mine = call(total_kernel, f32(tile), [VMEM], VMEM, (copies,), cost=(0, 1 << 17))
+    mine = call(total_kernel, f32((4,) + part_tile), [VMEM], VMEM, (copies,), cost=(0, 1 << 17))
     mine, top, rest, rel = lax.optimization_barrier((mine, top, rest, rel))
-    other = lax.ppermute(mine, "core", swap)
-    solution_shape = f32((VECS, 2 * ROWS))
-    part = call(own_kernel, solution_shape, [VMEM] * 3, VMEM, (mine, top, rest), cost=(10**7, 1 << 17))
+    mine = lax.all_to_all(mine, ("x", "core"), 0, 0, axis_index_groups=[[0, 1, 2, 3], [4, 5, 6, 7]], tiled=True)
     solved = call(
-        solve_kernel, solution_shape, [VMEM] * 4, VMEM, (part, other, top, rest), cost=(10**7, 1 << 17)
+        solve_kernel, f32((VECS, 2 * ROWS)), [VMEM] * 3, VMEM, (mine, top, rest), cost=(10**7, 1 << 17)
     )
     return (rel[None], solved[None, None])
 

time: 66.9 us -> 64.6 us (0.966)
  starting transfers between devices: 20.8 us -> 16.9 us
  blocking collectives: 35.3 us -> 37.8 us
  waiting for transfers between devices: 1.3 us -> 0.63 us
    all_to_all x0 -> x1, blocking collectives: none -> 7.47 us  [shards(): lax.all_to_all(mine, ('x', 'core'), 0, 0, axis_index_groups=[[0, 1, 2, 3]...]
    ppermute x1 -> x0, starting transfers between devices: 3.9 us -> none  [shards(): other = lax.ppermute(mine, 'core', swap)]
    all_to_all x1, blocking collectives: 15.8 us -> 13 us  [shards(): lax.all_to_all(copies, ('y', 'x'), 0, 0, axis_index_groups=[PLANE], tiled...]
    all_to_all x1, blocking collectives: 19.5 us -> 17.3 us  [shards(): lax.all_to_all(copies, 'z', 0, 0, axis_index_groups=[COLUMN], tiled=True)]
    ppermute x1 -> x0, waiting for transfers between devices: 0.67 us -> none  [shards(): other = lax.ppermute(mine, 'core', swap)]
    pallas_call x10 -> x9, Pallas kernels: 8.38 us -> 8.23 us  [call(): pl.pallas_call(kernel, out_shape=out_shape, in_specs=in_specs, out_specs=...]
  transfers between devices with their start and end apart: 3 -> 2, of which waited for: 2 -> 1; matrix products, arithmetic and copies ran while one was open for 0% -> 0% of each run, Pallas kernels for 5% -> 5%
where the time goes in v7:
time: 64.6 us; the launch traced here: 64.3 us
  blocking collectives  37.8 us (59%)
  starting transfers between devices  16.9 us (26%)
  Pallas kernels  8.23 us (13%)
  between operations  0.8 us (1%)
    all_to_all x1, blocking collectives, shards(): lax.all_to_all(copies, 'z', 0, 0, axis_index_groups=[COLUMN], tiled=True)  17.3 us
    all_to_all x1, blocking collectives, shards(): lax.all_to_all(copies, ('y', 'x'), 0, 0, axis_index_groups=[PLANE], tiled...  13 us
    ppermute x1, starting transfers between devices, shards(): core = lax.ppermute(pass_on, 'core', swap)  12.2 us
    pallas_call x9, Pallas kernels, call(): pl.pallas_call(kernel, out_shape=out_shape, in_specs=in_specs, out_specs=...  8.23 us
    all_to_all x1, blocking collectives, shards(): lax.all_to_all(mine, ('x', 'core'), 0, 0, axis_index_groups=[[0, 1, 2, 3]...  7.47 us
    ppermute x1, starting transfers between devices, shards(): chip = lax.ppermute(to_chip, ('x', 'core'), across)  4.64 us
  transfers between devices with their start and end apart: 2, of which 1 were waited for; matrix products, arithmetic and copies ran while one was open for 0% of the time, Pallas kernels for 5%

profile of v7, /device:TPU:1, one launch (start us, length us, event | category | flops | bytes accessed | tf_op | source)
XLA Modules:
  0.0 64.3 jit_solution(5901284718093780637)
XLA Ops:
  0.6 0.0 copy-start
  0.6 0.0 copy-start.1
  0.6 0.0 copy-start.2
  0.7 1.2 %shard_map.77 = bf16[8,128,128]{2,1,0:T(8,128)(2,1)S(1)} custom-call(bf16[8,128,128]{2,1,0:T(8,128)(2,1)} %bitcast.14, bf16[32,128,128]{2,1,0:T(8,128)(2,1)} %bitcast.6, bf16[32,128,128]{2,1,0:T(8,128)(2,1)} %bitcast.10), custom_call_target="tpu_custom_call" | custom-call | bytes 524288 | tf_op jit(solution)/shard_map/pallas_call | solution.py:42
  1.8 0.0 copy-start.3
  1.8 0.0 copy-start.4
  1.8 0.0 copy-start.5
  1.9 4.6 %collective-permute-start.1 = (bf16[8,128,128]{2,1,0:T(8,128)(2,1)S(1)}, bf16[8,128,128]{2,1,0:T(8,128)(2,1)S(1)}, u32[]{:S(2)}, u32[]{:S(2)}) collective-permute-start(bf16[8,128,128]{2,1,0:T(8,128)(2,1)S(1)} %shard_map.77), channel_id=1, source_target_pairs={{1,2},{2,1},{3,4},{4,3},{5,6},{6,5},{9,10},{10,9},{11,12},{12,11},... | collective-permute-start | bytes 786440 | tf_op jit(solution)/shard_map/ppermute | solution.py:391
  6.5 0.0 copy-done
  6.5 0.0 copy-done.1
  6.5 0.0 copy-done.2
  6.5 2.3 %shard_map.78 = (f32[32,32,128]{2,1,0:T(8,128)S(1)}, f32[3,8,32,128]{3,2,1,0:T(8,128)S(1)}, bf16[8,32,128]{2,1,0:T(8,128)(2,1)S(1)}, f32[2,32,128]{2,1,0:T(8,128)S(1)}, bf16[15,128,128]{2,1,0:T(8,128)(2,1)S(1)}) custom-call(bf16[32,32,128]{2,1,0:T(8,128)(2,1)S(1)} %bitcast.15, bf16[32,128,128]{2,1,0:T(8,128)(2,1)S(1)} %bitcast.7, ...), custom_call_target="tpu_custom_call" | custom-call | flops 400000000 | bytes 3145728 | tf_op jit(solution)/shard_map/pallas_call | solution.py:42
  8.8 12.2 %collective-permute-start = (bf16[15,128,128]{2,1,0:T(8,128)(2,1)S(1)}, bf16[15,128,128]{2,1,0:T(8,128)(2,1)S(1)}, u32[]{:S(2)}, u32[]{:S(2)}) collective-permute-start(bf16[15,128,128]{2,1,0:T(8,128)(2,1)S(1)} %get-tuple-element.37), channel_id=1, source_target_pairs={{0,1},{1,0},{2,3},{3,2},{4,5},{5,4},{6,7},{7,6},{8,9},{9,8},{10,11... | collective-permute-start | bytes 1474568 | tf_op jit(solution)/shard_map/ppermute | solution.py:414
  21.1 0.0 collective-permute-done.1.chip
  21.1 0.0 copy-done.3
  21.1 0.0 copy-done.4
  21.1 0.0 copy-done.5
  21.1 0.8 %shard_map.79 = (f32[4,32,128]{2,1,0:T(8,128)S(1)}, f32[32,128]{1,0:T(8,128)S(1)}) custom-call(bf16[8,128,128]{2,1,0:T(8,128)(2,1)S(1)} %collective-permute-done.1.chip, bf16[32,128,128]{2,1,0:T(8,128)(2,1)S(1)} %bitcast.8, bf16[32,128,128]{2,1,0:T(8,128)(2,1)S(1)} %bitcast.12, f32[3,8,32,128]{3,2,1,0:T(8,128)S(1)} %get-tuple-element.38.state, ...), custom_call_target="tpu_custom_call" | custom-call | flops 5000000000 | bytes 1048576 | tf_op jit(solution)/shard_map/pallas_call | solution.py:42
  21.9 0.6 collective-permute-done.core
  22.5 0.8 %shard_map.80 = (f32[4,32,128]{2,1,0:T(8,128)S(1)}, bf16[32,16,128]{2,1,0:T(8,128)(2,1)S(1)}) custom-call(bf16[15,128,128]{2,1,0:T(8,128)(2,1)S(1)} %collective-permute-done.core, bf16[32,128,128]{2,1,0:T(8,128)(2,1)S(1)} %bitcast.9, bf16[32,128,128]{2,1,0:T(8,128)(2,1)S(1)} %bitcast.13, f32[3,8,32,128]{3,2,1,0:T(8,128)S(1)} %get-tuple-element.38.state, ...), custom_call_target="tpu_custom_call" | custom-call | flops 100000000 | bytes 1048576 | tf_op jit(solution)/shard_map/pallas_call | solution.py:42
  23.3 13.0 %all_to_all.15.got = bf16[32,16,128]{2,1,0:T(8,128)(2,1)S(1)} all-to-all(bf16[32,16,128]{2,1,0:T(8,128)(2,1)S(1)} %get-tuple-element.43), channel_id=1, replica_groups={{516,0,2,4,6,128,130,132,134,896,898,900,902,256,258,260,262,768,770,77..., dimensions={0} | all-to-all | bytes 262144 | tf_op jit(solution)/shard_map/all_to_all | solution.py:439
  36.4 2.3 %shard_map.82 = (bf16[2,128,256]{2,1,0:T(8,128)(2,1)S(1)}, bf16[2,128,256]{2,1,0:T(8,128)(2,1)S(1)}, f32[32,32,128]{2,1,0:T(8,128)}) custom-call(bf16[128,128]{1,0:T(8,128)(2,1)S(1)} %copy-done.5, f32[2,128,128]{2,1,0:T(8,128)S(1)} %copy-done.4, f32[256,256]{1,0:T(8,128)S(1)} %copy-done.3, f32[4,32,128]{2,1,0:T(8,128)S(1)} %get-tuple-element.57.outer, ...), custom_call_target="tpu_custom_call" | custom-call | flops 100000000 | bytes 1048576 | tf_op jit(solution)/shard_map/pallas_call | solution.py:42
  38.7 17.3 %all_to_all.16.got = bf16[16,16,128]{2,1,0:T(8,128)(2,1)S(1)} all-to-all(bf16[16,16,128]{2,1,0:T(8,128)(2,1)S(1)} %shard_map.81), channel_id=1, replica_groups={{96,0,8,16,24,32,40,48,56,120,112,104,88,80,72,64},{97,1,9,17,25,33,41,..., dimensions={0} | all-to-all | bytes 131072 | tf_op jit(solution)/shard_map/all_to_all | solution.py:455
  56.0 0.1 shard_map.84
  56.0 7.5 %all_to_all.17.got = f32[4,16,128]{2,1,0:T(8,128)S(1)} all-to-all(f32[4,16,128]{2,1,0:T(8,128)S(1)} %shard_map.83), channel_id=1, replica_groups={{0,1,2,3},{4,5,6,7},{8,9,10,11},{12,13,14,15},{16,17,18,19},{20,21,22,2..., dimensions={0} | all-to-all | bytes 65536 | tf_op jit(solution)/shard_map/all_to_all | solution.py:469
  63.5 0.8 %shard_map.85 = f32[32,256]{1,0:T(8,128)} custom-call(f32[4,16,128]{2,1,0:T(8,128)S(1)} %all_to_all.17.got, bf16[2,128,256]{2,1,0:T(8,128)(2,1)S(1)} %get-tuple-element.68.top, bf16[2,128,256]{2,1,0:T(8,128)(2,1)S(1)} %get-tuple-element.69.rest), custom_call_target="tpu_custom_call" | custom-call | flops 10000000 | bytes 131072 | tf_op jit(solution)/shard_map/pallas_call | solution.py:42
  (2 shorter events, 0.0 us)
Async XLA Ops:
  0.6 5.9 %copy-start = (bf16[1,32,128,128]{3,2,1,0:T(8,128)(2,1)S(1)}, bf16[1,32,128,128]{3,2,1,0:T(8,128)(2,1)}, u32[]{:S(2)}) copy-start(bf16[1,32,128,128]{3,2,1,0:T(8,128)(2,1)} %param.7) | copy-start | bytes 3145732
  0.6 5.9 %copy-start.1 = (bf16[1,32,128,128]{3,2,1,0:T(8,128)(2,1)S(1)}, bf16[1,32,128,128]{3,2,1,0:T(8,128)(2,1)}, u32[]{:S(2)}) copy-start(bf16[1,32,128,128]{3,2,1,0:T(8,128)(2,1)} %param.8) | copy-start | bytes 3145732
  0.6 5.9 %copy-start.2 = (bf16[1,32,32,128]{3,2,1,0:T(8,128)(2,1)S(1)}, bf16[1,32,32,128]{3,2,1,0:T(8,128)(2,1)}, u32[]{:S(2)}) copy-start(bf16[1,32,32,128]{3,2,1,0:T(8,128)(2,1)} %param.6) | copy-start | bytes 786436
  1.8 19.3 %copy-start.3 = (f32[256,256]{1,0:T(8,128)S(1)}, f32[256,256]{1,0:T(8,128)}, u32[]{:S(2)}) copy-start(f32[256,256]{1,0:T(8,128)} %inverse.4) | copy-start | bytes 786436
  1.8 19.3 %copy-start.4 = (f32[2,128,128]{2,1,0:T(8,128)S(1)}, f32[2,128,128]{2,1,0:T(8,128)}, u32[]{:S(2)}) copy-start(f32[2,128,128]{2,1,0:T(8,128)} %level.4) | copy-start | bytes 393220
  1.8 19.3 %copy-start.5 = (bf16[128,128]{1,0:T(8,128)(2,1)S(1)}, bf16[128,128]{1,0:T(8,128)(2,1)}, u32[]{:S(2)}) copy-start(bf16[128,128]{1,0:T(8,128)(2,1)} %restrict.4) | copy-start | bytes 98308
  1.9 19.2 %collective-permute-start.1 = (bf16[8,128,128]{2,1,0:T(8,128)(2,1)S(1)}, bf16[8,128,128]{2,1,0:T(8,128)(2,1)S(1)}, u32[]{:S(2)}, u32[]{:S(2)}) collective-permute-start(bf16[8,128,128]{2,1,0:T(8,128)(2,1)S(1)} %shard_map.77), channel_id=1, source_target_pairs={{1,2},{2,1},{3,4},{4,3},{5,6},{6,5},{9,10},{10,9},{11,12},{12,11},... | collective-permute-start | bytes 786440 | tf_op jit(solution)/shard_map/ppermute | solution.py:391
  8.8 13.7 %collective-permute-start = (bf16[15,128,128]{2,1,0:T(8,128)(2,1)S(1)}, bf16[15,128,128]{2,1,0:T(8,128)(2,1)S(1)}, u32[]{:S(2)}, u32[]{:S(2)}) collective-permute-start(bf16[15,128,128]{2,1,0:T(8,128)(2,1)S(1)} %get-tuple-element.37), channel_id=1, source_target_pairs={{0,1},{1,0},{2,3},{3,2},{4,5},{5,4},{6,7},{7,6},{8,9},{9,8},{10,11... | collective-permute-start | bytes 1474568 | tf_op jit(solution)/shard_map/ppermute | solution.py:414

commit v8 on v7

--- a/solution.py
+++ b/solution.py
@@ -368,7 +368,7 @@
 
 
 def solve_kernel(got, top, rest, out):
-    tiles = [jnp.concatenate([got[c], got[2 + c]], axis=0) for c in range(2)]
+    tiles = [jnp.concatenate([got[u], got[d]], axis=0) for u, d in ((1, 0), (2, 3))]
     out[...] = mapped(tiles[0], top[0], rest[0]) + mapped(tiles[1], top[1], rest[1])
 
 
@@ -466,7 +466,7 @@
     )
     mine = call(total_kernel, f32((4,) + part_tile), [VMEM], VMEM, (copies,), cost=(0, 1 << 17))
     mine, top, rest, rel = lax.optimization_barrier((mine, top, rest, rel))
-    mine = lax.all_to_all(mine, ("x", "core"), 0, 0, axis_index_groups=[[0, 1, 2, 3], [4, 5, 6, 7]], tiled=True)
+    mine = lax.all_to_all(mine, ("x", "core"), 0, 0, axis_index_groups=[[2, 0, 1, 3], [6, 4, 5, 7]], tiled=True)
     solved = call(
         solve_kernel, f32((VECS, 2 * ROWS)), [VMEM] * 3, VMEM, (mine, top, rest), cost=(10**7, 1 << 17)
     )

time: 64.6 us -> 64.2 us (level)
  no operation moved by 1% of the time
where the time goes in v8:
time: 64.2 us; the launch traced here: 63.9 us
  blocking collectives  37.3 us (58%)
  starting transfers between devices  16.9 us (26%)
  Pallas kernels  8.23 us (13%)
  between operations  0.8 us (1%)
    all_to_all x1, blocking collectives, shards(): lax.all_to_all(copies, 'z', 0, 0, axis_index_groups=[COLUMN], tiled=True)  17.3 us
    all_to_all x1, blocking collectives, shards(): lax.all_to_all(copies, ('y', 'x'), 0, 0, axis_index_groups=[PLANE], tiled...  13 us
    ppermute x1, starting transfers between devices, shards(): core = lax.ppermute(pass_on, 'core', swap)  12.2 us
    pallas_call x9, Pallas kernels, call(): pl.pallas_call(kernel, out_shape=out_shape, in_specs=in_specs, out_specs=...  8.23 us
    all_to_all x1, blocking collectives, shards(): lax.all_to_all(mine, ('x', 'core'), 0, 0, axis_index_groups=[[2, 0, 1, 3]...  7.04 us
    ppermute x1, starting transfers between devices, shards(): chip = lax.ppermute(to_chip, ('x', 'core'), across)  4.64 us
  transfers between devices with their start and end apart: 2, of which 1 were waited for; matrix products, arithmetic and copies ran while one was open for 0% of the time, Pallas kernels for 5%

profile of v8, /device:TPU:1, one launch (start us, length us, event | category | flops | bytes accessed | tf_op | source)
XLA Modules:
  0.0 63.9 jit_solution(16293096383101788805)
XLA Ops:
  0.6 0.0 copy-start
  0.6 0.0 copy-start.1
  0.6 0.0 copy-start.2
  0.7 1.2 %shard_map.77 = bf16[8,128,128]{2,1,0:T(8,128)(2,1)S(1)} custom-call(bf16[8,128,128]{2,1,0:T(8,128)(2,1)} %bitcast.14, bf16[32,128,128]{2,1,0:T(8,128)(2,1)} %bitcast.6, bf16[32,128,128]{2,1,0:T(8,128)(2,1)} %bitcast.10), custom_call_target="tpu_custom_call" | custom-call | bytes 524288 | tf_op jit(solution)/shard_map/pallas_call | solution.py:42
  1.8 0.0 copy-start.3
  1.8 0.0 copy-start.4
  1.8 0.0 copy-start.5
  1.9 4.6 %collective-permute-start.1 = (bf16[8,128,128]{2,1,0:T(8,128)(2,1)S(1)}, bf16[8,128,128]{2,1,0:T(8,128)(2,1)S(1)}, u32[]{:S(2)}, u32[]{:S(2)}) collective-permute-start(bf16[8,128,128]{2,1,0:T(8,128)(2,1)S(1)} %shard_map.77), channel_id=1, source_target_pairs={{1,2},{2,1},{3,4},{4,3},{5,6},{6,5},{9,10},{10,9},{11,12},{12,11},... | collective-permute-start | bytes 786440 | tf_op jit(solution)/shard_map/ppermute | solution.py:391
  6.5 0.0 copy-done
  6.5 0.0 copy-done.1
  6.5 0.0 copy-done.2
  6.5 2.3 %shard_map.78 = (f32[32,32,128]{2,1,0:T(8,128)S(1)}, f32[3,8,32,128]{3,2,1,0:T(8,128)S(1)}, bf16[8,32,128]{2,1,0:T(8,128)(2,1)S(1)}, f32[2,32,128]{2,1,0:T(8,128)S(1)}, bf16[15,128,128]{2,1,0:T(8,128)(2,1)S(1)}) custom-call(bf16[32,32,128]{2,1,0:T(8,128)(2,1)S(1)} %bitcast.15, bf16[32,128,128]{2,1,0:T(8,128)(2,1)S(1)} %bitcast.7, ...), custom_call_target="tpu_custom_call" | custom-call | flops 400000000 | bytes 3145728 | tf_op jit(solution)/shard_map/pallas_call | solution.py:42
  8.8 12.2 %collective-permute-start = (bf16[15,128,128]{2,1,0:T(8,128)(2,1)S(1)}, bf16[15,128,128]{2,1,0:T(8,128)(2,1)S(1)}, u32[]{:S(2)}, u32[]{:S(2)}) collective-permute-start(bf16[15,128,128]{2,1,0:T(8,128)(2,1)S(1)} %get-tuple-element.37), channel_id=1, source_target_pairs={{0,1},{1,0},{2,3},{3,2},{4,5},{5,4},{6,7},{7,6},{8,9},{9,8},{10,11... | collective-permute-start | bytes 1474568 | tf_op jit(solution)/shard_map/ppermute | solution.py:414
  21.1 0.0 collective-permute-done.1.chip
  21.1 0.0 copy-done.3
  21.1 0.0 copy-done.4
  21.1 0.0 copy-done.5
  21.1 0.8 %shard_map.79 = (f32[4,32,128]{2,1,0:T(8,128)S(1)}, f32[32,128]{1,0:T(8,128)S(1)}) custom-call(bf16[8,128,128]{2,1,0:T(8,128)(2,1)S(1)} %collective-permute-done.1.chip, bf16[32,128,128]{2,1,0:T(8,128)(2,1)S(1)} %bitcast.8, bf16[32,128,128]{2,1,0:T(8,128)(2,1)S(1)} %bitcast.12, f32[3,8,32,128]{3,2,1,0:T(8,128)S(1)} %get-tuple-element.38.state, ...), custom_call_target="tpu_custom_call" | custom-call | flops 5000000000 | bytes 1048576 | tf_op jit(solution)/shard_map/pallas_call | solution.py:42
  21.9 0.6 collective-permute-done.core
  22.5 0.8 %shard_map.80 = (f32[4,32,128]{2,1,0:T(8,128)S(1)}, bf16[32,16,128]{2,1,0:T(8,128)(2,1)S(1)}) custom-call(bf16[15,128,128]{2,1,0:T(8,128)(2,1)S(1)} %collective-permute-done.core, bf16[32,128,128]{2,1,0:T(8,128)(2,1)S(1)} %bitcast.9, bf16[32,128,128]{2,1,0:T(8,128)(2,1)S(1)} %bitcast.13, f32[3,8,32,128]{3,2,1,0:T(8,128)S(1)} %get-tuple-element.38.state, ...), custom_call_target="tpu_custom_call" | custom-call | flops 100000000 | bytes 1048576 | tf_op jit(solution)/shard_map/pallas_call | solution.py:42
  23.3 13.0 %all_to_all.15.got = bf16[32,16,128]{2,1,0:T(8,128)(2,1)S(1)} all-to-all(bf16[32,16,128]{2,1,0:T(8,128)(2,1)S(1)} %get-tuple-element.43), channel_id=1, replica_groups={{516,0,2,4,6,128,130,132,134,896,898,900,902,256,258,260,262,768,770,77..., dimensions={0} | all-to-all | bytes 262144 | tf_op jit(solution)/shard_map/all_to_all | solution.py:439
  36.4 2.3 %shard_map.82 = (bf16[2,128,256]{2,1,0:T(8,128)(2,1)S(1)}, bf16[2,128,256]{2,1,0:T(8,128)(2,1)S(1)}, f32[32,32,128]{2,1,0:T(8,128)}) custom-call(bf16[128,128]{1,0:T(8,128)(2,1)S(1)} %copy-done.5, f32[2,128,128]{2,1,0:T(8,128)S(1)} %copy-done.4, f32[256,256]{1,0:T(8,128)S(1)} %copy-done.3, f32[4,32,128]{2,1,0:T(8,128)S(1)} %get-tuple-element.57.outer, ...), custom_call_target="tpu_custom_call" | custom-call | flops 100000000 | bytes 1048576 | tf_op jit(solution)/shard_map/pallas_call | solution.py:42
  38.7 17.3 %all_to_all.16.got = bf16[16,16,128]{2,1,0:T(8,128)(2,1)S(1)} all-to-all(bf16[16,16,128]{2,1,0:T(8,128)(2,1)S(1)} %shard_map.81), channel_id=1, replica_groups={{96,0,8,16,24,32,40,48,56,120,112,104,88,80,72,64},{97,1,9,17,25,33,41,..., dimensions={0} | all-to-all | bytes 131072 | tf_op jit(solution)/shard_map/all_to_all | solution.py:455
  56.0 0.1 shard_map.84
  56.0 7.0 %all_to_all.17.got = f32[4,16,128]{2,1,0:T(8,128)S(1)} all-to-all(f32[4,16,128]{2,1,0:T(8,128)S(1)} %shard_map.83), channel_id=1, replica_groups={{2,0,1,3},{6,4,5,7},{10,8,9,11},{14,12,13,15},{18,16,17,19},{22,20,21,2..., dimensions={0} | all-to-all | bytes 65536 | tf_op jit(solution)/shard_map/all_to_all | solution.py:469
  63.1 0.8 %shard_map.85 = f32[32,256]{1,0:T(8,128)} custom-call(f32[4,16,128]{2,1,0:T(8,128)S(1)} %all_to_all.17.got, bf16[2,128,256]{2,1,0:T(8,128)(2,1)S(1)} %get-tuple-element.68.top, bf16[2,128,256]{2,1,0:T(8,128)(2,1)S(1)} %get-tuple-element.69.rest), custom_call_target="tpu_custom_call" | custom-call | flops 10000000 | bytes 131072 | tf_op jit(solution)/shard_map/pallas_call | solution.py:42
  (2 shorter events, 0.0 us)
Async XLA Ops:
  0.6 5.9 %copy-start = (bf16[1,32,128,128]{3,2,1,0:T(8,128)(2,1)S(1)}, bf16[1,32,128,128]{3,2,1,0:T(8,128)(2,1)}, u32[]{:S(2)}) copy-start(bf16[1,32,128,128]{3,2,1,0:T(8,128)(2,1)} %param.7) | copy-start | bytes 3145732
  0.6 5.9 %copy-start.1 = (bf16[1,32,128,128]{3,2,1,0:T(8,128)(2,1)S(1)}, bf16[1,32,128,128]{3,2,1,0:T(8,128)(2,1)}, u32[]{:S(2)}) copy-start(bf16[1,32,128,128]{3,2,1,0:T(8,128)(2,1)} %param.8) | copy-start | bytes 3145732
  0.6 5.9 %copy-start.2 = (bf16[1,32,32,128]{3,2,1,0:T(8,128)(2,1)S(1)}, bf16[1,32,32,128]{3,2,1,0:T(8,128)(2,1)}, u32[]{:S(2)}) copy-start(bf16[1,32,32,128]{3,2,1,0:T(8,128)(2,1)} %param.6) | copy-start | bytes 786436
  1.8 19.3 %copy-start.3 = (f32[256,256]{1,0:T(8,128)S(1)}, f32[256,256]{1,0:T(8,128)}, u32[]{:S(2)}) copy-start(f32[256,256]{1,0:T(8,128)} %inverse.4) | copy-start | bytes 786436
  1.8 19.3 %copy-start.4 = (f32[2,128,128]{2,1,0:T(8,128)S(1)}, f32[2,128,128]{2,1,0:T(8,128)}, u32[]{:S(2)}) copy-start(f32[2,128,128]{2,1,0:T(8,128)} %level.4) | copy-start | bytes 393220
  1.8 19.3 %copy-start.5 = (bf16[128,128]{1,0:T(8,128)(2,1)S(1)}, bf16[128,128]{1,0:T(8,128)(2,1)}, u32[]{:S(2)}) copy-start(bf16[128,128]{1,0:T(8,128)(2,1)} %restrict.4) | copy-start | bytes 98308
  1.9 19.2 %collective-permute-start.1 = (bf16[8,128,128]{2,1,0:T(8,128)(2,1)S(1)}, bf16[8,128,128]{2,1,0:T(8,128)(2,1)S(1)}, u32[]{:S(2)}, u32[]{:S(2)}) collective-permute-start(bf16[8,128,128]{2,1,0:T(8,128)(2,1)S(1)} %shard_map.77), channel_id=1, source_target_pairs={{1,2},{2,1},{3,4},{4,3},{5,6},{6,5},{9,10},{10,9},{11,12},{12,11},... | collective-permute-start | bytes 786440 | tf_op jit(solution)/shard_map/ppermute | solution.py:391
  8.8 13.7 %collective-permute-start = (bf16[15,128,128]{2,1,0:T(8,128)(2,1)S(1)}, bf16[15,128,128]{2,1,0:T(8,128)(2,1)S(1)}, u32[]{:S(2)}, u32[]{:S(2)}) collective-permute-start(bf16[15,128,128]{2,1,0:T(8,128)(2,1)S(1)} %get-tuple-element.37), channel_id=1, source_target_pairs={{0,1},{1,0},{2,3},{3,2},{4,5},{5,4},{6,7},{7,6},{8,9},{9,8},{10,11... | collective-permute-start | bytes 1474568 | tf_op jit(solution)/shard_map/ppermute | solution.py:414
